TPU v7x, 32 devices: a whole 2x2x4 slice. The times are simulated.
32 devices in a mesh: seq: 8 (over z, x), batch: 4 (over y, core).
Axes of the slice: x: 2, y: 2, z: 4, core: 2. Of those that a mesh axis runs over, the one named last changes fastest.
Arguments:
- tokens: bfloat16 [2048, 12, 576], P('seq', 'batch'), may hold values from -6 to 6
- positions: int32 [2048, 12], P('seq', 'batch'), may hold values from 0 to 2047, as said below
- norm_attn: float32 [576], replicated, may hold values from 0.5 to 1.5
- w_query: bfloat16 [576, 576], replicated, may hold values from -0.5 to 0.5
- w_key: bfloat16 [576, 192], replicated, may hold values from -0.25 to 0.25
- w_value: bfloat16 [576, 192], replicated, may hold values from -0.25 to 0.25
- w_out: bfloat16 [576, 576], replicated, may hold values from -1 to 1
- norm_mlp: float32 [576], replicated, may hold values from 0.5 to 1.5
- w_gate: bfloat16 [576, 1536], replicated, may hold values from -0.25 to 0.25
- w_up: bfloat16 [576, 1536], replicated, may hold values from -0.25 to 0.25
- w_down: bfloat16 [1536, 576], replicated, may hold values from -0.15625 to 0.15625
- cotangent: bfloat16 [2048, 12, 576], P('seq', 'batch'), may hold values from -6 to 6
Outputs:
- block_out: bfloat16 [2048, 12, 576], P('seq', 'batch')
- d_tokens: bfloat16 [2048, 12, 576], P('seq', 'batch')
- g_norm_attn: float32 [576], replicated
- g_query: float32 [576, 576], replicated
- g_key: float32 [576, 192], replicated
- g_value: float32 [576, 192], replicated
- g_out: float32 [576, 576], replicated
- g_norm_mlp: float32 [576], replicated
- g_gate: float32 [576, 1536], replicated
- g_up: float32 [576, 1536], replicated
- g_down: float32 [1536, 576], replicated
Inputs may be any that keep to these rules, and one draw needn't show every extreme that they name: Along a sequence positions rise by one and return to 0 where a new document begins; sequence 0 is a single document.
All inputs are finite; a program needn't handle non-finite values.
Results may differ from a plain program's by a relative error of at most 0.019.
Values may be sent and summed in bfloat16 or wider, within the bound.
No kernel may reach another device: no remote copies, remote signals or barrier semaphores. Data moves between devices by JAX's collectives and lax.ppermute only.
A program may use at most 192 MiB of HBM per device.

v0:
```python
import functools
import math

import jax
import jax.numpy as jnp
from jax import lax
from jax.experimental import pallas as pl
from jax.experimental.pallas import tpu as pltpu
from jax.sharding import PartitionSpec as P

HEADS = 9
KV_HEADS = 3
HEAD_DIM = 64
PER = HEADS // KV_HEADS
LANES = 128

eps_norm = 1e-05
mask_low = -1e30
f32 = jnp.float32
bf16 = jnp.bfloat16

NN = (((1,), (0,)), ((), ()))
NT = (((1,), (1,)), ((), ()))
TN = (((0,), (0,)), ((), ()))
UNROLL = 4


def dot(left, right, dims=NN):
    return lax.dot_general(left, right, dims, preferred_element_type=f32)


def params(mib):
    return pltpu.CompilerParams(vmem_limit_bytes=mib * 1024 * 1024)


def full_spec(shape):
    zeros = (0,) * len(shape)
    return pl.BlockSpec(shape, lambda *_: zeros)


def lane_index(rows):
    return lax.broadcasted_iota(jnp.int32, (rows, LANES), 1)


def swap_halves(tile):
    half = HEAD_DIM // 2
    lane = lane_index(tile.shape[0])
    return jnp.where(
        lane % HEAD_DIM < half, pltpu.roll(tile, LANES - half, 1), pltpu.roll(tile, half, 1)
    )


def head_tiles(lin):
    rows, width = lin.shape
    if width % LANES:
        lin = jnp.concatenate([lin, jnp.zeros((rows, HEAD_DIM), lin.dtype)], axis=1)
    return [lin[:, at : at + LANES] for at in range(0, lin.shape[1], LANES)]


def pre_kernel(
    x_ref, norm_ref, wq_ref, wk_ref, wv_ref, cos_ref, sin_ref, a_ref, q_ref, kv_ref
):
    x = x_ref[0].T.astype(f32)
    rows, width = x.shape
    scale = lax.rsqrt(jnp.sum(x * x, axis=-1, keepdims=True) * (1.0 / width) + eps_norm)
    a = (x * scale * norm_ref[...]).astype(bf16)
    a_ref[0] = a
    cos, sin = cos_ref[0], sin_ref[0]
    low_half = lane_index(rows) < HEAD_DIM

    def turn(tile):
        return tile * cos + swap_halves(tile) * sin

    keys = [turn(tile) for tile in head_tiles(dot(a, wk_ref[...], NT))]
    values = head_tiles(dot(a, wv_ref[...], NT))
    for g in range(KV_HEADS):
        key, value = keys[g // 2], values[g // 2]
        if g % 2 == 0:
            value = pltpu.roll(value, HEAD_DIM, 1)
        else:
            key = pltpu.roll(key, HEAD_DIM, 1)
        kv_ref[0, :, g * LANES : (g + 1) * LANES] = jnp.where(low_half, key, value).astype(bf16)
    queries = [turn(tile) * 0.125 for tile in head_tiles(dot(a, wq_ref[...]))]
    for head in range(HEADS):
        tile = queries[head // 2]
        if head % 2:
            tile = pltpu.roll(tile, HEAD_DIM, 1)
        group, place = divmod(head, PER)
        q_ref[0, group, place * rows : (place + 1) * rows, :] = jnp.where(
            low_half, tile, 0.0
        ).astype(bf16)


def pre_call(x, norm, w_query, w_key, w_value, cos, sin):
    seqs, width, rows = x.shape
    row = lambda shape: pl.BlockSpec((1,) + shape, lambda s: (s,) + (0,) * len(shape))
    return pl.pallas_call(
        pre_kernel,
        grid=(seqs,),
        in_specs=[
            row((width, rows)),
            full_spec((1, width)),
            full_spec(w_query.shape),
            full_spec(w_key.shape),
            full_spec(w_value.shape),
            row((rows, LANES)),
            row((rows, LANES)),
        ],
        out_specs=[
            row((rows, width)),
            row((KV_HEADS, PER * rows, LANES)),
            row((rows, KV_HEADS * LANES)),
        ],
        out_shape=[
            jax.ShapeDtypeStruct((seqs, rows, width), bf16),
            jax.ShapeDtypeStruct((seqs, KV_HEADS, PER * rows, LANES), bf16),
            jax.ShapeDtypeStruct((seqs, rows, KV_HEADS * LANES), bf16),
        ],
        compiler_params=params(16),
        name="project",
    )(x, norm, w_query, w_key, w_value, cos, sin)


def causal_part(rows, heads):
    key = lax.broadcasted_iota(jnp.int32, (rows, rows), 0)
    query = lax.broadcasted_iota(jnp.int32, (rows, rows), 1)
    return jnp.concatenate([key <= query] * heads, axis=1)


def for_blocks(ids, me, seqs, own, pieces, counts, work, zeros=None):
    if own is not None:
        for s in range(seqs):
            work(s, own[s], None, (-1, s, s))
    first = 1
    for k, (parts, count) in enumerate(zip(pieces, counts)):
        least = ids[first]
        for n in range(1, seqs * count):
            least = jnp.minimum(least, ids[first + n])
        unroll = min(count, UNROLL)

        @pl.when(least < me)
        def _(parts=parts, first=first, count=count, k=k):
            def some(c, _):
                for s in range(seqs):
                    for u in range(unroll):
                        j = c * unroll + u
                        work(s, parts[s][j], ids[first + s * count + j] < me, (k, s, j))
                return 0

            if count == unroll:
                some(0, 0)
            else:
                lax.fori_loop(0, count // unroll, some, 0)

        if zeros is not None:

            @pl.when(least >= me)
            def _(k=k):
                zeros(k)

        first += seqs * count


def forward_kernel(counts, has_own, has_state, is_last, ids, *refs):
    refs = list(refs)
    q = refs.pop(0)
    seqs, rows = q.shape[0], q.shape[2] // PER
    own = refs.pop(0) if has_own else None
    pieces = [[refs.pop(0) for _ in range(seqs)] for _ in counts]
    if has_state:
        peak_in, total_in = refs.pop(0), refs.pop(0)
    outs, (peak, total) = refs[:-2], refs[-2:]
    me = ids[0]
    if has_state:
        peak[...] = peak_in[:, 0]
        total[...] = total_in[:, 0]
    low_half = lane_index(rows) < HEAD_DIM

    def attend(s, kv, seen):
        ones_values = jnp.where(low_half, jnp.ones((), bf16), kv)
        scores = dot(kv, q[s, 0], NT)
        if seen is None:
            scores = jnp.where(causal_part(rows, PER), scores, mask_low)
            new_peak = shift = jnp.max(scores, axis=0, keepdims=True)
        else:
            old_peak = peak[s]
            top = jnp.max(scores, axis=0, keepdims=True)
            new_peak = jnp.where(seen, jnp.maximum(old_peak, top), old_peak)
            shift = jnp.where(seen, new_peak, -mask_low)
        shares = jnp.exp(scores - shift).astype(bf16)
        added = dot(shares.T, ones_values)
        if seen is None:
            total[s] = added
        else:
            total[s] = total[s] * jnp.exp(old_peak - new_peak).T + added
        peak[s] = new_peak

    for_blocks(ids, me, seqs, own, pieces, counts, lambda s, kv, seen, store: attend(s, kv, seen))
    if is_last:
        attn, log_total = outs
        group = pl.program_id(0)
        for s in range(seqs):
            acc = total[s]
            normal = acc / pltpu.roll(acc, HEAD_DIM, 1)
            sums = acc.T[0:1]
            log_total[s, 0] = peak[s] + jnp.log(sums)
            values = normal[:, HEAD_DIM:].astype(bf16)
            for g in range(KV_HEADS):

                @pl.when(group == g)
                def _(values=values, s=s, g=g):
                    for h in range(PER):
                        at = (g * PER + h) * HEAD_DIM
                        attn[s, :, at : at + HEAD_DIM] = values[h * rows : (h + 1) * rows]

    else:
        outs[0][:, 0] = peak[...]
        outs[1][:, 0] = total[...]


def piece_spec(count, rows):
    return pl.BlockSpec((count, rows, LANES), lambda g, *_: (0, 0, g))


def group_spec(seqs, *shape):
    zeros = (0,) * len(shape)
    return pl.BlockSpec((seqs, 1) + shape, lambda g, *_: (0, g) + zeros)


def forward_call(ids, q, own, pieces, state, is_last):
    seqs, groups, wide, _ = q.shape
    rows = wide // PER
    counts = [parts[0].shape[0] for parts in pieces]
    arrays, specs = [q], [group_spec(seqs, wide, LANES)]
    if own is not None:
        arrays.append(own)
        specs.append(piece_spec(seqs, rows))
    for parts, count in zip(pieces, counts):
        arrays += parts
        specs += [piece_spec(count, rows)] * seqs
    row_spec, row_shape = group_spec(seqs, 1, wide), (seqs, groups, 1, wide)
    sum_spec, sum_shape = group_spec(seqs, wide, LANES), (seqs, groups, wide, LANES)
    if state is not None:
        arrays += list(state)
        specs += [row_spec, sum_spec]
    if is_last:
        attn_shape = (seqs, rows, HEADS * HEAD_DIM)
        out_shape = [
            jax.ShapeDtypeStruct(attn_shape, bf16),
            jax.ShapeDtypeStruct(row_shape, f32),
        ]
        out_specs = [full_spec(attn_shape), row_spec]
    else:
        out_shape = [
            jax.ShapeDtypeStruct(row_shape, f32),
            jax.ShapeDtypeStruct(sum_shape, f32),
        ]
        out_specs = [row_spec, sum_spec]
    return pl.pallas_call(
        functools.partial(
            forward_kernel, counts, own is not None, state is not None, is_last
        ),
        out_shape=out_shape,
        grid_spec=pltpu.PrefetchScalarGridSpec(
            num_scalar_prefetch=1,
            grid=(groups,),
            in_specs=specs,
            out_specs=out_specs,
            scratch_shapes=[
                pltpu.VMEM((seqs, 1, wide), f32),
                pltpu.VMEM((seqs, wide, LANES), f32),
            ],
        ),
        compiler_params=params(60),
        name="attend_forward",
    )(ids, *arrays)


def backward_kernel(counts, has_own, has_state, is_last, waits, ids, *refs):
    refs = list(refs)[waits:]
    q, d_out, log_total, delta = refs[:4]
    refs = refs[4:]
    seqs, rows = q.shape[0], q.shape[2] // PER
    own = refs.pop(0) if has_own else None
    pieces = [[refs.pop(0) for _ in range(seqs)] for _ in counts]
    d_query_in = refs.pop(0) if has_state else None
    cos, sin = (refs.pop(0), refs.pop(0)) if is_last else (None, None)
    d_own = refs.pop(0) if has_own else None
    d_pieces = [[refs.pop(0) for _ in range(seqs)] for _ in counts]
    d_query_out, d_query = refs
    me = ids[0]
    if has_state:
        d_query[...] = d_query_in[:, 0]
    else:
        d_query[...] = jnp.zeros_like(d_query)

    def back(s, kv, seen, place):
        q_all, d_all = q[s, 0], d_out[s, 0]
        scores = dot(kv, q_all, NT)
        if seen is None:
            probs = jnp.exp(scores - log_total[s, 0])
            probs = jnp.where(causal_part(rows, PER), probs, 0.0)
        else:
            probs = jnp.exp(scores - jnp.where(seen, log_total[s, 0], -mask_low))
        d_probs = dot(kv, d_all, NT)
        d_scores = (probs * (d_probs - delta[s, 0])).astype(bf16)
        d_query[s] += dot(d_scores.T, kv)
        terms = (dot(probs.astype(bf16), d_all) + dot(d_scores, q_all)).astype(bf16)
        piece, s, j = place
        if piece < 0:
            d_own[s] = terms
        else:
            d_pieces[piece][s][j] = terms

    def zeros(piece):
        for s in range(seqs):
            d_pieces[piece][s][...] = jnp.zeros(d_pieces[piece][s].shape, bf16)

    for_blocks(ids, me, seqs, own, pieces, counts, back, zeros)
    if is_last:
        group = pl.program_id(0)
        for s in range(seqs):
            turned = []
            for h in range(PER):
                tile = d_query[s, h * rows : (h + 1) * rows, :] * 0.125
                turned.append(
                    (tile * cos[s] - swap_halves(tile) * sin[s])[:, :HEAD_DIM].astype(bf16)
                )
            for g in range(KV_HEADS):

                @pl.when(group == g)
                def _(turned=turned, s=s, g=g):
                    for h in range(PER):
                        at = (g * PER + h) * HEAD_DIM
                        d_query_out[s, :, at : at + HEAD_DIM] = turned[h]

    else:
        d_query_out[:, 0] = d_query[...]


def backward_call(ids, q, d_out, log_total, delta, own, pieces, d_query, tables, after=()):
    seqs, groups, wide, _ = q.shape
    rows = wide // PER
    counts = [parts[0].shape[0] for parts in pieces]
    sum_spec, sum_shape = group_spec(seqs, wide, LANES), (seqs, groups, wide, LANES)
    row_spec = group_spec(seqs, 1, wide)
    arrays = [q, d_out, log_total, delta]
    specs = [sum_spec, sum_spec, row_spec, row_spec]
    out_shape, out_specs = [], []
    if own is not None:
        arrays.append(own)
        specs.append(piece_spec(seqs, rows))
        out_shape.append(jax.ShapeDtypeStruct(own.shape, bf16))
        out_specs.append(piece_spec(seqs, rows))
    for parts, count in zip(pieces, counts):
        arrays += parts
        specs += [piece_spec(count, rows)] * seqs
        out_shape += [jax.ShapeDtypeStruct(parts[0].shape, bf16)] * seqs
        out_specs += [piece_spec(count, rows)] * seqs
    if d_query is not None:
        arrays.append(d_query)
        specs.append(sum_spec)
    is_last = tables is not None
    if is_last:
        arrays += list(tables)
        specs += [full_spec((seqs, rows, LANES))] * 2
        shape = (seqs, rows, HEADS * HEAD_DIM)
        out_shape.append(jax.ShapeDtypeStruct(shape, bf16))
        out_specs.append(full_spec(shape))
    else:
        out_shape.append(jax.ShapeDtypeStruct(sum_shape, f32))
        out_specs.append(sum_spec)
    arrays = list(after) + arrays
    specs = [pl.BlockSpec(memory_space=pl.ANY)] * len(after) + specs
    outs = pl.pallas_call(
        functools.partial(
            backward_kernel, counts, own is not None, d_query is not None, is_last, len(after)
        ),
        out_shape=out_shape,
        grid_spec=pltpu.PrefetchScalarGridSpec(
            num_scalar_prefetch=1,
            grid=(groups,),
            in_specs=specs,
            out_specs=out_specs,
            scratch_shapes=[pltpu.VMEM((seqs, wide, LANES), f32)],
        ),
        compiler_params=params(60),
        name="attend_backward",
    )(ids, *arrays)
    d_own = None
    if own is not None:
        d_own, outs = outs[0], outs[1:]
    d_pieces = [list(outs[k * seqs : (k + 1) * seqs]) for k in range(len(counts))]
    return d_own, d_pieces, outs[-1]


def middle_kernel(
    x_ref,
    cot_ref,
    attn_ref,
    w_out_ref,
    norm_ref,
    w_gate_ref,
    w_up_ref,
    w_down_ref,
    out_ref,
    b_ref,
    hid_ref,
    d_gate_ref,
    d_up_ref,
    d_mid_ref,
    d_proj_ref,
    d_out_ref,
    delta_ref,
    g_norm_ref,
):
    x = x_ref[0].T.astype(f32)
    rows, width = x.shape
    cot = cot_ref[0].T
    attn = attn_ref[0]
    mid = x + dot(attn, w_out_ref[...])
    scale = lax.rsqrt(jnp.sum(mid * mid, axis=-1, keepdims=True) * (1.0 / width) + eps_norm)
    normed = mid * scale
    b = (normed * norm_ref[...]).astype(bf16)
    b_ref[0] = b
    gate = dot(b, w_gate_ref[...])
    up = dot(b, w_up_ref[...])
    sig = 1.0 / (1.0 + jnp.exp(-gate))
    active = gate * sig
    hid = (active * up).astype(bf16)
    hid_ref[0] = hid
    out_ref[0] = (mid + dot(hid, w_down_ref[...], NT)).astype(bf16).T
    d_hid = dot(cot, w_down_ref[...])
    d_gate = (d_hid * up * sig * (1.0 + gate * (1.0 - sig))).astype(bf16)
    d_up = (d_hid * active).astype(bf16)
    d_gate_ref[0] = d_gate
    d_up_ref[0] = d_up
    d_b = dot(d_gate, w_gate_ref[...], NT) + dot(d_up, w_up_ref[...], NT)
    g_norm = jnp.sum(d_b * normed, axis=0, keepdims=True)

    @pl.when(pl.program_id(0) == 0)
    def _():
        g_norm_ref[...] = g_norm

    @pl.when(pl.program_id(0) > 0)
    def _():
        g_norm_ref[...] += g_norm

    e = d_b * norm_ref[...]
    mean = jnp.sum(e * normed, axis=-1, keepdims=True) * (1.0 / width)
    d_mid = cot.astype(f32) + scale * (e - normed * mean)
    d_mid_ref[0] = d_mid
    d_proj = d_mid.astype(bf16)
    d_proj_ref[0] = d_proj
    d_attn = dot(d_proj, w_out_ref[...], NT).astype(bf16).astype(f32)
    both = d_attn * attn.astype(f32)
    high = both.astype(bf16)
    rest = (both - high.astype(f32)).astype(bf16)
    head = lax.broadcasted_iota(jnp.int32, (16, width), 0)
    feature = lax.broadcasted_iota(jnp.int32, (16, width), 1)
    picks = jnp.where(
        (feature >= head * HEAD_DIM) & (feature < (head + 1) * HEAD_DIM), 1.0, 0.0
    ).astype(bf16)
    sums = dot(picks, high, NT) + dot(picks, rest, NT)
    high_half = lane_index(rows) >= HEAD_DIM
    padded = jnp.concatenate([d_attn, jnp.zeros((rows, HEAD_DIM), f32)], axis=1)
    for k in range(HEADS):
        at = k // 2 * LANES
        tile = padded[:, at : at + LANES]
        if k % 2 == 0:
            tile = pltpu.roll(tile, HEAD_DIM, 1)
        group, place = divmod(k, PER)
        here = slice(place * rows, (place + 1) * rows)
        d_out_ref[0, group, here, :] = jnp.where(high_half, tile, 0.0).astype(bf16)
        delta_ref[0, group, 0:1, here] = sums[k : k + 1]


def middle_call(x, cot, attn, w_out, norm, w_gate, w_up, w_down):
    seqs, width, rows = x.shape
    hidden = w_gate.shape[1]
    row = lambda *shape: pl.BlockSpec((1,) + shape, lambda s: (s,) + (0,) * len(shape))
    wide = PER * rows
    shapes = [
        ((width, rows), bf16),
        ((rows, width), bf16),
        ((rows, hidden), bf16),
        ((rows, hidden), bf16),
        ((rows, hidden), bf16),
        ((rows, width), f32),
        ((rows, width), bf16),
        ((KV_HEADS, wide, LANES), bf16),
        ((KV_HEADS, 1, wide), f32),
    ]
    return pl.pallas_call(
        middle_kernel,
        grid=(seqs,),
        in_specs=[row(width, rows), row(width, rows), row(rows, width)]
        + [
            full_spec(w_out.shape),
            full_spec((1, width)),
            full_spec(w_gate.shape),
            full_spec(w_up.shape),
            full_spec(w_down.shape),
        ],
        out_specs=[row(*shape) for shape, _ in shapes] + [full_spec((1, width))],
        out_shape=[jax.ShapeDtypeStruct((seqs,) + shape, kind) for shape, kind in shapes]
        + [jax.ShapeDtypeStruct((1, width), f32)],
        compiler_params=params(60),
        name="feed_forward",
    )(x, cot, attn, w_out, norm, w_gate, w_up, w_down)


def ffn_place(k, t, tiles):
    if k < 2:
        return k, t
    return (0, tiles + t) if t < tiles // 2 else (1, tiles + t - tiles // 2)


def half_rows(places, width, parts):
    unit = 16 * (parts // 2)
    return -(-places * width // unit) * unit


def put(out_ref, place, width, tile):
    half, at = place
    out_ref[half, at * width : (at + 1) * width, :] = tile


def with_column(tile, column):
    free = lane_index(tile.shape[0]) >= HEAD_DIM
    return jnp.where(free, column, tile)


def ffn_grad_kernel(b_ref, cot_ref, hid_ref, d_gate_ref, d_up_ref, out_ref):
    width = b_ref.shape[1]
    hidden = hid_ref.shape[1]
    tiles = hidden // LANES
    chunk = 2 * LANES
    b_turned = b_ref[...].T
    cot_turned = jnp.concatenate([cot_ref[s] for s in range(cot_ref.shape[0])], axis=1)
    for k, (left, right) in enumerate(
        ((b_turned, d_gate_ref), (b_turned, d_up_ref), (cot_turned, hid_ref))
    ):
        for c in range(hidden // chunk):
            product = dot(left, right[:, c * chunk : (c + 1) * chunk]).astype(bf16)
            for u in range(2):
                put(
                    out_ref,
                    ffn_place(k, 2 * c + u, tiles),
                    width,
                    product[:, u * LANES : (u + 1) * LANES],
                )


def ffn_grad_call(b, cot, hid, d_gate, d_up):
    width = b.shape[1]
    tiles = hid.shape[1] // LANES
    return pl.pallas_call(
        ffn_grad_kernel,
        out_shape=jax.ShapeDtypeStruct((2, (tiles + tiles // 2) * width, LANES), bf16),
        compiler_params=params(60),
        name="ffn_grads",
    )(b, cot, hid, d_gate, d_up)


def ffn_unfold_kernel(gate_in, up_in, down_in, gate_ref, up_ref, down_ref):
    for source, target in ((gate_in, gate_ref), (up_in, up_ref), (down_in, down_ref)):
        for u in range(source.shape[1]):
            target[:, u * LANES : (u + 1) * LANES] = source[0, u].astype(f32)


def ffn_unfold_call(sums, width, hidden):
    tiles = hidden // LANES
    chunk = 2
    steps = tiles // chunk
    sums = sums.reshape(2, tiles + tiles // 2, width, LANES)
    block = (1, chunk, width, LANES)
    return pl.pallas_call(
        ffn_unfold_kernel,
        grid=(steps,),
        in_specs=[
            pl.BlockSpec(block, lambda i: (0, i, 0, 0)),
            pl.BlockSpec(block, lambda i: (1, i, 0, 0)),
            pl.BlockSpec(block, lambda i: (i // (steps // 2), steps + i % (steps // 2), 0, 0)),
        ],
        out_specs=[pl.BlockSpec((width, chunk * LANES), lambda i: (0, i))] * 3,
        out_shape=[jax.ShapeDtypeStruct((width, hidden), f32)] * 3,
        compiler_params=params(60),
        name="ffn_unfold",
    )(sums, sums, sums)


def unfold_square(products, out_ref, norm_ref):
    for t, product in enumerate(products):
        if t < len(products) - 1:
            out_ref[:, t * LANES : (t + 1) * LANES] = product
        else:
            out_ref[:, t * LANES :] = product[:, :HEAD_DIM]
            norm_ref[...] = product.T[HEAD_DIM : HEAD_DIM + 1, :]


def unfold_call(kernel, name, arrays, shapes):
    smem = pl.BlockSpec(memory_space=pltpu.SMEM)
    vmem = pl.BlockSpec(memory_space=pltpu.VMEM)
    return pl.pallas_call(
        kernel,
        in_specs=[smem if t.ndim == 1 else vmem for t in arrays],
        out_shape=[jax.ShapeDtypeStruct(shape, f32) for shape in shapes],
        compiler_params=params(48),
        name=name,
    )(*arrays)


def query_grad_kernel(
    a_ref, attn_ref, d_proj_ref, d_q_ref, g_norm_ref, w_ref, out_ref, g_ref, g_out_ref
):
    for t, tile in enumerate(head_tiles(dot(a_ref[...].T, d_q_ref[...]))):
        g_ref[t] = tile.astype(bf16)
    width = a_ref.shape[1]
    column = jnp.broadcast_to(g_norm_ref[...], (8, width)).T[:, :1]
    for t, tile in enumerate(head_tiles(dot(attn_ref[...].T, d_proj_ref[...]))):
        if t == g_out_ref.shape[0] - 1:
            tile = with_column(tile, column)
        g_out_ref[t] = tile.astype(bf16)
    out_ref[...] = dot(d_q_ref[...], w_ref[...], NT)


def query_grad_call(a, attn, d_proj, d_q, g_norm, w_query):
    rows, width = a.shape
    tiles = jax.ShapeDtypeStruct((-(-width // LANES), width, LANES), bf16)
    return pl.pallas_call(
        query_grad_kernel,
        out_shape=[jax.ShapeDtypeStruct((rows, width), f32), tiles, tiles],
        compiler_params=params(32),
        name="query_grads",
    )(a, attn, d_proj, d_q, g_norm, w_query)


def attn_place(t):
    return t % 2, t // 2


def last_kernel(
    x_ref, a_ref, norm_ref, wk_ref, wv_ref, cos_ref, sin_ref, d_kv_ref, d_aq_ref, d_mid_ref, g_q_ref,
    g_out_ref, out_ref, g_ref, d_pairs, d_norm,
):
    step = pl.program_id(0)
    x = x_ref[0].T.astype(f32)
    rows, width = x.shape
    low_half = lane_index(rows) < HEAD_DIM
    scale = lax.rsqrt(jnp.sum(x * x, axis=-1, keepdims=True) * (1.0 / width) + eps_norm)
    normed = x * scale
    parts = []
    for g in range(KV_HEADS):
        tile = d_kv_ref[0, :, g * LANES : (g + 1) * LANES].astype(f32)
        turned = tile * cos_ref[0] - swap_halves(tile) * sin_ref[0]
        parts.append(jnp.where(low_half, turned, tile))
    moved = [pltpu.roll(part, HEAD_DIM, 1) for part in parts]
    d_key = jnp.concatenate(
        [jnp.where(low_half, parts[0], moved[1]), parts[2][:, :HEAD_DIM]], axis=1
    ).astype(bf16)
    d_value = jnp.concatenate(
        [jnp.where(low_half, moved[0], parts[1]), moved[2][:, :HEAD_DIM]], axis=1
    ).astype(bf16)
    g_pairs = dot(a_ref[0], jnp.concatenate(parts, axis=1).astype(bf16), TN)
    d_a = d_aq_ref[0] + dot(d_key, wk_ref[...]) + dot(d_value, wv_ref[...])
    g_norm = jnp.sum(d_a * normed, axis=0, keepdims=True)

    @pl.when(step == 0)
    def _():
        d_norm[...] = g_norm
        d_pairs[...] = g_pairs

    @pl.when(step > 0)
    def _():
        d_norm[...] += g_norm
        d_pairs[...] += g_pairs

    e = d_a * norm_ref[...]
    mean = jnp.sum(e * normed, axis=-1, keepdims=True) * (1.0 / width)
    out_ref[0] = (d_mid_ref[0] + scale * (e - normed * mean)).astype(bf16).T

    @pl.when(step == pl.num_programs(0) - 1)
    def _():
        square = g_q_ref.shape[0]
        column = jnp.broadcast_to(d_norm[...], (8, width)).T[:, :1]
        for t in range(square):
            tile = g_q_ref[t]
            if t == square - 1:
                tile = with_column(tile.astype(f32), column).astype(bf16)
            put(g_ref, attn_place(t), width, tile)
        for g in range(KV_HEADS):
            put(
                g_ref,
                attn_place(square + g),
                width,
                d_pairs[:, g * LANES : (g + 1) * LANES].astype(bf16),
            )
        for t in range(square):
            put(g_ref, attn_place(square + KV_HEADS + t), width, g_out_ref[t])
        clear_rest(g_ref, 2 * square + KV_HEADS, width)


def last_call(x, a, norm, w_key, w_value, cos, sin, d_kv, d_aq, d_mid, g_query, g_out, parts):
    seqs, width, rows = x.shape
    row = lambda *shape: pl.BlockSpec((1,) + shape, lambda s: (s,) + (0,) * len(shape))
    places = -(-(2 * g_query.shape[0] + KV_HEADS) // 2)
    g_shape = (2, half_rows(places, width, parts), LANES)
    wide = KV_HEADS * LANES
    return pl.pallas_call(
        last_kernel,
        grid=(seqs,),
        in_specs=[
            row(width, rows),
            row(rows, width),
            full_spec((1, width)),
            full_spec(w_key.shape),
            full_spec(w_value.shape),
            row(rows, LANES),
            row(rows, LANES),
            row(rows, wide),
            row(rows, width),
            row(rows, width),
            full_spec(g_query.shape),
            full_spec(g_out.shape),
        ],
        out_specs=[row(width, rows), full_spec(g_shape)],
        out_shape=[
            jax.ShapeDtypeStruct((seqs, width, rows), bf16),
            jax.ShapeDtypeStruct(g_shape, bf16),
        ],
        scratch_shapes=[pltpu.VMEM((width, wide), f32), pltpu.VMEM((1, width), f32)],
        compiler_params=params(32),
        name="last_part",
    )(x, a, norm, w_key, w_value, cos, sin, d_kv, d_aq, d_mid, g_query, g_out)


def attn_unfold_kernel(
    side, mine, other, query_ref, key_ref, value_ref, norm_ref, out_ref, norm_two_ref
):
    width = query_ref.shape[0]
    square = -(-width // LANES)

    def spread(halves):
        def tile(t):
            half, at = attn_place(t)
            return halves[half][at * width : (at + 1) * width, :].astype(f32)

        unfold_square([tile(t) for t in range(square)], query_ref, norm_ref)
        for g in range(KV_HEADS):
            pair = tile(square + g)
            lanes = slice(g * HEAD_DIM, (g + 1) * HEAD_DIM)
            turned = pair.T
            key_ref[lanes, :] = turned[:HEAD_DIM]
            value_ref[lanes, :] = turned[HEAD_DIM:]
        first = square + KV_HEADS
        unfold_square([tile(first + t) for t in range(square)], out_ref, norm_two_ref)

    @pl.when(side[0] == 0)
    def _():
        spread((mine, other))

    @pl.when(side[0] != 0)
    def _():
        spread((other, mine))


def device_stages(seq_count, batch_count):
    masks = [1 << k for k in range(batch_count.bit_length() - 1)]
    masks += [mask * batch_count for mask in exchange_masks(seq_count)]
    return [masks[:1]] + [masks[k : k + 2] for k in range(1, len(masks), 2)]


def stage_places(stages, index):
    bits = {}
    for mask in sorted((m for stage in stages for m in stage), reverse=True):
        bit = (index >> (mask.bit_length() - 1)) & 1
        bits[mask] = bit
        index = index ^ (bit * mask)
    return [sum(bits[mask] << k for k, mask in enumerate(stage)) for stage in stages]


def swap_with(value, mask, devices):
    return lax.ppermute(value, ("seq", "batch"), [(i, i ^ mask) for i in range(devices)])


def scatter_stage(value, stage, place, devices):
    group = 1 << len(stage)
    masks = span(stage)
    value = value.reshape((group, -1, LANES))
    pick = lambda k: lax.dynamic_index_in_dim(value, place ^ k, 0, False)
    got = [swap_with(pick(k), masks[k], devices) for k in range(1, group)]
    return sum((g.astype(f32) for g in got), pick(0).astype(f32)).astype(bf16)


def gather_stage(value, stage, place, devices):
    group = 1 << len(stage)
    masks = span(stage)
    parts = jnp.stack([value] + [swap_with(value, masks[k], devices) for k in range(1, group)])
    for k in range(len(stage)):
        shape = parts.shape
        split = parts.reshape((group >> (k + 1), 2, 1 << k) + shape[1:])
        parts = jnp.where((place >> k) & 1 == 1, split[:, ::-1], split).reshape(shape)
    return parts


def gather_order(value, order, stages, places, devices):
    done = []
    for k in order:
        value = gather_stage(value, stages[k], places[k], devices)
        done.insert(0, k)
    back = sorted(range(len(done)), key=lambda i: done[i])
    return jnp.transpose(value, back + [len(done), len(done) + 1])


def gather_sums(part, stages, places, devices, chains):
    late = list(range(1, len(stages)))[::-1]
    step = part.shape[0] // chains
    got = [
        gather_order(
            part[c * step : (c + 1) * step],
            late[c % len(late) :] + late[: c % len(late)],
            stages,
            places,
            devices,
        )
        for c in range(chains)
    ]
    half = got[0] if chains == 1 else jnp.concatenate(got, axis=-2)
    half = half.reshape(-1, LANES)
    return half, swap_with(half, stages[0][0], devices)


def exchange_masks(count):
    masks = [1 << k for k in range(count.bit_length() - 1)]
    if count == 8:
        masks[2] = 6
    return masks


def chain_order(masks, chain):
    shift = chain % len(masks)
    return masks[shift:] + masks[:shift]


def span(masks):
    ids = [0]
    for mask in masks:
        ids += [k ^ mask for k in ids]
    return ids


def gather_blocks(kv, count):
    me = lax.axis_index("seq")
    masks = exchange_masks(count)
    seqs, last = kv.shape[0], len(masks) - 1
    held = [kv[s : s + 1] for s in range(seqs)]
    rounds, numbers = [], []

    def send(s, r, value, known, is_last):
        mask = chain_order(masks, s)[r]
        pairs = [
            (i, i ^ mask)
            for i in range(count)
            if not is_last or min(i ^ k for k in known) < i ^ mask
        ]
        return lax.ppermute(value, "seq", pairs), [me ^ (mask ^ k) for k in known]

    def keep(sent):
        rounds.append([value for value, _ in sent])
        numbers.append([k for _, known in sent for k in known])

    early = []
    for r in range(last):
        known = [span(chain_order(masks, s)[:r]) for s in range(seqs)]
        if r == last - 1:
            early = [send(s, last, held[s], known[s], True) for s in range(seqs)]
        sent = [send(s, r, held[s], known[s], False) for s in range(seqs)]
        keep(sent)
        if r < last - 1:
            held = [jnp.concatenate([h, v], axis=0) for h, (v, _) in zip(held, sent)]
    keep(early)
    keep(
        [
            send(
                s,
                last,
                rounds[last - 1][s],
                [chain_order(masks, s)[last - 1] ^ k for k in known[s]],
                True,
            )
            for s in range(seqs)
        ]
    )
    return rounds, numbers


def add_low(*terms):
    return sum((t.astype(f32) for t in terms[1:]), terms[0].astype(f32)).astype(bf16)


def return_round(parts, r, count):
    masks = exchange_masks(count)
    got = []
    for s, part in enumerate(parts):
        order = chain_order(masks, s)
        mask, known = order[r], span(order[:r])
        pairs = [
            (i, i ^ mask)
            for i in range(count)
            if r < len(masks) - 1 or min(i ^ mask ^ k for k in known) < i
        ]
        got.append(lax.ppermute(part, "seq", pairs))
    return got


def beside(tile):
    rows = tile.shape[0]
    half = rows // 2
    return jnp.where(
        lane_index(half) < HEAD_DIM, tile[:half], pltpu.roll(tile[half:], HEAD_DIM, 1)
    )


def stacked(tile):
    return jnp.concatenate([tile, pltpu.roll(tile, HEAD_DIM, 1)], axis=0)


def other_half(tile):
    return pltpu.roll(tile, HEAD_DIM, 1)


def join(low, high):
    return jnp.where(lane_index(low.shape[0]) < HEAD_DIM, low, high)


def low_only(tile):
    return jnp.where(lane_index(tile.shape[0]) < HEAD_DIM, tile, 0.0)


def high_only(tile):
    return jnp.where(lane_index(tile.shape[0]) < HEAD_DIM, 0.0, tile)


def write_long(ref, at, parts, more=None):
    h0, h1, h2, key, value = parts
    rows = key.shape[0]
    ref[at, 0:rows] = join(h0, other_half(h1)).astype(bf16)
    ref[at, rows : 2 * rows] = join(h2, other_half(key)).astype(bf16)
    ref[at, 2 * rows : rows * 5 // 2] = beside(value).astype(bf16)
    if more is not None:
        ref[at, rows * 5 // 2 :] = more


def read_long(message, rows):
    first = message[0:rows].astype(f32)
    second = message[rows : 2 * rows].astype(f32)
    value = stacked(message[2 * rows : rows * 5 // 2].astype(f32))
    return (first, other_half(first), second), join(other_half(second), other_half(value))


def write_short(ref, at, heads):
    rows = heads[0].shape[0]
    ref[at, 0:rows] = join(heads[0], other_half(heads[1])).astype(bf16)
    ref[at, rows:] = beside(heads[2]).astype(bf16)


def read_short(message):
    rows = message.shape[0] * 2 // 3
    first = message[0:rows].astype(f32)
    return first, other_half(first), stacked(message[rows:].astype(f32))


def units_pre_kernel(
    ids, x_ref, norm_ref, wq_ref, wk_ref, wv_ref, cos_ref, sin_ref, a_ref, out_ref, q_ref, kv_ref
):
    step = pl.program_id(0)
    count = out_ref.shape[0]
    me = ids[0]
    x = x_ref[0].T.astype(f32)
    rows, width = x.shape
    scale = lax.rsqrt(jnp.sum(x * x, axis=-1, keepdims=True) * (1.0 / width) + eps_norm)
    a = (x * scale * norm_ref[...]).astype(bf16)
    a_ref[0] = a
    cos, sin = cos_ref[0], sin_ref[0]

    def turn(tile):
        return tile * cos + swap_halves(tile) * sin

    def heads_of(tiles, many):
        return [tiles[h // 2] if h % 2 == 0 else other_half(tiles[h // 2]) for h in range(many)]

    queries = heads_of([turn(t) * 0.125 for t in head_tiles(dot(a, wq_ref[...]))], HEADS)
    keys = heads_of([turn(t) for t in head_tiles(dot(a, wk_ref[...], NT))], KV_HEADS)
    values = heads_of(head_tiles(dot(a, wv_ref[...], NT)), KV_HEADS)
    for g in range(KV_HEADS):
        parts = queries[g * PER : (g + 1) * PER] + [keys[g], values[g]]
        unit = step * KV_HEADS + g

        @pl.when(unit < count)
        def _(parts=parts, unit=unit):
            write_long(out_ref, lax.rem(unit - me + count, count), parts)

        @pl.when(unit == count)
        def _(parts=parts):
            for h in range(PER):
                q_ref[h * rows : (h + 1) * rows] = low_only(parts[h]).astype(bf16)
            kv_ref[0] = join(parts[3], other_half(parts[4])).astype(bf16)


def units_pre_call(ids, x, norm, w_query, w_key, w_value, cos, sin, count):
    seqs, width, rows = x.shape
    row = lambda shape: pl.BlockSpec((1,) + shape, lambda s, *_: (s,) + (0,) * len(shape))
    long_shape = (count, rows * 5 // 2, LANES)
    q_shape = (PER * rows, LANES)
    kv_shape = (1, rows, LANES)
    return pl.pallas_call(
        units_pre_kernel,
        grid_spec=pltpu.PrefetchScalarGridSpec(
            num_scalar_prefetch=1,
            grid=(seqs,),
            in_specs=[
                row((width, rows)),
                full_spec((1, width)),
                full_spec(w_query.shape),
                full_spec(w_key.shape),
                full_spec(w_value.shape),
                row((rows, LANES)),
                row((rows, LANES)),
            ],
            out_specs=[row((rows, width))]
            + [full_spec(shape) for shape in (long_shape, q_shape, kv_shape)],
        ),
        out_shape=[
            jax.ShapeDtypeStruct((seqs, rows, width), bf16),
            jax.ShapeDtypeStruct(long_shape, bf16),
            jax.ShapeDtypeStruct(q_shape, bf16),
            jax.ShapeDtypeStruct(kv_shape, bf16),
        ],
        compiler_params=params(60),
        name="project",
    )(ids, x, norm, w_query, w_key, w_value, cos, sin)


def attend_row(q, blocks, seen=None):
    rows = blocks[0].shape[0]
    peak = sums = None
    for first in range(0, len(blocks), UNROLL):
        part = blocks[first : first + UNROLL]
        scores = [dot(kv, q, NT) for kv in part]
        if first + len(part) == len(blocks):
            scores[-1] = jnp.where(causal_part(rows, PER), scores[-1], mask_low)
        tops = [jnp.max(sc, axis=0, keepdims=True) for sc in scores]
        flags = [None] * len(part)
        if seen is not None:
            flags = (seen + [None])[first : first + UNROLL]
            tops = [t if f is None else jnp.where(f, t, mask_low) for t, f in zip(tops, flags)]
        new_peak = functools.reduce(jnp.maximum, tops if peak is None else tops + [peak])
        shifts = [new_peak if f is None else jnp.where(f, new_peak, -mask_low) for f in flags]
        shares = [jnp.exp(sc - sh).astype(bf16).T for sc, sh in zip(scores, shifts)]
        ones = lane_index(rows) < HEAD_DIM
        values = [jnp.where(ones, jnp.ones((), bf16), kv) for kv in part]
        added = dot(jnp.concatenate(shares, axis=1), jnp.concatenate(values, axis=0))
        if peak is not None:
            fading = jnp.broadcast_to(jnp.exp(peak - new_peak), (LANES, peak.shape[1])).T
            added = sums * fading + added
        peak, sums = new_peak, added
    return peak, sums


def attend_result(peak, total):
    rows = total.shape[0] // PER
    moved = other_half(total)
    normal = moved / total
    log_total = peak + jnp.log(total.T[0:1])
    return [normal[h * rows : (h + 1) * rows] for h in range(PER)], log_total


def units_forward_kernel(count, ids, *refs):
    messages = refs[:count]
    out_ref, log_ref, q_ref, kv_ref = refs[-4:]
    rows = kv_ref.shape[1]
    me = ids[0]
    for t in range(count):
        block = lax.rem(me - t + count, count)
        heads, kv = read_long(messages[t], rows)
        for h in range(PER):
            q_ref[block, h * rows : (h + 1) * rows] = low_only(heads[h]).astype(bf16)
        kv_ref[block] = kv.astype(bf16)
    for i in range(count):
        new_peak, sums = attend_row(q_ref[i], [kv_ref[j] for j in range(i + 1)])
        heads, log_total = attend_result(new_peak, sums)
        log_ref[i] = log_total
        write_short(out_ref, lax.rem(i - me + count, count), heads)


def units_forward_call(ids, messages, after):
    count = len(messages)
    rows = messages[0].shape[0] * 2 // 5
    wide = PER * rows
    vmem = pl.BlockSpec(memory_space=pltpu.VMEM)
    return pl.pallas_call(
        functools.partial(units_forward_kernel, count),
        in_specs=[pl.BlockSpec(memory_space=pltpu.SMEM)]
        + [vmem] * count
        + [pl.BlockSpec(memory_space=pl.ANY)] * len(after),
        out_shape=[
            jax.ShapeDtypeStruct((count, rows * 3 // 2, LANES), bf16),
            jax.ShapeDtypeStruct((count, 1, wide), f32),
            jax.ShapeDtypeStruct((count, wide, LANES), bf16),
            jax.ShapeDtypeStruct((count, rows, LANES), bf16),
        ],
        compiler_params=params(48),
        name="units_forward",
    )(ids, *messages, *after)


def last_unit_forward_kernel(ids, q_ref, kv_ref, out_ref, log_ref):
    me = ids[0]
    count = kv_ref.shape[0]
    others = span(exchange_masks(count))[1:]
    blocks = [kv_ref[p] for p in range(1, count)] + [kv_ref[0]]
    heads, log_total = attend_result(
        *attend_row(q_ref[...], blocks, [(me ^ k) < me for k in others])
    )
    log_ref[...] = log_total
    write_short(out_ref, 0, heads)


def last_unit_forward_call(ids, q, kv):
    wide = q.shape[0]
    vmem = pl.BlockSpec(memory_space=pltpu.VMEM)
    return pl.pallas_call(
        last_unit_forward_kernel,
        in_specs=[pl.BlockSpec(memory_space=pltpu.SMEM), vmem, vmem],
        out_shape=[
            jax.ShapeDtypeStruct((1, wide // 2, LANES), bf16),
            jax.ShapeDtypeStruct((1, wide), f32),
        ],
        compiler_params=params(32),
        name="last_unit_forward",
    )(ids, q, kv)


def attend_back(q, d_out, kv, log_total, delta, diagonal):
    rows = kv.shape[0]
    scores = dot(kv, q, NT)
    probs = jnp.exp(scores - log_total)
    if diagonal:
        probs = jnp.where(causal_part(rows, PER), probs, 0.0)
    d_probs = dot(kv, d_out, NT)
    d_scores = (probs * (d_probs - delta)).astype(bf16)
    return (
        dot(probs.astype(bf16), d_out) + dot(d_scores, q),
        dot(d_scores.T, kv),
    )


def unpack_out(message, attn):
    heads, values = read_short(message), read_short(attn)
    delta = [
        jnp.sum(low_only(d * o).T, axis=0, keepdims=True) for d, o in zip(heads, values)
    ]
    d_out = jnp.concatenate([high_only(other_half(d)) for d in heads], axis=0)
    return d_out.astype(bf16), jnp.concatenate(delta, axis=1)


def last_unit_backward_kernel(
    ids, q_ref, kv_ref, d_ref, attn_ref, log_ref, d_kv_ref, d_q_ref, d_out
):
    me = ids[0]
    count = kv_ref.shape[0]
    d_value, delta = unpack_out(d_ref[...], attn_ref[...])
    d_out[...] = d_value
    log_total = log_ref[...]
    total = None
    for p, k in list(enumerate(span(exchange_masks(count))))[1:]:
        shift = jnp.where((me ^ k) < me, log_total, -mask_low)
        d_kv, d_q = attend_back(q_ref[...], d_out[...], kv_ref[p], shift, delta, False)
        d_kv_ref[me ^ k] = d_kv.astype(bf16)
        total = d_q if total is None else total + d_q
    d_kv, d_q = attend_back(q_ref[...], d_out[...], kv_ref[0], log_total, delta, True)
    d_kv_ref[me] = d_kv.astype(bf16)
    d_q_ref[...] = total + d_q


def last_unit_backward_call(ids, q, kv, d_message, attn, log_total):
    vmem = pl.BlockSpec(memory_space=pltpu.VMEM)
    return pl.pallas_call(
        last_unit_backward_kernel,
        in_specs=[pl.BlockSpec(memory_space=pltpu.SMEM)] + [vmem] * 5,
        out_shape=[
            jax.ShapeDtypeStruct(kv.shape, bf16),
            jax.ShapeDtypeStruct(q.shape, f32),
        ],
        scratch_shapes=[pltpu.VMEM(q.shape, bf16)],
        compiler_params=params(24),
        name="last_unit_backward",
    )(ids, q, kv, d_message, attn, log_total)


def units_backward_kernel(count, ids, *refs):
    messages, refs = refs[:count], refs[count:]
    q_ref, kv_ref, attn_ref, log_ref, last_ref, out_ref, d_out, delta, d_kv = refs
    rows = kv_ref.shape[1]
    me = ids[0]
    for t in range(count):
        block = lax.rem(me - t + count, count)
        value, row = unpack_out(messages[t][...], attn_ref[(count - t) % count])
        d_out[block] = value
        delta[block] = row
    for i in reversed(range(count)):
        d_query = None
        for first in range(0, i + 1, 2):
            places = list(range(first, min(first + 2, i + 1)))
            blocks = [kv_ref[j] for j in places]
            probs, d_scores = [], []
            for j, kv in zip(places, blocks):
                prob = jnp.exp(dot(kv, q_ref[i], NT) - log_ref[i])
                if j == i:
                    prob = jnp.where(causal_part(rows, PER), prob, 0.0)
                d_prob = dot(kv, d_out[i], NT)
                d_scores.append((prob * (d_prob - delta[i])).astype(bf16))
                probs.append(prob.astype(bf16))
            for j, prob, d_score in zip(places, probs, d_scores):
                term = dot(prob, d_out[i]) + dot(d_score, q_ref[i])
                d_kv[j] = term if i == count - 1 else d_kv[j] + term
            term = dot(jnp.concatenate([d.T for d in d_scores], axis=1), jnp.concatenate(blocks, axis=0))
            d_query = term if d_query is None else d_query + term
        tile = d_kv[i]
        write_long(
            out_ref,
            lax.rem(i - me + count, count),
            [d_query[h * rows : (h + 1) * rows] for h in range(PER)] + [tile, other_half(tile)],
            last_ref[i],
        )


def units_backward_call(ids, messages, q, kv, attn, log_total, last_d_kv):
    count, rows, _ = kv.shape
    wide = PER * rows
    vmem = pl.BlockSpec(memory_space=pltpu.VMEM)
    return pl.pallas_call(
        functools.partial(units_backward_kernel, count),
        in_specs=[pl.BlockSpec(memory_space=pltpu.SMEM)]
        + [vmem] * (count + 5),
        out_shape=jax.ShapeDtypeStruct((count, rows * 7 // 2, LANES), bf16),
        scratch_shapes=[
            pltpu.VMEM((count, wide, LANES), bf16),
            pltpu.VMEM((count, 1, wide), f32),
            pltpu.VMEM((count, rows, LANES), f32),
        ],
        compiler_params=params(56),
        name="units_backward",
    )(ids, *messages, q, kv, attn, log_total, last_d_kv)


def units_ffn_kernel(
    count,
    ids,
    x_ref,
    cot_ref,
    norm_ref,
    w_out_ref,
    w_gate_hbm,
    w_up_hbm,
    w_down_hbm,
    *refs,
):
    messages, last_message = refs[:count], refs[count]
    (
        mid_ref, attn, hid_hbm, d_gate_hbm, d_up_hbm, g_hbm,
        units, w_gate, w_up, w_down, cot, b, hid, d_gate, d_up, g_buf, w_sems, h_sems, g_sems,
    ) = refs[count + 1 :]
    me = ids[0]
    seqs, width, rows = x_ref.shape
    hidden = w_gate.shape[1]
    tiles = hidden // LANES
    loads = [
        pltpu.make_async_copy(source, target, w_sems.at[k])
        for k, (source, target) in enumerate(
            ((w_gate_hbm, w_gate), (w_up_hbm, w_up), (w_down_hbm, w_down))
        )
    ]
    for load in loads:
        load.start()
    for t in range(count):
        units[lax.rem(me - t + count, count)] = messages[t][...]
    units[count] = last_message[0]
    for s in range(seqs):
        here = slice(s * rows, (s + 1) * rows)
        heads = []
        for g in range(KV_HEADS):
            heads += read_short(units[s * KV_HEADS + g])
        parts = [join(heads[h], other_half(heads[h + 1])) for h in range(0, HEADS - 1, 2)]
        attn_rows = jnp.concatenate(parts + [heads[HEADS - 1][:, :HEAD_DIM]], axis=1).astype(bf16)
        attn[s] = attn_rows
        cot[here] = cot_ref[s].T
        mid_rows = x_ref[s].T.astype(f32) + dot(attn_rows, w_out_ref[...])
        scale = lax.rsqrt(
            jnp.sum(mid_rows * mid_rows, axis=-1, keepdims=True) * (1.0 / width) + eps_norm
        )
        mid_ref[s] = mid_rows
        b[here] = (mid_rows * scale * norm_ref[...]).astype(bf16)
    for load in loads:
        load.wait()
    chunk = 2 * LANES
    stores = []

    def store(source, target, sem):
        copy = pltpu.make_async_copy(source, target, sem)
        copy.start()
        stores.append(copy)

    for c in range(hidden // chunk):
        lanes = pl.ds(c * chunk, chunk)
        gate = dot(b[...], w_gate[:, lanes])
        up = dot(b[...], w_up[:, lanes])
        d_hid = dot(cot[...], w_down[:, lanes])
        sig = 1.0 / (1.0 + jnp.exp(-gate))
        active = gate * sig
        hid[:, lanes] = (active * up).astype(bf16)
        d_gate[:, lanes] = (d_hid * up * sig * (1.0 + gate * (1.0 - sig))).astype(bf16)
        d_up[:, lanes] = (d_hid * active).astype(bf16)
    for k, (source, target) in enumerate(((hid, hid_hbm), (d_gate, d_gate_hbm), (d_up, d_up_hbm))):
        store(source, target, h_sems.at[k])
    b_turned = b[...].T
    cot_turned = jnp.concatenate([cot_ref[s] for s in range(seqs)], axis=1)
    for k, (left, right) in enumerate(((b_turned, d_gate), (b_turned, d_up), (cot_turned, hid))):
        for c in range(hidden // chunk):
            product = dot(left, right[:, c * chunk : (c + 1) * chunk]).astype(bf16)
            for u in range(2):
                t = 2 * c + u
                half, at = ffn_place(k, t, tiles)
                here = pl.ds(at * width, width)
                g_buf[half, here, :] = product[:, u * LANES : (u + 1) * LANES]
                store(g_buf.at[half, here], g_hbm.at[half, here], g_sems.at[k * tiles + t])
    for copy in stores:
        copy.wait()


def units_ffn_call(ids, x, cot, messages, last_message, w_out, norm, w_gate, w_up, w_down):
    seqs, width, rows = x.shape
    hidden = w_gate.shape[1]
    count = len(messages)
    tokens = seqs * rows
    short = (rows * 3 // 2, LANES)
    tiles = hidden // LANES
    g_shape = (2, (tiles + tiles // 2) * width, LANES)
    vmem = pl.BlockSpec(memory_space=pltpu.VMEM)
    hbm = pl.BlockSpec(memory_space=pl.ANY)
    wide = (tokens, hidden)
    return pl.pallas_call(
        functools.partial(units_ffn_kernel, count),
        in_specs=[pl.BlockSpec(memory_space=pltpu.SMEM)]
        + [vmem] * 4
        + [hbm] * 3
        + [vmem] * (count + 1),
        out_specs=[vmem] * 2 + [hbm] * 4,
        out_shape=[
            jax.ShapeDtypeStruct((seqs, rows, width), f32),
            jax.ShapeDtypeStruct((seqs, rows, width), bf16),
            jax.ShapeDtypeStruct(wide, bf16),
            jax.ShapeDtypeStruct(wide, bf16),
            jax.ShapeDtypeStruct(wide, bf16),
            jax.ShapeDtypeStruct(g_shape, bf16),
        ],
        scratch_shapes=[
            pltpu.VMEM((count + 1,) + short, bf16),
            pltpu.VMEM(w_gate.shape, bf16),
            pltpu.VMEM(w_up.shape, bf16),
            pltpu.VMEM(w_down.shape, bf16),
            pltpu.VMEM((tokens, width), bf16),
            pltpu.VMEM((tokens, width), bf16),
            pltpu.VMEM(wide, bf16),
            pltpu.VMEM(wide, bf16),
            pltpu.VMEM(wide, bf16),
            pltpu.VMEM(g_shape, bf16),
            pltpu.SemaphoreType.DMA((3,)),
            pltpu.SemaphoreType.DMA((3,)),
            pltpu.SemaphoreType.DMA((3 * tiles,)),
        ],
        compiler_params=params(60),
        name="feed_forward",
    )(ids, x, cot, norm, w_out, w_gate, w_up, w_down, *messages, last_message)


def units_back_kernel(
    count,
    ids,
    mid_ref,
    cot_ref,
    d_gate_ref,
    d_up_ref,
    norm_ref,
    w_out_ref,
    w_gate_ref,
    w_up_ref,
    d_mid_ref,
    d_out_ref,
    d_last_ref,
    g_norm_ref,
):
    step = pl.program_id(0)
    me = ids[0]
    mid = mid_ref[0]
    rows, width = mid.shape
    cot = cot_ref[0].T
    scale = lax.rsqrt(jnp.sum(mid * mid, axis=-1, keepdims=True) * (1.0 / width) + eps_norm)
    normed = mid * scale
    d_b = dot(d_gate_ref[...], w_gate_ref[...], NT) + dot(d_up_ref[...], w_up_ref[...], NT)
    norm_term = jnp.sum(d_b * normed, axis=0, keepdims=True)
    e = d_b * norm_ref[...]
    mean = jnp.sum(e * normed, axis=-1, keepdims=True) * (1.0 / width)
    d_mid = cot.astype(f32) + scale * (e - normed * mean)
    d_mid_ref[0] = d_mid
    d_proj = d_mid.astype(bf16)
    d_tiles = head_tiles(dot(d_proj, w_out_ref[...], NT))
    d_heads = [
        d_tiles[h // 2] if h % 2 == 0 else other_half(d_tiles[h // 2]) for h in range(HEADS)
    ]
    for g in range(KV_HEADS):
        unit = step * KV_HEADS + g

        @pl.when(unit < count)
        def _(g=g, unit=unit):
            at = lax.rem(unit - me + count, count)
            write_short(d_out_ref, at, d_heads[g * PER : (g + 1) * PER])

        @pl.when(unit == count)
        def _(g=g):
            write_short(d_last_ref, 0, d_heads[g * PER : (g + 1) * PER])

    @pl.when(step == 0)
    def _():
        g_norm_ref[...] = norm_term

    @pl.when(step > 0)
    def _():
        g_norm_ref[...] += norm_term


def units_back_call(ids, mid, cot, d_gate, d_up, norm, w_out, w_gate, w_up, count):
    seqs, rows, width = mid.shape
    hidden = w_gate.shape[1]
    row = lambda *shape: pl.BlockSpec((1,) + shape, lambda s, *_: (s,) + (0,) * len(shape))
    part = pl.BlockSpec((rows, hidden), lambda s, *_: (s, 0))
    short = (rows * 3 // 2, LANES)
    return pl.pallas_call(
        functools.partial(units_back_kernel, count),
        grid_spec=pltpu.PrefetchScalarGridSpec(
            num_scalar_prefetch=1,
            grid=(seqs,),
            in_specs=[row(rows, width), row(width, rows), part, part, full_spec((1, width))]
            + [full_spec(w_out.shape), full_spec(w_gate.shape), full_spec(w_up.shape)],
            out_specs=[
                row(rows, width),
                full_spec((count,) + short),
                full_spec((1,) + short),
                full_spec((1, width)),
            ],
        ),
        out_shape=[
            jax.ShapeDtypeStruct((seqs, rows, width), f32),
            jax.ShapeDtypeStruct((count,) + short, bf16),
            jax.ShapeDtypeStruct((1,) + short, bf16),
            jax.ShapeDtypeStruct((1, width), f32),
        ],
        compiler_params=params(60),
        name="feed_back",
    )(ids, mid, cot, d_gate, d_up, norm, w_out, w_gate, w_up)


def units_out_kernel(
    mid_ref, attn_ref, hid_ref, d_mid_ref, g_norm_ref, w_down_ref, out_ref, g_ref, g_out
):
    step = pl.program_id(0)
    out_ref[0] = (mid_ref[0] + dot(hid_ref[...], w_down_ref[...], NT)).astype(bf16).T
    term = dot(attn_ref[0].T, d_mid_ref[0].astype(bf16))

    @pl.when(step == 0)
    def _():
        g_out[...] = term

    @pl.when(step > 0)
    def _():
        g_out[...] += term

    @pl.when(step == pl.num_programs(0) - 1)
    def _():
        column = jnp.broadcast_to(g_norm_ref[...], (8, g_norm_ref.shape[1])).T[:, :1]
        for t, tile in enumerate(head_tiles(g_out[...])):
            if t == g_ref.shape[0] - 1:
                tile = with_column(tile, column)
            g_ref[t] = tile.astype(bf16)


def units_out_call(mid, attn, hid, d_mid, g_norm, w_down):
    seqs, rows, width = mid.shape
    hidden = w_down.shape[1]
    row = lambda *shape: pl.BlockSpec((1,) + shape, lambda s: (s,) + (0,) * len(shape))
    g_shape = (-(-width // LANES), width, LANES)
    return pl.pallas_call(
        units_out_kernel,
        grid=(seqs,),
        in_specs=[
            row(rows, width),
            row(rows, width),
            pl.BlockSpec((rows, hidden), lambda s: (s, 0)),
            row(rows, width),
            full_spec((1, width)),
            full_spec(w_down.shape),
        ],
        out_specs=[row(width, rows), full_spec(g_shape)],
        out_shape=[
            jax.ShapeDtypeStruct((seqs, width, rows), bf16),
            jax.ShapeDtypeStruct(g_shape, bf16),
        ],
        scratch_shapes=[pltpu.VMEM((width, width), f32)],
        compiler_params=params(60),
        name="feed_out",
    )(mid, attn, hid, d_mid, g_norm, w_down)


def units_last_kernel(
    count, ids, x_ref, a_ref, norm_ref, wq_ref, wk_ref, wv_ref, cos_ref, sin_ref, d_mid_ref, last_q_ref,
    g_out_ref, *refs,
):
    messages = refs[:count]
    out_ref, g_ref, units, g_query, g_pairs, d_norm = refs[count:]
    step = pl.program_id(0)
    me = ids[0]
    x = x_ref[0].T.astype(f32)
    rows, width = x.shape

    @pl.when(step == 0)
    def _():
        for t in range(count):
            units[lax.rem(me - t + count, count)] = messages[t][: rows * 5 // 2]
        last_kv = sum(messages[t][rows * 5 // 2 :].astype(f32) for t in range(count))
        heads = [last_q_ref[h * rows : (h + 1) * rows] for h in range(PER)]
        write_long(units, count, heads + [last_kv, other_half(last_kv)])

    cos, sin = cos_ref[0], sin_ref[0]

    def turn(tile):
        return tile * cos - swap_halves(tile) * sin

    heads, keys, values = [], [], []
    for g in range(KV_HEADS):
        parts, kv = read_long(units[step * KV_HEADS + g], rows)
        heads += parts
        keys.append(kv)
        values.append(other_half(kv))

    def in_tiles(parts, scale):
        tiles = [
            join(parts[h], other_half(parts[h + 1])) for h in range(0, len(parts) - 1, 2)
        ] + [parts[-1]]
        return tiles if scale is None else [turn(t) * scale for t in tiles]

    def flat(tiles):
        return jnp.concatenate(tiles[:-1] + [tiles[-1][:, :HEAD_DIM]], axis=1).astype(bf16)

    d_query = flat(in_tiles(heads, 0.125))
    key_tiles = in_tiles(keys, 1.0)
    d_key, d_value = flat(key_tiles), flat(in_tiles(values, None))
    turned = [key_tiles[g // 2] if g % 2 == 0 else other_half(key_tiles[g // 2]) for g in range(KV_HEADS)]
    pairs = jnp.concatenate(
        [join(turned[g], other_half(values[g])) for g in range(KV_HEADS)], axis=1
    ).astype(bf16)
    a_turned = a_ref[0].T
    query_term = dot(a_turned, d_query)
    pair_term = dot(a_turned, pairs)
    d_a = (
        dot(d_query, wq_ref[...], NT) + dot(d_key, wk_ref[...]) + dot(d_value, wv_ref[...])
    )
    scale = lax.rsqrt(jnp.sum(x * x, axis=-1, keepdims=True) * (1.0 / width) + eps_norm)
    normed = x * scale
    norm_term = jnp.sum(d_a * normed, axis=0, keepdims=True)

    @pl.when(step == 0)
    def _():
        d_norm[...] = norm_term
        g_query[...] = query_term
        g_pairs[...] = pair_term

    @pl.when(step > 0)
    def _():
        d_norm[...] += norm_term
        g_query[...] += query_term
        g_pairs[...] += pair_term

    e = d_a * norm_ref[...]
    mean = jnp.sum(e * normed, axis=-1, keepdims=True) * (1.0 / width)
    out_ref[0] = (d_mid_ref[0] + scale * (e - normed * mean)).astype(bf16).T

    @pl.when(step == pl.num_programs(0) - 1)
    def _():
        square = -(-width // LANES)
        column = jnp.broadcast_to(d_norm[...], (8, width)).T[:, :1]
        for t, tile in enumerate(head_tiles(g_query[...])):
            if t == square - 1:
                tile = with_column(tile, column)
            put(g_ref, attn_place(t), width, tile.astype(bf16))
        for g in range(KV_HEADS):
            tile = g_pairs[:, g * LANES : (g + 1) * LANES]
            put(g_ref, attn_place(square + g), width, tile.astype(bf16))
        for t in range(square):
            put(g_ref, attn_place(square + KV_HEADS + t), width, g_out_ref[t])
        clear_rest(g_ref, 2 * square + KV_HEADS, width)


def clear_rest(g_ref, places, width):
    for half in range(2):
        used = (places + 1 - half) // 2 * width
        left_over = g_ref.shape[1] - used
        if left_over:
            g_ref[half, used:, :] = jnp.zeros((left_over, LANES), bf16)


def units_last_call(
    ids, x, a, norm, w_query, w_key, w_value, cos, sin, d_mid, last_d_q, g_out, messages, parts
):
    seqs, width, rows = x.shape
    count = len(messages)
    row = lambda *shape: pl.BlockSpec((1,) + shape, lambda s, *_: (s,) + (0,) * len(shape))
    places = -(-(2 * -(-width // LANES) + KV_HEADS) // 2)
    g_shape = (2, half_rows(places, width, parts), LANES)
    return pl.pallas_call(
        functools.partial(units_last_kernel, count),
        grid_spec=pltpu.PrefetchScalarGridSpec(
            num_scalar_prefetch=1,
            grid=(seqs,),
            in_specs=[
                row(width, rows),
                row(rows, width),
                full_spec((1, width)),
                full_spec(w_query.shape),
                full_spec(w_key.shape),
                full_spec(w_value.shape),
                row(rows, LANES),
                row(rows, LANES),
                row(rows, width),
                full_spec(last_d_q.shape),
                full_spec(g_out.shape),
            ]
            + [full_spec(m.shape) for m in messages],
            out_specs=[row(width, rows), full_spec(g_shape)],
            scratch_shapes=[
                pltpu.VMEM((count + 1, rows * 5 // 2, LANES), bf16),
                pltpu.VMEM((width, width), f32),
                pltpu.VMEM((width, KV_HEADS * LANES), f32),
                pltpu.VMEM((1, width), f32),
            ],
        ),
        out_shape=[
            jax.ShapeDtypeStruct((seqs, width, rows), bf16),
            jax.ShapeDtypeStruct(g_shape, bf16),
        ],
        compiler_params=params(60),
        name="last_part",
    )(ids, x, a, norm, w_query, w_key, w_value, cos, sin, d_mid, last_d_q, g_out, *messages)


def to_all(messages):
    count = messages.shape[0]
    return [messages[0]] + [
        lax.ppermute(messages[t], "seq", [(i, (i + t) % count) for i in range(count)])
        for t in range(1, count)
    ]


def rope_tables(positions):
    half = HEAD_DIM // 2
    lane = jnp.arange(LANES, dtype=jnp.int32)
    frequency = jnp.exp((lane % half).astype(f32) * (-math.log(10000.0) / half))
    angles = positions.T.astype(f32)[..., None] * frequency
    return jnp.cos(angles), jnp.where(lane % HEAD_DIM < half, -1.0, 1.0) * jnp.sin(angles)


def spread_layer(
    x, cot, cos, sin, norm_one, norm_two, w_query, wk_turned, wv_turned, w_out, w_gate, w_up,
    w_down_turned, count, devices, sum_over, places_ok,
):
    seqs, width, rows = x.shape
    me = lax.axis_index("seq")
    a, q, kv = pre_call(x, norm_one, w_query, wk_turned, wv_turned, cos, sin)
    rounds, numbers = gather_blocks(kv, count)
    last = len(rounds) - 2

    def ids_of(picked):
        return jnp.stack([me] + [k for part in picked for k in part]).astype(jnp.int32)

    state = forward_call(ids_of(numbers[:last]), q, kv, rounds[:last], None, False)
    far, far_ids = rounds[last:], ids_of(numbers[last:])
    attn, log_total = forward_call(far_ids, q, None, far, state, True)
    (block_out, b, hid, d_gate, d_up, d_mid, d_proj, d_out, delta, g_norm_mlp) = middle_call(
        x, cot, attn, w_out, norm_two, w_gate, w_up, w_down_turned
    )
    flat = lambda t: t.reshape(seqs * rows, t.shape[-1])
    g_ffn = ffn_grad_call(flat(b), cot, flat(hid), flat(d_gate), flat(d_up))
    g_ffn = lax.psum(g_ffn, ("seq", "batch"))
    common = (q, d_out, log_total, delta)
    _, far_terms, d_query = backward_call(far_ids, *common, None, far, None, None)
    far_terms = [jnp.concatenate([t, u], axis=0) for t, u in zip(*far_terms)]
    got = [return_round(far_terms, last, count)]
    _, mid_terms, d_query = backward_call(
        ids_of(numbers[last - 1 : last]), *common, None, rounds[last - 1 : last], d_query, None
    )
    half = far_terms[0].shape[0] // 2
    mid_terms = [add_low(t, g[half:]) for t, g in zip(mid_terms[0], got[0])]
    got.append(return_round(mid_terms, last - 1, count))
    own_terms, near_terms, d_q = backward_call(
        ids_of(numbers[: last - 1]), *common, kv, rounds[: last - 1], d_query, (cos, sin),
        tuple(mid_terms),
    )
    for r in reversed(range(last - 1)):
        size = 1 << r
        terms = [
            add_low(t, *(g[s][size : 2 * size] for g in got)) for s, t in enumerate(near_terms[r])
        ]
        got.append(return_round(terms, r, count))
    d_kv = jnp.concatenate(
        [add_low(own_terms[s : s + 1], *(g[s][:1] for g in got)) for s in range(seqs)], axis=0
    )
    d_aq, g_query, g_out = query_grad_call(
        flat(a), flat(attn), flat(d_proj), flat(d_q), g_norm_mlp, w_query
    )
    d_tokens, g_attn = last_call(
        x, a, norm_one, wk_turned, wv_turned, cos, sin, d_kv,
        d_aq.reshape(seqs, rows, width), d_mid, g_query, g_out, devices,
    )
    return block_out, d_tokens, g_ffn, sum_over(g_attn)


def units_layer(
    x, cot, cos, sin, norm_one, norm_two, w_query, wk_turned, wv_turned, w_out, w_gate, w_up,
    w_down_turned, count, devices, sum_over, places_ok,
):
    seqs, width, rows = x.shape
    flat = lambda t: t.reshape(seqs * rows, t.shape[-1])
    ids = lax.axis_index("seq").astype(jnp.int32).reshape(1)
    a, messages, last_q, last_kv = units_pre_call(
        ids, x, norm_one, w_query, wk_turned, wv_turned, cos, sin, count
    )
    masks = exchange_masks(count)
    swap = lambda part, mask: lax.ppermute(part, "seq", [(i, i ^ mask) for i in range(count)])
    arrived = to_all(messages)
    for mask in masks[:-1]:
        last_kv = jnp.concatenate([last_kv, swap(last_kv, mask)], axis=0)
    attn_out, log_total, q, kv = units_forward_call(ids, arrived, (last_kv,))
    last_kv = jnp.concatenate([last_kv, swap(last_kv, masks[-1])], axis=0)
    last_attn, last_log = last_unit_forward_call(ids, last_q, last_kv)
    mid, attn, hid, d_gate, d_up, g_ffn = units_ffn_call(
        ids, x, cot, to_all(attn_out), last_attn, w_out, norm_two, w_gate, w_up, w_down_turned
    )
    g_ffn = lax.psum(g_ffn, ("seq", "batch"))

    def backward(mid, attn, hid, d_gate, d_up, q, kv, attn_out, log_total, last_attn, last_log, a):
        d_mid, d_messages, d_last, g_norm_mlp = units_back_call(
            ids, mid, cot, d_gate, d_up, norm_two, w_out, w_gate, w_up, count
        )
        block_out, g_out = units_out_call(mid, attn, hid, d_mid, g_norm_mlp, w_down_turned)
        last_d_kv, last_d_q = last_unit_backward_call(
            ids, last_q, last_kv, d_last[0], last_attn[0], last_log
        )
        d_all = units_backward_call(
            ids, to_all(d_messages), q, kv, attn_out, log_total, last_d_kv
        )
        d_tokens, g_attn = units_last_call(
            ids, x, a, norm_one, w_query, wk_turned, wv_turned, cos, sin, d_mid, last_d_q, g_out,
            to_all(d_all), devices,
        )
        return (block_out, d_tokens) + sum_over(g_attn)

    block_out, d_tokens, *attn_sums = in_one_piece(
        places_ok,
        backward,
        (mid, attn, hid, d_gate, d_up, q, kv, attn_out, log_total, last_attn, last_log, a),
    )
    return block_out, d_tokens, g_ffn, attn_sums


def in_one_piece(always, part, operands):
    shapes = jax.eval_shape(part, *operands)

    def never(*_):
        return jax.tree.map(lambda t: jnp.zeros(t.shape, t.dtype), shapes)

    return lax.cond(always, part, never, *operands)


def on_device(
    tokens,
    positions,
    norm_attn,
    w_query,
    w_key,
    w_value,
    w_out,
    norm_mlp,
    w_gate,
    w_up,
    w_down,
    cotangent,
):
    rows, seqs, width = tokens.shape
    hidden = w_gate.shape[1]
    kv_width = KV_HEADS * HEAD_DIM
    count, batches = lax.axis_size("seq"), lax.axis_size("batch")
    me = lax.axis_index("seq")
    devices = count * batches
    stages = device_stages(count, batches)
    places = stage_places(stages, me * batches + lax.axis_index("batch"))
    x = jnp.transpose(tokens, (1, 2, 0))
    cot = jnp.transpose(cotangent, (1, 2, 0))
    wk_turned, wv_turned, w_down_turned = w_key.T, w_value.T, w_down.T
    cos, sin = rope_tables(positions)
    norm_one, norm_two = norm_attn[None], norm_mlp[None]
    def sum_over(value):
        for stage, place in zip(stages, places):
            value = scatter_stage(value, stage, place, devices)
        return gather_sums(value, stages, places, devices, 1)

    layer = units_layer if count == seqs * KV_HEADS - 1 else spread_layer
    block_out, d_tokens, g_ffn, attn_sums = layer(
        x, cot, cos, sin, norm_one, norm_two, w_query, wk_turned, wv_turned, w_out, w_gate, w_up,
        w_down_turned, count, devices, sum_over, positions[0, 0] >= 0,
    )
    side = places[0].reshape(1).astype(jnp.int32)
    g_gate, g_up, g_down = ffn_unfold_call(g_ffn, width, hidden)
    g_query, g_key, g_value, g_norm_attn, g_out, g_norm_mlp = unfold_call(
        attn_unfold_kernel,
        "attn_unfold",
        (side, *attn_sums),
        [(width, width), (kv_width, width), (kv_width, width), (1, width)]
        + [(width, width), (1, width)],
    )
    return (
        jnp.transpose(block_out, (2, 0, 1)),
        jnp.transpose(d_tokens, (2, 0, 1)),
        g_norm_attn[0],
        g_query,
        g_key.T,
        g_value.T,
        g_out,
        g_norm_mlp[0],
        g_gate,
        g_up,
        g_down.T,
    )


def solution(mesh):
    split = P("seq", "batch", None)
    return jax.shard_map(
        on_device,
        mesh=mesh,
        in_specs=(split, P("seq", "batch")) + (P(),) * 9 + (split,),
        out_specs=(split, split) + (P(),) * 9,
        check_vma=False,
    )
```

profile of v0, /device:TPU:0, one launch (start us, length us, event | category | flops | bytes accessed | tf_op | source)
XLA Modules:
  0.0 330.9 jit_solution(15027242779744002981)
XLA Ops:
  10.1 7.4 %project.1 = (bf16[3,256,576]{2,1,0:T(8,128)(2,1)}, bf16[8,640,128]{2,1,0:T(8,128)(2,1)}, bf16[768,128]{1,0:T(8,128)(2,1)S(1)}, bf16[1,256,128]{2,1,0:T(8,128)(2,1)}) custom-call(s32[1]{0:T(128)} %bitcast.48.ids, bf16[3,576,256]{2,1,0:T(8,128)(2,1)} %bitcast.124, f32[1,576]{1,0:T(1,128)S(1)} %broadcast_in_dim.18.norm_ref, bf16[576,576]{1,0:T(8,128)(2,1)} %wq_ref.1, ...), custom_call_target="tpu_custom_call" | custom-call | tf_op jit(solution)/shard_map/project/pallas_call | solution.py:1017
  17.5 3.0 collective-permute-start.35
  22.1 2.1 collective-permute-start.29
  25.9 2.4 collective-permute-start.30
  29.5 2.6 collective-permute-done.28.refs_1_
  33.7 4.5 %collective-permute-done.36 = bf16[2,256,128]{2,1,0:T(8,128)(2,1)S(1)} collective-permute-done((bf16[2,256,128]{2,1,0:T(8,128)(2,1)S(1)}, bf16[2,256,128]{2,1,0:T(8,128)(2,1)S(1)}, u32[]{:S(2)}, u32[]{:S(2)}) %collective-permute-start.36) | collective-permute-done | bytes 131104 | tf_op jit(solution)/shard_map/ppermute | solution.py:1748
  38.3 3.3 collective-permute-start.34
  41.7 2.3 collective-permute-done.30.refs_3_
  43.9 16.4 %collective-permute-start.44 = (bf16[4,256,128]{2,1,0:T(8,128)(2,1)S(1)}, bf16[4,256,128]{2,1,0:T(8,128)(2,1)S(1)}, u32[]{:S(2)}, u32[]{:S(2)}) collective-permute-start(bf16[4,256,128]{2,1,0:T(8,128)(2,1)S(1)} %get-tuple-element.227.refs_8_), channel_id=1, source_target_pairs={{0,24},{4,28},{8,16},{12,20},{16,8},{20,12},{24,0},{28,4},{1,25},{... | collective-permute-start | bytes 786440 | tf_op jit(solution)/shard_map/ppermute | solution.py:1748
  60.3 13.0 %units_forward.1 = (bf16[8,384,128]{2,1,0:T(8,128)(2,1)S(1)}, f32[8,1,768]{2,1,0:T(1,128)}, bf16[8,768,128]{2,1,0:T(8,128)(2,1)}, bf16[8,256,128]{2,1,0:T(8,128)(2,1)}) custom-call(s32[1]{0:T(128)} %bitcast.48.ids, bf16[640,128]{1,0:T(8,128)(2,1)S(1)} %get-tuple-element.217.refs_0_, bf16[640,128]{1,0:T(8,128)(2,1)S(1)} %collective-permute-done.28.refs_1_, ...), custom_call_target="tpu_custom_call" | custom-call | tf_op jit(solution)/shard_map/units_forward/pallas_call | solution.py:1102
  76.8 3.3 collective-permute-start.40
  80.0 2.5 collective-permute-done.37.refs_1_
  83.4 8.8 %collective-permute-start.43 = (bf16[384,128]{1,0:T(8,128)(2,1)S(1)}, bf16[384,128]{1,0:T(8,128)(2,1)S(1)}, u32[]{:S(2)}, u32[]{:S(2)}) collective-permute-start(bf16[384,128]{1,0:T(8,128)(2,1)S(1)} %get-tuple-element.218), channel_id=1, source_target_pairs={{0,28},{4,0},{8,4},{12,8},{16,12},{20,16},{24,20},{28,24},{1,29},{... | collective-permute-start | bytes 294920 | tf_op jit(solution)/shard_map/ppermute | solution.py:1669
  92.3 3.5 %last_unit_forward.1 = (bf16[1,384,128]{2,1,0:T(8,128)(2,1)}, f32[1,768]{1,0:T(1,128)}) custom-call(s32[1]{0:T(128)} %bitcast.48.ids, bf16[768,128]{1,0:T(8,128)(2,1)S(1)} %get-tuple-element.162.q_ref, bf16[8,256,128]{2,1,0:T(8,128)(2,1)S(1)} %constant_dynamic-update-slice_fusion.3.kv_ref), custom_call_target="tpu_custom_call" | custom-call | tf_op jit(solution)/shard_map/last_unit_forward/pallas_call | solution.py:1133
  96.6 20.5 %feed_forward.1 = (f32[3,256,576]{2,1,0:T(8,128)S(1)}, bf16[3,256,576]{2,1,0:T(8,128)(2,1)}, bf16[768,1536]{1,0:T(8,128)(2,1)}, bf16[768,1536]{1,0:T(8,128)(2,1)...) custom-call(s32[1]{0:T(128)} %bitcast.48.ids, bf16[3,576,256]{2,1,0:T(8,128)(2,1)S(1)} %bitcast.125, ...), custom_call_target="tpu_custom_call" | custom-call | tf_op jit(solution)/shard_map/feed_forward/pallas_call | solution.py:1353
  119.2 192.1 %conditional.1 = (bf16[3,576,256]{2,1,0:T(8,128)(2,1)}, bf16[3,576,256]{2,1,0:T(8,128)(2,1)}, bf16[4096,128]{1,0:T(8,128)(2,1)}, bf16[4096,128]{1,0:T(8,128)(2,1)}) conditional(s32[]{:T(128)} %bitcast.47, () %tuple.16, (s32[1]{0:T(128)}, f32[3,256,576]{2,1,0:T(8,128)S(1)}, bf16[3,576,256]{2,1,0:T(8,128)(2,1)}, bf16[768,1536]{1,0:T(8,128)(2,1)}, ...), branch_computations={%region_0.1_spmd, %region_1.2_spmd} | conditional | flops 6684727 | bytes 64948420 | solution.py:1791
  119.2 12.5 %feed_back.1 = (f32[3,256,576]{2,1,0:T(8,128)}, bf16[8,384,128]{2,1,0:T(8,128)(2,1)}, bf16[1,384,128]{2,1,0:T(8,128)(2,1)}, f32[1,576]{1,0:T(1,128)}) custom-call(s32[1]{0:T(128)} %get-tuple-element.79.ids, f32[3,256,576]{2,1,0:T(8,128)S(1)} %get-tuple-element.76.mid_ref, bf16[3,576,256]{2,1,0:T(8,128)(2,1)} %get-tuple-element.80.cot_ref, ...), custom_call_target="tpu_custom_call" | custom-call | tf_op jit(solution)/shard_map/cond/branch_1_fun/feed_back/pallas_call | solution.py:1449
  131.8 2.0 slice_bitcast_fusion.8
  135.9 3.2 collective-permute-start.3
  139.1 3.2 collective-permute-start.4
  142.3 2.1 collective-permute-done.refs_1_
  144.5 3.9 %collective-permute-start.6 = (bf16[384,128]{1,0:T(8,128)(2,1)S(1)}, bf16[384,128]{1,0:T(8,128)(2,1)S(1)}, u32[]{:S(2)}, u32[]{:S(2)}) collective-permute-start(bf16[384,128]{1,0:T(8,128)(2,1)S(1)} %get-tuple-element.199), channel_id=1, source_target_pairs={{0,28},{4,0},{8,4},{12,8},{16,12},{20,16},{24,20},{28,24},{1,29},{... | collective-permute-start | bytes 294920 | tf_op jit(solution)/shard_map/cond/branch_1_fun/ppermute | solution.py:1669
  149.2 5.9 %last_unit_backward.1 = (bf16[8,256,128]{2,1,0:T(8,128)(2,1)S(1)}, f32[768,128]{1,0:T(8,128)S(1)}) custom-call(s32[1]{0:T(128)} %get-tuple-element.79.ids, bf16[768,128]{1,0:T(8,128)(2,1)} %get-tuple-element.99.q_ref, bf16[8,256,128]{2,1,0:T(8,128)(2,1)S(1)} %copy-done.10, bf16[384,128]{1,0:T(8,128)(2,1)S(1)} %bitcast.123, bf16[384,128]{1,0:T(8,128)(2,1)} %bitcast.146, ...), custom_call_target="tpu_custom_call" | custom-call | tf_op jit(solution)/shard_map/cond/branch_1_fun/last_unit_backward/pallas_call | solution.py:1189
  157.8 24.5 %units_backward.1 = bf16[8,896,128]{2,1,0:T(8,128)(2,1)} custom-call(s32[1]{0:T(128)} %get-tuple-element.79.ids, bf16[384,128]{1,0:T(8,128)(2,1)} %get-tuple-element.206.refs_0_, bf16[384,128]{1,0:T(8,128)(2,1)} %copy-done.24, bf16[384,128]{1,0:T(8,128)(2,1)} %copy-done.25, bf16[384,128]{1,0:T(8,128)(2,1)} %copy-done.26, bf16[384,128]{1,0:T(8,128)(2,1)} %copy-done.27, ...), custom_call_target="tpu_custom_call" | custom-call | tf_op jit(solution)/shard_map/cond/branch_1_fun/units_backward/pallas_call | solution.py:1243
  182.3 2.7 slice_bitcast_fusion
  185.8 7.2 %collective-permute-start.8 = (bf16[896,128]{1,0:T(8,128)(2,1)S(1)}, bf16[896,128]{1,0:T(8,128)(2,1)S(1)}, u32[]{:S(2)}, u32[]{:S(2)}) collective-permute-start(bf16[896,128]{1,0:T(8,128)(2,1)S(1)} %get-tuple-element.193), channel_id=1, source_target_pairs={{0,8},{4,12},{8,16},{12,20},{16,24},{20,28},{24,0},{28,4},{1,9},{5... | collective-permute-start | bytes 688136 | tf_op jit(solution)/shard_map/cond/branch_1_fun/ppermute | solution.py:1669
  194.3 3.4 %collective-permute-start.11 = (bf16[896,128]{1,0:T(8,128)(2,1)}, bf16[896,128]{1,0:T(8,128)(2,1)}, u32[]{:S(2)}, u32[]{:S(2)}) collective-permute-start(bf16[896,128]{1,0:T(8,128)(2,1)} %get-tuple-element.190), channel_id=1, source_target_pairs={{0,20},{4,24},{8,28},{12,0},{16,4},{20,8},{24,12},{28,16},{1,21},{... | collective-permute-start | bytes 688136 | tf_op jit(solution)/shard_map/cond/branch_1_fun/ppermute | solution.py:1669
  197.6 1.7 collective-permute-done.7.refs_1_
  201.2 5.2 %collective-permute-start.13 = (bf16[896,128]{1,0:T(8,128)(2,1)}, bf16[896,128]{1,0:T(8,128)(2,1)}, u32[]{:S(2)}, u32[]{:S(2)}) collective-permute-start(bf16[896,128]{1,0:T(8,128)(2,1)} %get-tuple-element.188), channel_id=1, source_target_pairs={{0,28},{4,0},{8,4},{12,8},{16,12},{20,16},{24,20},{28,24},{1,29},{... | collective-permute-start | bytes 688136 | tf_op jit(solution)/shard_map/cond/branch_1_fun/ppermute | solution.py:1669
  206.4 7.4 %feed_out.1 = (bf16[3,576,256]{2,1,0:T(8,128)(2,1)}, bf16[5,576,128]{2,1,0:T(8,128)(2,1)}) custom-call(f32[3,256,576]{2,1,0:T(8,128)S(1)} %get-tuple-element.76.mid_ref, bf16[3,256,576]{2,1,0:T(8,128)(2,1)} %get-tuple-element.77.attn_ref, bf16[768,1536]{1,0:T(8,128)(2,1)} %get-tuple-element.78.hid_ref, f32[3,256,576]{2,1,0:T(8,128)} %get-tuple-element.87.d_mid_ref, ...), custom_call_target="tpu_custom_call" | custom-call | tf_op jit(solution)/shard_map/cond/branch_1_fun/feed_out/pallas_call | solution.py:1503
  213.8 5.4 %collective-permute-done.9.refs_3_ = bf16[896,128]{1,0:T(8,128)(2,1)} collective-permute-done((bf16[896,128]{1,0:T(8,128)(2,1)}, bf16[896,128]{1,0:T(8,128)(2,1)}, u32[]{:S(2)}, u32[]{:S(2)}) %collective-permute-start.9) | collective-permute-done | bytes 229408 | tf_op jit(solution)/shard_map/cond/branch_1_fun/ppermute | solution.py:1669
  220.7 2.5 collective-permute-done.13.refs_7_
  223.1 11.2 %last_part.1 = (bf16[3,576,256]{2,1,0:T(8,128)(2,1)}, bf16[2,4096,128]{2,1,0:T(8,128)(2,1)}) custom-call(s32[1]{0:T(128)} %get-tuple-element.79.ids, bf16[3,576,256]{2,1,0:T(8,128)(2,1)S(1)} %get-tuple-element.91.x_ref, bf16[3,256,576]{2,1,0:T(8,128)(2,1)} %get-tuple-element.92.a_ref, f32[1,576]{1,0:T(1,128)S(1)} %get-tuple-element.93.norm_ref, ...), custom_call_target="tpu_custom_call" | custom-call | tf_op jit(solution)/shard_map/cond/branch_1_fun/last_part/pallas_call | solution.py:1630
  235.7 2.6 collective-permute-done.14
  239.9 4.3 %collective-permute-start.17 = (bf16[1024,128]{1,0:T(8,128)(2,1)S(1)}, bf16[1024,128]{1,0:T(8,128)(2,1)S(1)}, u32[]{:S(2)}, u32[]{:S(2)}) collective-permute-start(bf16[1024,128]{1,0:T(8,128)(2,1)S(1)} %get-tuple-element.197), channel_id=1, source_target_pairs={{0,6},{1,7},{2,4},{3,5},{4,2},{5,3},{6,0},{7,1},{8,14},{9,15},{10,... | collective-permute-start | bytes 786440 | tf_op jit(solution)/shard_map/cond/branch_1_fun/ppermute | solution.py:784
  244.9 6.5 %collective-permute-done.17 = bf16[1024,128]{1,0:T(8,128)(2,1)S(1)} collective-permute-done((bf16[1024,128]{1,0:T(8,128)(2,1)S(1)}, bf16[1024,128]{1,0:T(8,128)(2,1)S(1)}, u32[]{:S(2)}, u32[]{:S(2)}) %collective-permute-start.17) | collective-permute-done | bytes 262176 | tf_op jit(solution)/shard_map/cond/branch_1_fun/ppermute | solution.py:784
  251.4 8.1 %collective-permute-done.16 = bf16[1024,128]{1,0:T(8,128)(2,1)S(1)} collective-permute-done((bf16[1024,128]{1,0:T(8,128)(2,1)S(1)}, bf16[1024,128]{1,0:T(8,128)(2,1)S(1)}, u32[]{:S(2)}, u32[]{:S(2)}) %collective-permute-start.16) | collective-permute-done | bytes 262176 | tf_op jit(solution)/shard_map/cond/branch_1_fun/ppermute | solution.py:784
  259.8 11.0 %collective-permute-start.20 = (bf16[256,128]{1,0:T(8,128)(2,1)S(1)}, bf16[256,128]{1,0:T(8,128)(2,1)S(1)}, u32[]{:S(2)}, u32[]{:S(2)}) collective-permute-start(bf16[256,128]{1,0:T(8,128)(2,1)S(1)} %get-tuple-element.208), channel_id=1, source_target_pairs={{0,16},{1,17},{2,18},{3,19},{4,20},{5,21},{6,22},{7,23},{8,24},{9,... | collective-permute-start | bytes 196616 | tf_op jit(solution)/shard_map/cond/branch_1_fun/ppermute | solution.py:784
  272.3 2.4 collective-permute-done.20
  274.7 2.4 collective-permute-done.19
  277.2 2.7 collective-permute-start.23
  280.9 4.2 %collective-permute-done.23 = bf16[256,128]{1,0:T(8,128)(2,1)S(1)} collective-permute-done((bf16[256,128]{1,0:T(8,128)(2,1)S(1)}, bf16[256,128]{1,0:T(8,128)(2,1)S(1)}, u32[]{:S(2)}, u32[]{:S(2)}) %collective-permute-start.23) | collective-permute-done | bytes 65568 | tf_op jit(solution)/shard_map/cond/branch_1_fun/ppermute | solution.py:784
  285.1 2.6 collective-permute-done.22
  292.1 9.6 %collective-permute-done.26 = bf16[4,256,128]{2,1,0:T(8,128)(2,1)S(1)} collective-permute-done((bf16[4,256,128]{2,1,0:T(8,128)(2,1)S(1)}, bf16[4,256,128]{2,1,0:T(8,128)(2,1)S(1)}, u32[]{:S(2)}, u32[]{:S(2)}) %collective-permute-start.26) | collective-permute-done | bytes 262176 | tf_op jit(solution)/shard_map/cond/branch_1_fun/ppermute | solution.py:784
  301.7 4.4 %collective-permute-done.25 = bf16[4,256,128]{2,1,0:T(8,128)(2,1)S(1)} collective-permute-done((bf16[4,256,128]{2,1,0:T(8,128)(2,1)S(1)}, bf16[4,256,128]{2,1,0:T(8,128)(2,1)S(1)}, u32[]{:S(2)}, u32[]{:S(2)}) %collective-permute-start.25) | collective-permute-done | bytes 262176 | tf_op jit(solution)/shard_map/cond/branch_1_fun/ppermute | solution.py:784
  308.0 3.0 collective-permute-done.27
  311.3 3.9 %attn_unfold.1 = (f32[576,576]{1,0:T(8,128)}, f32[192,576]{1,0:T(8,128)}, f32[192,576]{1,0:T(8,128)}, f32[1,576]{1,0:T(1,128)S(1)}, f32[576,576]{1,0:T(8,128)}, /*index=5*/f32[1,576]{1,0:T(1,128)S(1)}) custom-call(s32[1]{0:T(128)} %bitcast.73.side, bf16[4096,128]{1,0:T(8,128)(2,1)} %get-tuple-element.176.mine, bf16[4096,128]{1,0:T(8,128)(2,1)} %get-tuple-element.177.other), custom_call_target="tpu_custom_call" | custom-call | tf_op jit(solution)/shard_map/attn_unfold/pallas_call | solution.py:605
  316.4 7.2 %ffn_unfold.1 = (f32[576,1536]{1,0:T(8,128)}, f32[576,1536]{1,0:T(8,128)}, f32[576,1536]{1,0:T(8,128)}) custom-call(bf16[2,18,576,128]{3,2,1,0:T(8,128)(2,1)} %all-reduce.2.cloned.1.call-done.gate_in.up_in.down_in, bf16[2,18,576,128]{3,2,1,0:T(8,128)(2,1)} %all-reduce.2.cloned.1.call-done.gate_in.up_in.down_in, ...), custom_call_target="tpu_custom_call" | custom-call | tf_op jit(solution)/shard_map/ffn_unfold/pallas_call | solution.py:578
  (160 shorter events, 40.4 us)
Async XLA Ops:
  7.2 309.2 %all-reduce.2.cloned.1.call-start = ((), (), s32[]{:S(2)}) async-start(), calls=%async_computation | async-start | bytes 10616832 | tf_op jit(solution)/shard_map/psum | solution.py:1758
  17.5 74.8 %copy-start.12 = (bf16[768,128]{1,0:T(8,128)(2,1)}, bf16[768,128]{1,0:T(8,128)(2,1)S(1)}, u32[]{:S(2)}) copy-start(bf16[768,128]{1,0:T(8,128)(2,1)S(1)} %get-tuple-element.162.q_ref) | copy-start | bytes 589828
  17.5 6.7 %collective-permute-start.35 = (bf16[1,256,128]{2,1,0:T(8,128)(2,1)}, bf16[1,256,128]{2,1,0:T(8,128)(2,1)S(1)}, u32[]{:S(2)}, u32[]{:S(2)}) collective-permute-start(bf16[1,256,128]{2,1,0:T(8,128)(2,1)} %get-tuple-element.160), channel_id=1, source_target_pairs={{0,4},{4,0},{8,12},{12,8},{16,20},{20,16},{24,28},{28,24},{1,5},{5... | collective-permute-start | bytes 196616 | tf_op jit(solution)/shard_map/ppermute | solution.py:1748
  22.0 10.1 %collective-permute-start.28 = (bf16[640,128]{1,0:T(8,128)(2,1)S(1)}, bf16[640,128]{1,0:T(8,128)(2,1)S(1)}, u32[]{:S(2)}, u32[]{:S(2)}) collective-permute-start(bf16[640,128]{1,0:T(8,128)(2,1)S(1)} %get-tuple-element.216), channel_id=1, source_target_pairs={{0,4},{4,8},{8,12},{12,16},{16,20},{20,24},{24,28},{28,0},{1,5},{5... | collective-permute-start | bytes 491528 | tf_op jit(solution)/shard_map/ppermute | solution.py:1669
  22.1 53.6 %copy-start.35 = (f32[576]{0:T(1024)S(1)}, f32[576]{0:T(1024)}, u32[]{:S(2)}) copy-start(f32[576]{0:T(1024)} %param.21) | copy-start | bytes 6916
  22.1 10.0 %collective-permute-start.29 = (bf16[640,128]{1,0:T(8,128)(2,1)S(1)}, bf16[640,128]{1,0:T(8,128)(2,1)S(1)}, u32[]{:S(2)}, u32[]{:S(2)}) collective-permute-start(bf16[640,128]{1,0:T(8,128)(2,1)S(1)} %get-tuple-element.215), channel_id=1, source_target_pairs={{0,8},{4,12},{8,16},{12,20},{16,24},{20,28},{24,0},{28,4},{1,9},{5... | collective-permute-start | bytes 491528 | tf_op jit(solution)/shard_map/ppermute | solution.py:1669
  24.2 14.0 %collective-permute-start.36 = (bf16[2,256,128]{2,1,0:T(8,128)(2,1)S(1)}, bf16[2,256,128]{2,1,0:T(8,128)(2,1)S(1)}, u32[]{:S(2)}, u32[]{:S(2)}) collective-permute-start(bf16[2,256,128]{2,1,0:T(8,128)(2,1)S(1)} %pad_maximum_fusion.2), channel_id=1, source_target_pairs={{0,8},{4,12},{8,0},{12,4},{16,24},{20,28},{24,16},{28,20},{1,9},{5... | collective-permute-start | bytes 393224 | tf_op jit(solution)/shard_map/ppermute | solution.py:1748
  25.9 18.0 %collective-permute-start.30 = (bf16[640,128]{1,0:T(8,128)(2,1)S(1)}, bf16[640,128]{1,0:T(8,128)(2,1)S(1)}, u32[]{:S(2)}, u32[]{:S(2)}) collective-permute-start(bf16[640,128]{1,0:T(8,128)(2,1)S(1)} %get-tuple-element.214), channel_id=1, source_target_pairs={{0,12},{4,16},{8,20},{12,24},{16,28},{20,0},{24,4},{28,8},{1,13},{... | collective-permute-start | bytes 491528 | tf_op jit(solution)/shard_map/ppermute | solution.py:1669
  28.3 32.0 %collective-permute-start.31 = (bf16[640,128]{1,0:T(8,128)(2,1)S(1)}, bf16[640,128]{1,0:T(8,128)(2,1)S(1)}, u32[]{:S(2)}, u32[]{:S(2)}) collective-permute-start(bf16[640,128]{1,0:T(8,128)(2,1)S(1)} %get-tuple-element.213), channel_id=1, source_target_pairs={{0,16},{4,20},{8,24},{12,28},{16,0},{20,4},{24,8},{28,12},{1,17},{... | collective-permute-start | bytes 491528 | tf_op jit(solution)/shard_map/ppermute | solution.py:1669
  32.1 28.2 %collective-permute-start.32 = (bf16[640,128]{1,0:T(8,128)(2,1)S(1)}, bf16[640,128]{1,0:T(8,128)(2,1)S(1)}, u32[]{:S(2)}, u32[]{:S(2)}) collective-permute-start(bf16[640,128]{1,0:T(8,128)(2,1)S(1)} %get-tuple-element.212), channel_id=1, source_target_pairs={{0,20},{4,24},{8,28},{12,0},{16,4},{20,8},{24,12},{28,16},{1,21},{... | collective-permute-start | bytes 491528 | tf_op jit(solution)/shard_map/ppermute | solution.py:1669
  32.1 28.2 %collective-permute-start.33 = (bf16[640,128]{1,0:T(8,128)(2,1)S(1)}, bf16[640,128]{1,0:T(8,128)(2,1)S(1)}, u32[]{:S(2)}, u32[]{:S(2)}) collective-permute-start(bf16[640,128]{1,0:T(8,128)(2,1)S(1)} %get-tuple-element.211), channel_id=1, source_target_pairs={{0,24},{4,28},{8,0},{12,4},{16,8},{20,12},{24,16},{28,20},{1,25},{... | collective-permute-start | bytes 491528 | tf_op jit(solution)/shard_map/ppermute | solution.py:1669
  38.3 22.0 %collective-permute-start.34 = (bf16[640,128]{1,0:T(8,128)(2,1)S(1)}, bf16[640,128]{1,0:T(8,128)(2,1)S(1)}, u32[]{:S(2)}, u32[]{:S(2)}) collective-permute-start(bf16[640,128]{1,0:T(8,128)(2,1)S(1)} %get-tuple-element.210), channel_id=1, source_target_pairs={{0,28},{4,0},{8,4},{12,8},{16,12},{20,16},{24,20},{28,24},{1,29},{... | collective-permute-start | bytes 491528 | tf_op jit(solution)/shard_map/ppermute | solution.py:1669
  43.9 39.5 %collective-permute-start.44 = (bf16[4,256,128]{2,1,0:T(8,128)(2,1)S(1)}, bf16[4,256,128]{2,1,0:T(8,128)(2,1)S(1)}, u32[]{:S(2)}, u32[]{:S(2)}) collective-permute-start(bf16[4,256,128]{2,1,0:T(8,128)(2,1)S(1)} %get-tuple-element.227.refs_8_), channel_id=1, source_target_pairs={{0,24},{4,28},{8,16},{12,20},{16,8},{20,12},{24,0},{28,4},{1,25},{... | collective-permute-start | bytes 786440 | tf_op jit(solution)/shard_map/ppermute | solution.py:1748
  74.1 8.4 %collective-permute-start.37 = (bf16[384,128]{1,0:T(8,128)(2,1)S(1)}, bf16[384,128]{1,0:T(8,128)(2,1)S(1)}, u32[]{:S(2)}, u32[]{:S(2)}) collective-permute-start(bf16[384,128]{1,0:T(8,128)(2,1)S(1)} %get-tuple-element.224), channel_id=1, source_target_pairs={{0,4},{4,8},{8,12},{12,16},{16,20},{20,24},{24,28},{28,0},{1,5},{5... | collective-permute-start | bytes 294920 | tf_op jit(solution)/shard_map/ppermute | solution.py:1669
  74.2 9.0 %collective-permute-start.38 = (bf16[384,128]{1,0:T(8,128)(2,1)S(1)}, bf16[384,128]{1,0:T(8,128)(2,1)S(1)}, u32[]{:S(2)}, u32[]{:S(2)}) collective-permute-start(bf16[384,128]{1,0:T(8,128)(2,1)S(1)} %get-tuple-element.223), channel_id=1, source_target_pairs={{0,8},{4,12},{8,16},{12,20},{16,24},{20,28},{24,0},{28,4},{1,9},{5... | collective-permute-start | bytes 294920 | tf_op jit(solution)/shard_map/ppermute | solution.py:1669
  76.3 19.5 %collective-permute-start.39 = (bf16[384,128]{1,0:T(8,128)(2,1)S(1)}, bf16[384,128]{1,0:T(8,128)(2,1)S(1)}, u32[]{:S(2)}, u32[]{:S(2)}) collective-permute-start(bf16[384,128]{1,0:T(8,128)(2,1)S(1)} %get-tuple-element.222), channel_id=1, source_target_pairs={{0,12},{4,16},{8,20},{12,24},{16,28},{20,0},{24,4},{28,8},{1,13},{... | collective-permute-start | bytes 294920 | tf_op jit(solution)/shard_map/ppermute | solution.py:1669
  76.8 19.1 %collective-permute-start.40 = (bf16[384,128]{1,0:T(8,128)(2,1)S(1)}, bf16[384,128]{1,0:T(8,128)(2,1)S(1)}, u32[]{:S(2)}, u32[]{:S(2)}) collective-permute-start(bf16[384,128]{1,0:T(8,128)(2,1)S(1)} %get-tuple-element.221), channel_id=1, source_target_pairs={{0,16},{4,20},{8,24},{12,28},{16,0},{20,4},{24,8},{28,12},{1,17},{... | collective-permute-start | bytes 294920 | tf_op jit(solution)/shard_map/ppermute | solution.py:1669
  82.6 13.3 %collective-permute-start.41 = (bf16[384,128]{1,0:T(8,128)(2,1)S(1)}, bf16[384,128]{1,0:T(8,128)(2,1)S(1)}, u32[]{:S(2)}, u32[]{:S(2)}) collective-permute-start(bf16[384,128]{1,0:T(8,128)(2,1)S(1)} %get-tuple-element.220), channel_id=1, source_target_pairs={{0,20},{4,24},{8,28},{12,0},{16,4},{20,8},{24,12},{28,16},{1,21},{... | collective-permute-start | bytes 294920 | tf_op jit(solution)/shard_map/ppermute | solution.py:1669
  83.2 12.7 %collective-permute-start.42 = (bf16[384,128]{1,0:T(8,128)(2,1)S(1)}, bf16[384,128]{1,0:T(8,128)(2,1)S(1)}, u32[]{:S(2)}, u32[]{:S(2)}) collective-permute-start(bf16[384,128]{1,0:T(8,128)(2,1)S(1)} %get-tuple-element.219), channel_id=1, source_target_pairs={{0,24},{4,28},{8,0},{12,4},{16,8},{20,12},{24,16},{28,20},{1,25},{... | collective-permute-start | bytes 294920 | tf_op jit(solution)/shard_map/ppermute | solution.py:1669
  83.4 12.5 %collective-permute-start.43 = (bf16[384,128]{1,0:T(8,128)(2,1)S(1)}, bf16[384,128]{1,0:T(8,128)(2,1)S(1)}, u32[]{:S(2)}, u32[]{:S(2)}) collective-permute-start(bf16[384,128]{1,0:T(8,128)(2,1)S(1)} %get-tuple-element.218), channel_id=1, source_target_pairs={{0,28},{4,0},{8,4},{12,8},{16,12},{20,16},{24,20},{28,24},{1,29},{... | collective-permute-start | bytes 294920 | tf_op jit(solution)/shard_map/ppermute | solution.py:1669
  133.8 10.7 %collective-permute-start = (bf16[384,128]{1,0:T(8,128)(2,1)S(1)}, bf16[384,128]{1,0:T(8,128)(2,1)S(1)}, u32[]{:S(2)}, u32[]{:S(2)}) collective-permute-start(bf16[384,128]{1,0:T(8,128)(2,1)S(1)} %get-tuple-element.205), channel_id=1, source_target_pairs={{0,4},{4,8},{8,12},{12,16},{16,20},{20,24},{24,28},{28,0},{1,5},{5... | collective-permute-start | bytes 294920 | tf_op jit(solution)/shard_map/cond/branch_1_fun/ppermute | solution.py:1669
  133.8 10.7 %collective-permute-start.1 = (bf16[384,128]{1,0:T(8,128)(2,1)S(1)}, bf16[384,128]{1,0:T(8,128)(2,1)S(1)}, u32[]{:S(2)}, u32[]{:S(2)}) collective-permute-start(bf16[384,128]{1,0:T(8,128)(2,1)S(1)} %get-tuple-element.204), channel_id=1, source_target_pairs={{0,8},{4,12},{8,16},{12,20},{16,24},{20,28},{24,0},{28,4},{1,9},{5... | collective-permute-start | bytes 294920 | tf_op jit(solution)/shard_map/cond/branch_1_fun/ppermute | solution.py:1669
  134.8 21.8 %collective-permute-start.2 = (bf16[384,128]{1,0:T(8,128)(2,1)S(1)}, bf16[384,128]{1,0:T(8,128)(2,1)S(1)}, u32[]{:S(2)}, u32[]{:S(2)}) collective-permute-start(bf16[384,128]{1,0:T(8,128)(2,1)S(1)} %get-tuple-element.203), channel_id=1, source_target_pairs={{0,12},{4,16},{8,20},{12,24},{16,28},{20,0},{24,4},{28,8},{1,13},{... | collective-permute-start | bytes 294920 | tf_op jit(solution)/shard_map/cond/branch_1_fun/ppermute | solution.py:1669
  135.9 20.8 %collective-permute-start.3 = (bf16[384,128]{1,0:T(8,128)(2,1)S(1)}, bf16[384,128]{1,0:T(8,128)(2,1)S(1)}, u32[]{:S(2)}, u32[]{:S(2)}) collective-permute-start(bf16[384,128]{1,0:T(8,128)(2,1)S(1)} %get-tuple-element.202), channel_id=1, source_target_pairs={{0,16},{4,20},{8,24},{12,28},{16,0},{20,4},{24,8},{28,12},{1,17},{... | collective-permute-start | bytes 294920 | tf_op jit(solution)/shard_map/cond/branch_1_fun/ppermute | solution.py:1669
  139.1 17.6 %collective-permute-start.4 = (bf16[384,128]{1,0:T(8,128)(2,1)S(1)}, bf16[384,128]{1,0:T(8,128)(2,1)S(1)}, u32[]{:S(2)}, u32[]{:S(2)}) collective-permute-start(bf16[384,128]{1,0:T(8,128)(2,1)S(1)} %get-tuple-element.201), channel_id=1, source_target_pairs={{0,20},{4,24},{8,28},{12,0},{16,4},{20,8},{24,12},{28,16},{1,21},{... | collective-permute-start | bytes 294920 | tf_op jit(solution)/shard_map/cond/branch_1_fun/ppermute | solution.py:1669
  144.4 12.3 %collective-permute-start.5 = (bf16[384,128]{1,0:T(8,128)(2,1)S(1)}, bf16[384,128]{1,0:T(8,128)(2,1)S(1)}, u32[]{:S(2)}, u32[]{:S(2)}) collective-permute-start(bf16[384,128]{1,0:T(8,128)(2,1)S(1)} %get-tuple-element.200), channel_id=1, source_target_pairs={{0,24},{4,28},{8,0},{12,4},{16,8},{20,12},{24,16},{28,20},{1,25},{... | collective-permute-start | bytes 294920 | tf_op jit(solution)/shard_map/cond/branch_1_fun/ppermute | solution.py:1669
  144.5 12.7 %collective-permute-start.6 = (bf16[384,128]{1,0:T(8,128)(2,1)S(1)}, bf16[384,128]{1,0:T(8,128)(2,1)S(1)}, u32[]{:S(2)}, u32[]{:S(2)}) collective-permute-start(bf16[384,128]{1,0:T(8,128)(2,1)S(1)} %get-tuple-element.199), channel_id=1, source_target_pairs={{0,28},{4,0},{8,4},{12,8},{16,12},{20,16},{24,20},{28,24},{1,29},{... | collective-permute-start | bytes 294920 | tf_op jit(solution)/shard_map/cond/branch_1_fun/ppermute | solution.py:1669
  185.0 14.4 %collective-permute-start.7 = (bf16[896,128]{1,0:T(8,128)(2,1)S(1)}, bf16[896,128]{1,0:T(8,128)(2,1)S(1)}, u32[]{:S(2)}, u32[]{:S(2)}) collective-permute-start(bf16[896,128]{1,0:T(8,128)(2,1)S(1)} %get-tuple-element.194), channel_id=1, source_target_pairs={{0,4},{4,8},{8,12},{12,16},{16,20},{20,24},{24,28},{28,0},{1,5},{5... | collective-permute-start | bytes 688136 | tf_op jit(solution)/shard_map/cond/branch_1_fun/ppermute | solution.py:1669
  185.8 14.7 %collective-permute-start.8 = (bf16[896,128]{1,0:T(8,128)(2,1)S(1)}, bf16[896,128]{1,0:T(8,128)(2,1)S(1)}, u32[]{:S(2)}, u32[]{:S(2)}) collective-permute-start(bf16[896,128]{1,0:T(8,128)(2,1)S(1)} %get-tuple-element.193), channel_id=1, source_target_pairs={{0,8},{4,12},{8,16},{12,20},{16,24},{20,28},{24,0},{28,4},{1,9},{5... | collective-permute-start | bytes 688136 | tf_op jit(solution)/shard_map/cond/branch_1_fun/ppermute | solution.py:1669
  193.1 26.1 %collective-permute-start.9 = (bf16[896,128]{1,0:T(8,128)(2,1)}, bf16[896,128]{1,0:T(8,128)(2,1)}, u32[]{:S(2)}, u32[]{:S(2)}) collective-permute-start(bf16[896,128]{1,0:T(8,128)(2,1)} %get-tuple-element.192), channel_id=1, source_target_pairs={{0,12},{4,16},{8,20},{12,24},{16,28},{20,0},{24,4},{28,8},{1,13},{... | collective-permute-start | bytes 688136 | tf_op jit(solution)/shard_map/cond/branch_1_fun/ppermute | solution.py:1669
  193.1 27.0 %collective-permute-start.10 = (bf16[896,128]{1,0:T(8,128)(2,1)}, bf16[896,128]{1,0:T(8,128)(2,1)}, u32[]{:S(2)}, u32[]{:S(2)}) collective-permute-start(bf16[896,128]{1,0:T(8,128)(2,1)} %get-tuple-element.191), channel_id=1, source_target_pairs={{0,16},{4,20},{8,24},{12,28},{16,0},{20,4},{24,8},{28,12},{1,17},{... | collective-permute-start | bytes 688136 | tf_op jit(solution)/shard_map/cond/branch_1_fun/ppermute | solution.py:1669
  194.3 25.9 %collective-permute-start.11 = (bf16[896,128]{1,0:T(8,128)(2,1)}, bf16[896,128]{1,0:T(8,128)(2,1)}, u32[]{:S(2)}, u32[]{:S(2)}) collective-permute-start(bf16[896,128]{1,0:T(8,128)(2,1)} %get-tuple-element.190), channel_id=1, source_target_pairs={{0,20},{4,24},{8,28},{12,0},{16,4},{20,8},{24,12},{28,16},{1,21},{... | collective-permute-start | bytes 688136 | tf_op jit(solution)/shard_map/cond/branch_1_fun/ppermute | solution.py:1669
  199.4 21.3 %collective-permute-start.12 = (bf16[896,128]{1,0:T(8,128)(2,1)}, bf16[896,128]{1,0:T(8,128)(2,1)}, u32[]{:S(2)}, u32[]{:S(2)}) collective-permute-start(bf16[896,128]{1,0:T(8,128)(2,1)} %get-tuple-element.189), channel_id=1, source_target_pairs={{0,24},{4,28},{8,0},{12,4},{16,8},{20,12},{24,16},{28,20},{1,25},{... | collective-permute-start | bytes 688136 | tf_op jit(solution)/shard_map/cond/branch_1_fun/ppermute | solution.py:1669
  201.2 21.9 %collective-permute-start.13 = (bf16[896,128]{1,0:T(8,128)(2,1)}, bf16[896,128]{1,0:T(8,128)(2,1)}, u32[]{:S(2)}, u32[]{:S(2)}) collective-permute-start(bf16[896,128]{1,0:T(8,128)(2,1)} %get-tuple-element.188), channel_id=1, source_target_pairs={{0,28},{4,0},{8,4},{12,8},{16,12},{20,16},{24,20},{28,24},{1,29},{... | collective-permute-start | bytes 688136 | tf_op jit(solution)/shard_map/cond/branch_1_fun/ppermute | solution.py:1669
  235.6 2.7 collective-permute-start.14
  239.9 11.4 %collective-permute-start.17 = (bf16[1024,128]{1,0:T(8,128)(2,1)S(1)}, bf16[1024,128]{1,0:T(8,128)(2,1)S(1)}, u32[]{:S(2)}, u32[]{:S(2)}) collective-permute-start(bf16[1024,128]{1,0:T(8,128)(2,1)S(1)} %get-tuple-element.197), channel_id=1, source_target_pairs={{0,6},{1,7},{2,4},{3,5},{4,2},{5,3},{6,0},{7,1},{8,14},{9,15},{10,... | collective-permute-start | bytes 786440 | tf_op jit(solution)/shard_map/cond/branch_1_fun/ppermute | solution.py:784
  244.2 15.2 %collective-permute-start.16 = (bf16[1024,128]{1,0:T(8,128)(2,1)S(1)}, bf16[1024,128]{1,0:T(8,128)(2,1)S(1)}, u32[]{:S(2)}, u32[]{:S(2)}) collective-permute-start(bf16[1024,128]{1,0:T(8,128)(2,1)S(1)} %get-tuple-element.198), channel_id=1, source_target_pairs={{0,4},{1,5},{2,6},{3,7},{4,0},{5,1},{6,2},{7,3},{8,12},{9,13},{10,... | collective-permute-start | bytes 786440 | tf_op jit(solution)/shard_map/cond/branch_1_fun/ppermute | solution.py:784
  244.2 15.4 %collective-permute-start.15 = (bf16[1024,128]{1,0:T(8,128)(2,1)S(1)}, bf16[1024,128]{1,0:T(8,128)(2,1)S(1)}, u32[]{:S(2)}, u32[]{:S(2)}) collective-permute-start(bf16[1024,128]{1,0:T(8,128)(2,1)S(1)} %get-tuple-element.196), channel_id=1, source_target_pairs={{0,2},{1,3},{2,0},{3,1},{4,6},{5,7},{6,4},{7,5},{8,10},{9,11},{10,... | collective-permute-start | bytes 786440 | tf_op jit(solution)/shard_map/cond/branch_1_fun/ppermute | solution.py:784
  259.8 14.9 %collective-permute-start.20 = (bf16[256,128]{1,0:T(8,128)(2,1)S(1)}, bf16[256,128]{1,0:T(8,128)(2,1)S(1)}, u32[]{:S(2)}, u32[]{:S(2)}) collective-permute-start(bf16[256,128]{1,0:T(8,128)(2,1)S(1)} %get-tuple-element.208), channel_id=1, source_target_pairs={{0,16},{1,17},{2,18},{3,19},{4,20},{5,21},{6,22},{7,23},{8,24},{9,... | collective-permute-start | bytes 196616 | tf_op jit(solution)/shard_map/cond/branch_1_fun/ppermute | solution.py:784
  270.8 6.3 %collective-permute-start.19 = (bf16[256,128]{1,0:T(8,128)(2,1)S(1)}, bf16[256,128]{1,0:T(8,128)(2,1)S(1)}, u32[]{:S(2)}, u32[]{:S(2)}) collective-permute-start(bf16[256,128]{1,0:T(8,128)(2,1)S(1)} %get-tuple-element.209), channel_id=1, source_target_pairs={{0,24},{1,25},{2,26},{3,27},{4,28},{5,29},{6,30},{7,31},{8,16},{9,... | collective-permute-start | bytes 196616 | tf_op jit(solution)/shard_map/cond/branch_1_fun/ppermute | solution.py:784
  272.1 5.0 %collective-permute-start.18 = (bf16[256,128]{1,0:T(8,128)(2,1)S(1)}, bf16[256,128]{1,0:T(8,128)(2,1)S(1)}, u32[]{:S(2)}, u32[]{:S(2)}) collective-permute-start(bf16[256,128]{1,0:T(8,128)(2,1)S(1)} %get-tuple-element.207), channel_id=1, source_target_pairs={{0,8},{1,9},{2,10},{3,11},{4,12},{5,13},{6,14},{7,15},{8,0},{9,1},... | collective-permute-start | bytes 196616 | tf_op jit(solution)/shard_map/cond/branch_1_fun/ppermute | solution.py:784
  277.2 7.9 %collective-permute-start.23 = (bf16[256,128]{1,0:T(8,128)(2,1)S(1)}, bf16[256,128]{1,0:T(8,128)(2,1)S(1)}, u32[]{:S(2)}, u32[]{:S(2)}) collective-permute-start(bf16[256,128]{1,0:T(8,128)(2,1)S(1)} %fusion.8), channel_id=1, source_target_pairs={{0,16},{1,17},{2,18},{3,19},{4,20},{5,21},{6,22},{7,23},{8,24},{9,... | collective-permute-start | bytes 196616 | tf_op jit(solution)/shard_map/cond/branch_1_fun/ppermute | solution.py:784
  279.9 7.8 %collective-permute-start.22 = (bf16[256,128]{1,0:T(8,128)(2,1)S(1)}, bf16[256,128]{1,0:T(8,128)(2,1)S(1)}, u32[]{:S(2)}, u32[]{:S(2)}) collective-permute-start(bf16[256,128]{1,0:T(8,128)(2,1)S(1)} %fusion.8), channel_id=1, source_target_pairs={{0,24},{1,25},{2,26},{3,27},{4,28},{5,29},{6,30},{7,31},{8,16},{9,... | collective-permute-start | bytes 196616 | tf_op jit(solution)/shard_map/cond/branch_1_fun/ppermute | solution.py:784
  280.4 8.0 %collective-permute-start.21 = (bf16[256,128]{1,0:T(8,128)(2,1)S(1)}, bf16[256,128]{1,0:T(8,128)(2,1)S(1)}, u32[]{:S(2)}, u32[]{:S(2)}) collective-permute-start(bf16[256,128]{1,0:T(8,128)(2,1)S(1)} %fusion.8), channel_id=1, source_target_pairs={{0,8},{1,9},{2,10},{3,11},{4,12},{5,13},{6,14},{7,15},{8,0},{9,1},... | collective-permute-start | bytes 196616 | tf_op jit(solution)/shard_map/cond/branch_1_fun/ppermute | solution.py:784
  288.6 13.2 %collective-permute-start.26 = (bf16[4,256,128]{2,1,0:T(8,128)(2,1)S(1)}, bf16[4,256,128]{2,1,0:T(8,128)(2,1)S(1)}, u32[]{:S(2)}, u32[]{:S(2)}) collective-permute-start(bf16[4,256,128]{2,1,0:T(8,128)(2,1)S(1)} %bitcast.138), channel_id=1, source_target_pairs={{0,6},{1,7},{2,4},{3,5},{4,2},{5,3},{6,0},{7,1},{8,14},{9,15},{10,... | collective-permute-start | bytes 786440 | tf_op jit(solution)/shard_map/cond/branch_1_fun/ppermute | solution.py:784
  290.3 15.8 %collective-permute-start.25 = (bf16[4,256,128]{2,1,0:T(8,128)(2,1)S(1)}, bf16[4,256,128]{2,1,0:T(8,128)(2,1)S(1)}, u32[]{:S(2)}, u32[]{:S(2)}) collective-permute-start(bf16[4,256,128]{2,1,0:T(8,128)(2,1)S(1)} %bitcast.139), channel_id=1, source_target_pairs={{0,4},{1,5},{2,6},{3,7},{4,0},{5,1},{6,2},{7,3},{8,12},{9,13},{10,... | collective-permute-start | bytes 786440 | tf_op jit(solution)/shard_map/cond/branch_1_fun/ppermute | solution.py:784
  290.4 16.0 %collective-permute-start.24 = (bf16[4,256,128]{2,1,0:T(8,128)(2,1)S(1)}, bf16[4,256,128]{2,1,0:T(8,128)(2,1)S(1)}, u32[]{:S(2)}, u32[]{:S(2)}) collective-permute-start(bf16[4,256,128]{2,1,0:T(8,128)(2,1)S(1)} %bitcast.140), channel_id=1, source_target_pairs={{0,2},{1,3},{2,0},{3,1},{4,6},{5,7},{6,4},{7,5},{8,10},{9,11},{10,... | collective-permute-start | bytes 786440 | tf_op jit(solution)/shard_map/cond/branch_1_fun/ppermute | solution.py:784
  308.0 3.0 collective-permute-start.27
  (35 other events, 297.6 us)
Sparse Core Ops, SparseCore 0:
  117.3 195.8 all-reduce.1
where the time goes:
time: 335 us; the launch traced here: 331 us
  Pallas kernels  117 us (35%)
  starting transfers between devices  103 us (31%)
  waiting for transfers between devices  73 us (22%)
  between operations  15.6 us (5%)
  local copies, waits for them, and re-layouts  15.5 us (5%)
  other arithmetic  6.8 us (2%)
    ppermute x28, starting transfers between devices, to_all(): lax.ppermute(messages[t], 'seq', [(i, (i + t) % count) for i in range(cou...  56.7 us
    ppermute x14, waiting for transfers between devices, swap_with(): lax.ppermute(value, ('seq', 'batch'), [(i, i ^ mask) for i in range(devic...  47 us
    ppermute x14, starting transfers between devices, swap_with(): lax.ppermute(value, ('seq', 'batch'), [(i, i ^ mask) for i in range(devic...  24.8 us
    pallas_call x1, Pallas kernels, units_backward_call(): pl.pallas_call(functools.partial(units_backward_kernel, count), in_specs=...  24.5 us
    ppermute x28, waiting for transfers between devices, to_all(): lax.ppermute(messages[t], 'seq', [(i, (i + t) % count) for i in range(cou...  21.4 us
    ppermute x3, starting transfers between devices, units_layer(): lax.ppermute(part, 'seq', [(i, i ^ mask) for i in range(count)])  21 us
    pallas_call x1, Pallas kernels, units_ffn_call(): pl.pallas_call(functools.partial(units_ffn_kernel, count), in_specs=[pl.B...  20.5 us
    pallas_call x1, Pallas kernels, units_forward_call(): pl.pallas_call(functools.partial(units_forward_kernel, count), in_specs=[...  13 us
  transfers between devices with their start and end apart: 46, of which 26 were waited for; matrix products, arithmetic and copies ran while one was open for 5% of the time, Pallas kernels for 25%

commit v1 on v0

--- a/solution.py
+++ b/solution.py
@@ -33,6 +33,10 @@
     return pltpu.CompilerParams(vmem_limit_bytes=mib * 1024 * 1024)
 
 
+def as_row(ref):
+    return ref[...].reshape(1, ref.shape[0])
+
+
 def full_spec(shape):
     zeros = (0,) * len(shape)
     return pl.BlockSpec(shape, lambda *_: zeros)
@@ -63,7 +67,7 @@
     x = x_ref[0].T.astype(f32)
     rows, width = x.shape
     scale = lax.rsqrt(jnp.sum(x * x, axis=-1, keepdims=True) * (1.0 / width) + eps_norm)
-    a = (x * scale * norm_ref[...]).astype(bf16)
+    a = (x * scale * as_row(norm_ref)).astype(bf16)
     a_ref[0] = a
     cos, sin = cos_ref[0], sin_ref[0]
     low_half = lane_index(rows) < HEAD_DIM
@@ -99,7 +103,7 @@
         grid=(seqs,),
         in_specs=[
             row((width, rows)),
-            full_spec((1, width)),
+            full_spec((width,)),
             full_spec(w_query.shape),
             full_spec(w_key.shape),
             full_spec(w_value.shape),
@@ -421,7 +425,7 @@
     mid = x + dot(attn, w_out_ref[...])
     scale = lax.rsqrt(jnp.sum(mid * mid, axis=-1, keepdims=True) * (1.0 / width) + eps_norm)
     normed = mid * scale
-    b = (normed * norm_ref[...]).astype(bf16)
+    b = (normed * as_row(norm_ref)).astype(bf16)
     b_ref[0] = b
     gate = dot(b, w_gate_ref[...])
     up = dot(b, w_up_ref[...])
@@ -446,7 +450,7 @@
     def _():
         g_norm_ref[...] += g_norm
 
-    e = d_b * norm_ref[...]
+    e = d_b * as_row(norm_ref)
     mean = jnp.sum(e * normed, axis=-1, keepdims=True) * (1.0 / width)
     d_mid = cot.astype(f32) + scale * (e - normed * mean)
     d_mid_ref[0] = d_mid
@@ -497,7 +501,7 @@
         in_specs=[row(width, rows), row(width, rows), row(rows, width)]
         + [
             full_spec(w_out.shape),
-            full_spec((1, width)),
+            full_spec((width,)),
             full_spec(w_gate.shape),
             full_spec(w_up.shape),
             full_spec(w_down.shape),
@@ -596,7 +600,7 @@
             out_ref[:, t * LANES : (t + 1) * LANES] = product
         else:
             out_ref[:, t * LANES :] = product[:, :HEAD_DIM]
-            norm_ref[...] = product.T[HEAD_DIM : HEAD_DIM + 1, :]
+            norm_ref[...] = product.T[HEAD_DIM, :]
 
 
 def unfold_call(kernel, name, arrays, shapes):
@@ -676,7 +680,7 @@
         d_norm[...] += g_norm
         d_pairs[...] += g_pairs
 
-    e = d_a * norm_ref[...]
+    e = d_a * as_row(norm_ref)
     mean = jnp.sum(e * normed, axis=-1, keepdims=True) * (1.0 / width)
     out_ref[0] = (d_mid_ref[0] + scale * (e - normed * mean)).astype(bf16).T
 
@@ -713,7 +717,7 @@
         in_specs=[
             row(width, rows),
             row(rows, width),
-            full_spec((1, width)),
+            full_spec((width,)),
             full_spec(w_key.shape),
             full_spec(w_value.shape),
             row(rows, LANES),
@@ -972,74 +976,63 @@
 
 
 def units_pre_kernel(
-    ids, x_ref, norm_ref, wq_ref, wk_ref, wv_ref, cos_ref, sin_ref, a_ref, out_ref, q_ref, kv_ref
+    count, ids, x_ref, norm_ref, wq_ref, wk_ref, wv_ref, cos_ref, sin_ref, *refs
 ):
-    step = pl.program_id(0)
-    count = out_ref.shape[0]
+    outs, (a_ref, q_ref, kv_ref, out_ref) = refs[:count], refs[count:]
     me = ids[0]
-    x = x_ref[0].T.astype(f32)
-    rows, width = x.shape
-    scale = lax.rsqrt(jnp.sum(x * x, axis=-1, keepdims=True) * (1.0 / width) + eps_norm)
-    a = (x * scale * norm_ref[...]).astype(bf16)
-    a_ref[0] = a
-    cos, sin = cos_ref[0], sin_ref[0]
-
-    def turn(tile):
-        return tile * cos + swap_halves(tile) * sin
+    seqs, width, rows = x_ref.shape
 
     def heads_of(tiles, many):
         return [tiles[h // 2] if h % 2 == 0 else other_half(tiles[h // 2]) for h in range(many)]
 
-    queries = heads_of([turn(t) * 0.125 for t in head_tiles(dot(a, wq_ref[...]))], HEADS)
-    keys = heads_of([turn(t) for t in head_tiles(dot(a, wk_ref[...], NT))], KV_HEADS)
-    values = heads_of(head_tiles(dot(a, wv_ref[...], NT)), KV_HEADS)
-    for g in range(KV_HEADS):
-        parts = queries[g * PER : (g + 1) * PER] + [keys[g], values[g]]
-        unit = step * KV_HEADS + g
-
-        @pl.when(unit < count)
-        def _(parts=parts, unit=unit):
-            write_long(out_ref, lax.rem(unit - me + count, count), parts)
-
-        @pl.when(unit == count)
-        def _(parts=parts):
-            for h in range(PER):
-                q_ref[h * rows : (h + 1) * rows] = low_only(parts[h]).astype(bf16)
-            kv_ref[0] = join(parts[3], other_half(parts[4])).astype(bf16)
+    for s in range(seqs):
+        x = x_ref[s].T.astype(f32)
+        scale = lax.rsqrt(jnp.sum(x * x, axis=-1, keepdims=True) * (1.0 / width) + eps_norm)
+        a = (x * scale * as_row(norm_ref)).astype(bf16)
+        a_ref[s] = a
+        cos, sin = cos_ref[s], sin_ref[s]
+
+        def turn(tile, cos=cos, sin=sin):
+            return tile * cos + swap_halves(tile) * sin
+
+        queries = heads_of([turn(t) * 0.125 for t in head_tiles(dot(a, wq_ref[...]))], HEADS)
+        keys = heads_of([turn(t) for t in head_tiles(dot(a, wk_ref[...], NT))], KV_HEADS)
+        values = heads_of(head_tiles(dot(a, wv_ref[...], NT)), KV_HEADS)
+        for g in range(KV_HEADS):
+            parts = queries[g * PER : (g + 1) * PER] + [keys[g], values[g]]
+            unit = s * KV_HEADS + g
+            if unit < count:
+                write_long(out_ref, lax.rem(unit - me + count, count), parts)
+            else:
+                for h in range(PER):
+                    q_ref[h * rows : (h + 1) * rows] = low_only(parts[h]).astype(bf16)
+                kv_ref[0] = join(parts[3], other_half(parts[4])).astype(bf16)
+    hand_out(out_ref, outs)
+
+
+def hand_out(messages, outs):
+    for t, out in enumerate(outs):
+        out[...] = messages[t]
 
 
 def units_pre_call(ids, x, norm, w_query, w_key, w_value, cos, sin, count):
     seqs, width, rows = x.shape
-    row = lambda shape: pl.BlockSpec((1,) + shape, lambda s, *_: (s,) + (0,) * len(shape))
-    long_shape = (count, rows * 5 // 2, LANES)
-    q_shape = (PER * rows, LANES)
-    kv_shape = (1, rows, LANES)
-    return pl.pallas_call(
-        units_pre_kernel,
-        grid_spec=pltpu.PrefetchScalarGridSpec(
-            num_scalar_prefetch=1,
-            grid=(seqs,),
-            in_specs=[
-                row((width, rows)),
-                full_spec((1, width)),
-                full_spec(w_query.shape),
-                full_spec(w_key.shape),
-                full_spec(w_value.shape),
-                row((rows, LANES)),
-                row((rows, LANES)),
-            ],
-            out_specs=[row((rows, width))]
-            + [full_spec(shape) for shape in (long_shape, q_shape, kv_shape)],
-        ),
-        out_shape=[
+    vmem = pl.BlockSpec(memory_space=pltpu.VMEM)
+    message = (rows * 5 // 2, LANES)
+    outs = pl.pallas_call(
+        functools.partial(units_pre_kernel, count),
+        in_specs=[pl.BlockSpec(memory_space=pltpu.SMEM)] + [vmem] * 7,
+        out_shape=[jax.ShapeDtypeStruct(message, bf16)] * count
+        + [
             jax.ShapeDtypeStruct((seqs, rows, width), bf16),
-            jax.ShapeDtypeStruct(long_shape, bf16),
-            jax.ShapeDtypeStruct(q_shape, bf16),
-            jax.ShapeDtypeStruct(kv_shape, bf16),
+            jax.ShapeDtypeStruct((PER * rows, LANES), bf16),
+            jax.ShapeDtypeStruct((1, rows, LANES), bf16),
         ],
+        scratch_shapes=[pltpu.VMEM((count,) + message, bf16)],
         compiler_params=params(60),
         name="project",
     )(ids, x, norm, w_query, w_key, w_value, cos, sin)
+    return (outs[:count],) + tuple(outs[count:])
 
 
 def attend_row(q, blocks, seen=None):
@@ -1078,7 +1071,7 @@
 
 def units_forward_kernel(count, ids, *refs):
     messages = refs[:count]
-    out_ref, log_ref, q_ref, kv_ref = refs[-4:]
+    outs, (log_ref, q_ref, kv_ref, out_ref) = refs[-4 - count : -4], refs[-4:]
     rows = kv_ref.shape[1]
     me = ids[0]
     for t in range(count):
@@ -1092,6 +1085,7 @@
         heads, log_total = attend_result(new_peak, sums)
         log_ref[i] = log_total
         write_short(out_ref, lax.rem(i - me + count, count), heads)
+    hand_out(out_ref, outs)
 
 
 def units_forward_call(ids, messages, after):
@@ -1099,20 +1093,23 @@
     rows = messages[0].shape[0] * 2 // 5
     wide = PER * rows
     vmem = pl.BlockSpec(memory_space=pltpu.VMEM)
-    return pl.pallas_call(
+    message = (rows * 3 // 2, LANES)
+    outs = pl.pallas_call(
         functools.partial(units_forward_kernel, count),
         in_specs=[pl.BlockSpec(memory_space=pltpu.SMEM)]
         + [vmem] * count
         + [pl.BlockSpec(memory_space=pl.ANY)] * len(after),
-        out_shape=[
-            jax.ShapeDtypeStruct((count, rows * 3 // 2, LANES), bf16),
+        out_shape=[jax.ShapeDtypeStruct(message, bf16)] * count
+        + [
             jax.ShapeDtypeStruct((count, 1, wide), f32),
             jax.ShapeDtypeStruct((count, wide, LANES), bf16),
             jax.ShapeDtypeStruct((count, rows, LANES), bf16),
         ],
+        scratch_shapes=[pltpu.VMEM((count,) + message, bf16)],
         compiler_params=params(48),
         name="units_forward",
     )(ids, *messages, *after)
+    return (outs[:count],) + tuple(outs[count:])
 
 
 def last_unit_forward_kernel(ids, q_ref, kv_ref, out_ref, log_ref):
@@ -1201,12 +1198,14 @@
 
 def units_backward_kernel(count, ids, *refs):
     messages, refs = refs[:count], refs[count:]
-    q_ref, kv_ref, attn_ref, log_ref, last_ref, out_ref, d_out, delta, d_kv = refs
+    attn, refs = refs[:count], refs[count:]
+    q_ref, kv_ref, log_ref, last_ref = refs[:4]
+    outs, (out_ref, d_out, delta, d_kv) = refs[4:-4], refs[-4:]
     rows = kv_ref.shape[1]
     me = ids[0]
     for t in range(count):
         block = lax.rem(me - t + count, count)
-        value, row = unpack_out(messages[t][...], attn_ref[(count - t) % count])
+        value, row = unpack_out(messages[t][...], attn[(count - t) % count][...])
         d_out[block] = value
         delta[block] = row
     for i in reversed(range(count)):
@@ -1234,25 +1233,27 @@
             [d_query[h * rows : (h + 1) * rows] for h in range(PER)] + [tile, other_half(tile)],
             last_ref[i],
         )
+    hand_out(out_ref, outs)
 
 
 def units_backward_call(ids, messages, q, kv, attn, log_total, last_d_kv):
     count, rows, _ = kv.shape
     wide = PER * rows
     vmem = pl.BlockSpec(memory_space=pltpu.VMEM)
+    message = (rows * 7 // 2, LANES)
     return pl.pallas_call(
         functools.partial(units_backward_kernel, count),
-        in_specs=[pl.BlockSpec(memory_space=pltpu.SMEM)]
-        + [vmem] * (count + 5),
-        out_shape=jax.ShapeDtypeStruct((count, rows * 7 // 2, LANES), bf16),
+        in_specs=[pl.BlockSpec(memory_space=pltpu.SMEM)] + [vmem] * (2 * count + 4),
+        out_shape=[jax.ShapeDtypeStruct(message, bf16)] * count,
         scratch_shapes=[
+            pltpu.VMEM((count,) + message, bf16),
             pltpu.VMEM((count, wide, LANES), bf16),
             pltpu.VMEM((count, 1, wide), f32),
             pltpu.VMEM((count, rows, LANES), f32),
         ],
         compiler_params=params(56),
         name="units_backward",
-    )(ids, *messages, q, kv, attn, log_total, last_d_kv)
+    )(ids, *messages, *attn, q, kv, log_total, last_d_kv)
 
 
 def units_ffn_kernel(
@@ -1269,8 +1270,8 @@
 ):
     messages, last_message = refs[:count], refs[count]
     (
-        mid_ref, attn, hid_hbm, d_gate_hbm, d_up_hbm, g_hbm,
-        units, w_gate, w_up, w_down, cot, b, hid, d_gate, d_up, g_buf, w_sems, h_sems, g_sems,
+        mid_hbm, attn_hbm, hid_hbm, d_gate_hbm, d_up_hbm, g_hbm,
+        units, w_gate, w_up, w_down, mid, attn, cot, b, hid, d_gate, d_up, g_buf, w_sems, out_sems,
     ) = refs[count + 1 :]
     me = ids[0]
     seqs, width, rows = x_ref.shape
@@ -1284,6 +1285,13 @@
     ]
     for load in loads:
         load.start()
+    stores = []
+
+    def store(source, target):
+        copy = pltpu.make_async_copy(source, target, out_sems.at[len(stores)])
+        copy.start()
+        stores.append(copy)
+
     for t in range(count):
         units[lax.rem(me - t + count, count)] = messages[t][...]
     units[count] = last_message[0]
@@ -1300,17 +1308,23 @@
         scale = lax.rsqrt(
             jnp.sum(mid_rows * mid_rows, axis=-1, keepdims=True) * (1.0 / width) + eps_norm
         )
-        mid_ref[s] = mid_rows
-        b[here] = (mid_rows * scale * norm_ref[...]).astype(bf16)
+        mid[s] = mid_rows
+        b[here] = (mid_rows * scale * as_row(norm_ref)).astype(bf16)
+    store(mid, mid_hbm)
+    store(attn, attn_hbm)
+    b_turned = b[...].T
+    cot_turned = jnp.concatenate([cot_ref[s] for s in range(seqs)], axis=1)
     for load in loads:
         load.wait()
     chunk = 2 * LANES
-    stores = []
-
-    def store(source, target, sem):
-        copy = pltpu.make_async_copy(source, target, sem)
-        copy.start()
-        stores.append(copy)
+
+    def gradient(k, c, left, right):
+        product = dot(left, right[:, c * chunk : (c + 1) * chunk]).astype(bf16)
+        for u in range(2):
+            half, at = ffn_place(k, 2 * c + u, tiles)
+            here = pl.ds(at * width, width)
+            g_buf[half, here, :] = product[:, u * LANES : (u + 1) * LANES]
+            store(g_buf.at[half, here], g_hbm.at[half, here])
 
     for c in range(hidden // chunk):
         lanes = pl.ds(c * chunk, chunk)
@@ -1322,19 +1336,11 @@
         hid[:, lanes] = (active * up).astype(bf16)
         d_gate[:, lanes] = (d_hid * up * sig * (1.0 + gate * (1.0 - sig))).astype(bf16)
         d_up[:, lanes] = (d_hid * active).astype(bf16)
-    for k, (source, target) in enumerate(((hid, hid_hbm), (d_gate, d_gate_hbm), (d_up, d_up_hbm))):
-        store(source, target, h_sems.at[k])
-    b_turned = b[...].T
-    cot_turned = jnp.concatenate([cot_ref[s] for s in range(seqs)], axis=1)
+    for source, target in ((d_gate, d_gate_hbm), (d_up, d_up_hbm), (hid, hid_hbm)):
+        store(source, target)
     for k, (left, right) in enumerate(((b_turned, d_gate), (b_turned, d_up), (cot_turned, hid))):
         for c in range(hidden // chunk):
-            product = dot(left, right[:, c * chunk : (c + 1) * chunk]).astype(bf16)
-            for u in range(2):
-                t = 2 * c + u
-                half, at = ffn_place(k, t, tiles)
-                here = pl.ds(at * width, width)
-                g_buf[half, here, :] = product[:, u * LANES : (u + 1) * LANES]
-                store(g_buf.at[half, here], g_hbm.at[half, here], g_sems.at[k * tiles + t])
+            gradient(k, c, left, right)
     for copy in stores:
         copy.wait()
 
@@ -1356,7 +1362,7 @@
         + [vmem] * 4
         + [hbm] * 3
         + [vmem] * (count + 1),
-        out_specs=[vmem] * 2 + [hbm] * 4,
+        out_specs=[hbm] * 6,
         out_shape=[
             jax.ShapeDtypeStruct((seqs, rows, width), f32),
             jax.ShapeDtypeStruct((seqs, rows, width), bf16),
@@ -1370,6 +1376,8 @@
             pltpu.VMEM(w_gate.shape, bf16),
             pltpu.VMEM(w_up.shape, bf16),
             pltpu.VMEM(w_down.shape, bf16),
+            pltpu.VMEM((seqs, rows, width), f32),
+            pltpu.VMEM((seqs, rows, width), bf16),
             pltpu.VMEM((tokens, width), bf16),
             pltpu.VMEM((tokens, width), bf16),
             pltpu.VMEM(wide, bf16),
@@ -1377,8 +1385,7 @@
             pltpu.VMEM(wide, bf16),
             pltpu.VMEM(g_shape, bf16),
             pltpu.SemaphoreType.DMA((3,)),
-            pltpu.SemaphoreType.DMA((3,)),
-            pltpu.SemaphoreType.DMA((3 * tiles,)),
+            pltpu.SemaphoreType.DMA((5 + 3 * tiles,)),
         ],
         compiler_params=params(60),
         name="feed_forward",
@@ -1397,10 +1404,11 @@
     w_gate_ref,
     w_up_ref,
     d_mid_ref,
-    d_out_ref,
     d_last_ref,
     g_norm_ref,
+    *refs,
 ):
+    outs, d_out_ref = refs[:count], refs[count]
     step = pl.program_id(0)
     me = ids[0]
     mid = mid_ref[0]
@@ -1410,7 +1418,7 @@
     normed = mid * scale
     d_b = dot(d_gate_ref[...], w_gate_ref[...], NT) + dot(d_up_ref[...], w_up_ref[...], NT)
     norm_term = jnp.sum(d_b * normed, axis=0, keepdims=True)
-    e = d_b * norm_ref[...]
+    e = d_b * as_row(norm_ref)
     mean = jnp.sum(e * normed, axis=-1, keepdims=True) * (1.0 / width)
     d_mid = cot.astype(f32) + scale * (e - normed * mean)
     d_mid_ref[0] = d_mid
@@ -1439,6 +1447,10 @@
     def _():
         g_norm_ref[...] += norm_term
 
+    @pl.when(step == pl.num_programs(0) - 1)
+    def _():
+        hand_out(d_out_ref, outs)
+
 
 def units_back_call(ids, mid, cot, d_gate, d_up, norm, w_out, w_gate, w_up, count):
     seqs, rows, width = mid.shape
@@ -1446,29 +1458,31 @@
     row = lambda *shape: pl.BlockSpec((1,) + shape, lambda s, *_: (s,) + (0,) * len(shape))
     part = pl.BlockSpec((rows, hidden), lambda s, *_: (s, 0))
     short = (rows * 3 // 2, LANES)
-    return pl.pallas_call(
+    outs = pl.pallas_call(
         functools.partial(units_back_kernel, count),
         grid_spec=pltpu.PrefetchScalarGridSpec(
             num_scalar_prefetch=1,
             grid=(seqs,),
-            in_specs=[row(rows, width), row(width, rows), part, part, full_spec((1, width))]
+            in_specs=[row(rows, width), row(width, rows), part, part, full_spec((width,))]
             + [full_spec(w_out.shape), full_spec(w_gate.shape), full_spec(w_up.shape)],
             out_specs=[
                 row(rows, width),
-                full_spec((count,) + short),
                 full_spec((1,) + short),
                 full_spec((1, width)),
-            ],
+            ]
+            + [full_spec(short)] * count,
+            scratch_shapes=[pltpu.VMEM((count,) + short, bf16)],
         ),
         out_shape=[
             jax.ShapeDtypeStruct((seqs, rows, width), f32),
-            jax.ShapeDtypeStruct((count,) + short, bf16),
             jax.ShapeDtypeStruct((1,) + short, bf16),
             jax.ShapeDtypeStruct((1, width), f32),
-        ],
+        ]
+        + [jax.ShapeDtypeStruct(short, bf16)] * count,
         compiler_params=params(60),
         name="feed_back",
     )(ids, mid, cot, d_gate, d_up, norm, w_out, w_gate, w_up)
+    return (outs[3:],) + tuple(outs[:3])
 
 
 def units_out_kernel(
@@ -1527,88 +1541,73 @@
     g_out_ref, *refs,
 ):
     messages = refs[:count]
-    out_ref, g_ref, units, g_query, g_pairs, d_norm = refs[count:]
-    step = pl.program_id(0)
+    out_ref, g_ref, units = refs[count:]
     me = ids[0]
-    x = x_ref[0].T.astype(f32)
-    rows, width = x.shape
-
-    @pl.when(step == 0)
-    def _():
-        for t in range(count):
-            units[lax.rem(me - t + count, count)] = messages[t][: rows * 5 // 2]
-        last_kv = sum(messages[t][rows * 5 // 2 :].astype(f32) for t in range(count))
-        heads = [last_q_ref[h * rows : (h + 1) * rows] for h in range(PER)]
-        write_long(units, count, heads + [last_kv, other_half(last_kv)])
-
-    cos, sin = cos_ref[0], sin_ref[0]
-
-    def turn(tile):
-        return tile * cos - swap_halves(tile) * sin
-
-    heads, keys, values = [], [], []
-    for g in range(KV_HEADS):
-        parts, kv = read_long(units[step * KV_HEADS + g], rows)
-        heads += parts
-        keys.append(kv)
-        values.append(other_half(kv))
-
-    def in_tiles(parts, scale):
-        tiles = [
-            join(parts[h], other_half(parts[h + 1])) for h in range(0, len(parts) - 1, 2)
-        ] + [parts[-1]]
-        return tiles if scale is None else [turn(t) * scale for t in tiles]
+    seqs, width, rows = x_ref.shape
+    for t in range(count):
+        units[lax.rem(me - t + count, count)] = messages[t][: rows * 5 // 2]
+    last_kv = sum(messages[t][rows * 5 // 2 :].astype(f32) for t in range(count))
+    heads = [last_q_ref[h * rows : (h + 1) * rows] for h in range(PER)]
+    write_long(units, count, heads + [last_kv, other_half(last_kv)])
 
     def flat(tiles):
         return jnp.concatenate(tiles[:-1] + [tiles[-1][:, :HEAD_DIM]], axis=1).astype(bf16)
 
-    d_query = flat(in_tiles(heads, 0.125))
-    key_tiles = in_tiles(keys, 1.0)
-    d_key, d_value = flat(key_tiles), flat(in_tiles(values, None))
-    turned = [key_tiles[g // 2] if g % 2 == 0 else other_half(key_tiles[g // 2]) for g in range(KV_HEADS)]
-    pairs = jnp.concatenate(
-        [join(turned[g], other_half(values[g])) for g in range(KV_HEADS)], axis=1
-    ).astype(bf16)
-    a_turned = a_ref[0].T
-    query_term = dot(a_turned, d_query)
-    pair_term = dot(a_turned, pairs)
-    d_a = (
-        dot(d_query, wq_ref[...], NT) + dot(d_key, wk_ref[...]) + dot(d_value, wv_ref[...])
-    )
-    scale = lax.rsqrt(jnp.sum(x * x, axis=-1, keepdims=True) * (1.0 / width) + eps_norm)
-    normed = x * scale
-    norm_term = jnp.sum(d_a * normed, axis=0, keepdims=True)
-
-    @pl.when(step == 0)
-    def _():
-        d_norm[...] = norm_term
-        g_query[...] = query_term
-        g_pairs[...] = pair_term
-
-    @pl.when(step > 0)
-    def _():
-        d_norm[...] += norm_term
-        g_query[...] += query_term
-        g_pairs[...] += pair_term
-
-    e = d_a * norm_ref[...]
-    mean = jnp.sum(e * normed, axis=-1, keepdims=True) * (1.0 / width)
-    out_ref[0] = (d_mid_ref[0] + scale * (e - normed * mean)).astype(bf16).T
-
-    @pl.when(step == pl.num_programs(0) - 1)
-    def _():
-        square = -(-width // LANES)
-        column = jnp.broadcast_to(d_norm[...], (8, width)).T[:, :1]
-        for t, tile in enumerate(head_tiles(g_query[...])):
-            if t == square - 1:
-                tile = with_column(tile, column)
-            put(g_ref, attn_place(t), width, tile.astype(bf16))
+    d_queries, d_pairs = [], []
+    g_norm = None
+    for s in range(seqs):
+        cos, sin = cos_ref[s], sin_ref[s]
+
+        def turn(tile, cos=cos, sin=sin):
+            return tile * cos - swap_halves(tile) * sin
+
+        def in_tiles(parts):
+            return [
+                join(parts[h], other_half(parts[h + 1])) for h in range(0, len(parts) - 1, 2)
+            ] + [parts[-1]]
+
+        heads, keys, values = [], [], []
         for g in range(KV_HEADS):
-            tile = g_pairs[:, g * LANES : (g + 1) * LANES]
-            put(g_ref, attn_place(square + g), width, tile.astype(bf16))
-        for t in range(square):
-            put(g_ref, attn_place(square + KV_HEADS + t), width, g_out_ref[t])
-        clear_rest(g_ref, 2 * square + KV_HEADS, width)
+            parts, kv = read_long(units[s * KV_HEADS + g], rows)
+            heads += parts
+            keys.append(kv)
+            values.append(other_half(kv))
+        d_query = flat([turn(t) * 0.125 for t in in_tiles(heads)])
+        key_tiles = [turn(t) for t in in_tiles(keys)]
+        d_key, d_value = flat(key_tiles), flat(in_tiles(values))
+        turned = [
+            key_tiles[g // 2] if g % 2 == 0 else other_half(key_tiles[g // 2])
+            for g in range(KV_HEADS)
+        ]
+        pairs = [join(turned[g], other_half(values[g])) for g in range(KV_HEADS)]
+        d_queries.append(d_query)
+        d_pairs.append(jnp.concatenate(pairs, axis=1).astype(bf16))
+        d_a = (
+            dot(d_query, wq_ref[...], NT) + dot(d_key, wk_ref[...]) + dot(d_value, wv_ref[...])
+        )
+        x = x_ref[s].T.astype(f32)
+        scale = lax.rsqrt(jnp.sum(x * x, axis=-1, keepdims=True) * (1.0 / width) + eps_norm)
+        normed = x * scale
+        term = jnp.sum(d_a * normed, axis=0, keepdims=True)
+        g_norm = term if g_norm is None else g_norm + term
+        e = d_a * as_row(norm_ref)
+        mean = jnp.sum(e * normed, axis=-1, keepdims=True) * (1.0 / width)
+        out_ref[s] = (d_mid_ref[s] + scale * (e - normed * mean)).astype(bf16).T
+    a_turned = jnp.concatenate([a_ref[s].T for s in range(seqs)], axis=1)
+    g_query = dot(a_turned, jnp.concatenate(d_queries, axis=0))
+    g_pairs = dot(a_turned, jnp.concatenate(d_pairs, axis=0))
+    square = -(-width // LANES)
+    column = jnp.broadcast_to(g_norm, (8, width)).T[:, :1]
+    for t, tile in enumerate(head_tiles(g_query)):
+        if t == square - 1:
+            tile = with_column(tile, column)
+        put(g_ref, attn_place(t), width, tile.astype(bf16))
+    for g in range(KV_HEADS):
+        tile = g_pairs[:, g * LANES : (g + 1) * LANES]
+        put(g_ref, attn_place(square + g), width, tile.astype(bf16))
+    for t in range(square):
+        put(g_ref, attn_place(square + KV_HEADS + t), width, g_out_ref[t])
+    clear_rest(g_ref, 2 * square + KV_HEADS, width)
 
 
 def clear_rest(g_ref, places, width):
@@ -1624,47 +1623,23 @@
 ):
     seqs, width, rows = x.shape
     count = len(messages)
-    row = lambda *shape: pl.BlockSpec((1,) + shape, lambda s, *_: (s,) + (0,) * len(shape))
+    vmem = pl.BlockSpec(memory_space=pltpu.VMEM)
     places = -(-(2 * -(-width // LANES) + KV_HEADS) // 2)
-    g_shape = (2, half_rows(places, width, parts), LANES)
     return pl.pallas_call(
         functools.partial(units_last_kernel, count),
-        grid_spec=pltpu.PrefetchScalarGridSpec(
-            num_scalar_prefetch=1,
-            grid=(seqs,),
-            in_specs=[
-                row(width, rows),
-                row(rows, width),
-                full_spec((1, width)),
-                full_spec(w_query.shape),
-                full_spec(w_key.shape),
-                full_spec(w_value.shape),
-                row(rows, LANES),
-                row(rows, LANES),
-                row(rows, width),
-                full_spec(last_d_q.shape),
-                full_spec(g_out.shape),
-            ]
-            + [full_spec(m.shape) for m in messages],
-            out_specs=[row(width, rows), full_spec(g_shape)],
-            scratch_shapes=[
-                pltpu.VMEM((count + 1, rows * 5 // 2, LANES), bf16),
-                pltpu.VMEM((width, width), f32),
-                pltpu.VMEM((width, KV_HEADS * LANES), f32),
-                pltpu.VMEM((1, width), f32),
-            ],
-        ),
+        in_specs=[pl.BlockSpec(memory_space=pltpu.SMEM)] + [vmem] * (11 + count),
         out_shape=[
             jax.ShapeDtypeStruct((seqs, width, rows), bf16),
-            jax.ShapeDtypeStruct(g_shape, bf16),
+            jax.ShapeDtypeStruct((2, half_rows(places, width, parts), LANES), bf16),
         ],
+        scratch_shapes=[pltpu.VMEM((count + 1, rows * 5 // 2, LANES), bf16)],
         compiler_params=params(60),
         name="last_part",
     )(ids, x, a, norm, w_query, w_key, w_value, cos, sin, d_mid, last_d_q, g_out, *messages)
 
 
 def to_all(messages):
-    count = messages.shape[0]
+    count = len(messages)
     return [messages[0]] + [
         lax.ppermute(messages[t], "seq", [(i, (i + t) % count) for i in range(count)])
         for t in range(1, count)
@@ -1741,16 +1716,18 @@
     seqs, width, rows = x.shape
     flat = lambda t: t.reshape(seqs * rows, t.shape[-1])
     ids = lax.axis_index("seq").astype(jnp.int32).reshape(1)
-    a, messages, last_q, last_kv = units_pre_call(
+    messages, a, last_q, last_kv = units_pre_call(
         ids, x, norm_one, w_query, wk_turned, wv_turned, cos, sin, count
     )
     masks = exchange_masks(count)
     swap = lambda part, mask: lax.ppermute(part, "seq", [(i, i ^ mask) for i in range(count)])
-    arrived = to_all(messages)
-    for mask in masks[:-1]:
+    last_kv = jnp.concatenate([last_kv, swap(last_kv, masks[0])], axis=0)
+    arrived, last_kv = lax.optimization_barrier((to_all(messages), last_kv))
+    first, *later = masks[1:]
+    last_kv = jnp.concatenate([last_kv, swap(last_kv, first)], axis=0)
+    attn_out, log_total, q, kv = units_forward_call(ids, arrived, ())
+    for mask in later:
         last_kv = jnp.concatenate([last_kv, swap(last_kv, mask)], axis=0)
-    attn_out, log_total, q, kv = units_forward_call(ids, arrived, (last_kv,))
-    last_kv = jnp.concatenate([last_kv, swap(last_kv, masks[-1])], axis=0)
     last_attn, last_log = last_unit_forward_call(ids, last_q, last_kv)
     mid, attn, hid, d_gate, d_up, g_ffn = units_ffn_call(
         ids, x, cot, to_all(attn_out), last_attn, w_out, norm_two, w_gate, w_up, w_down_turned
@@ -1758,7 +1735,7 @@
     g_ffn = lax.psum(g_ffn, ("seq", "batch"))
 
     def backward(mid, attn, hid, d_gate, d_up, q, kv, attn_out, log_total, last_attn, last_log, a):
-        d_mid, d_messages, d_last, g_norm_mlp = units_back_call(
+        d_messages, d_mid, d_last, g_norm_mlp = units_back_call(
             ids, mid, cot, d_gate, d_up, norm_two, w_out, w_gate, w_up, count
         )
         block_out, g_out = units_out_call(mid, attn, hid, d_mid, g_norm_mlp, w_down_turned)
@@ -1817,7 +1794,7 @@
     cot = jnp.transpose(cotangent, (1, 2, 0))
     wk_turned, wv_turned, w_down_turned = w_key.T, w_value.T, w_down.T
     cos, sin = rope_tables(positions)
-    norm_one, norm_two = norm_attn[None], norm_mlp[None]
+    norm_one, norm_two = norm_attn, norm_mlp
     def sum_over(value):
         for stage, place in zip(stages, places):
             value = scatter_stage(value, stage, place, devices)
@@ -1834,18 +1811,18 @@
         attn_unfold_kernel,
         "attn_unfold",
         (side, *attn_sums),
-        [(width, width), (kv_width, width), (kv_width, width), (1, width)]
-        + [(width, width), (1, width)],
+        [(width, width), (kv_width, width), (kv_width, width), (width,)]
+        + [(width, width), (width,)],
     )
     return (
         jnp.transpose(block_out, (2, 0, 1)),
         jnp.transpose(d_tokens, (2, 0, 1)),
-        g_norm_attn[0],
+        g_norm_attn,
         g_query,
         g_key.T,
         g_value.T,
         g_out,
-        g_norm_mlp[0],
+        g_norm_mlp,
         g_gate,
         g_up,
         g_down.T,

time: 335 us -> 324 us (0.967)
  waiting for transfers between devices: 73 us -> 83 us
  local copies, waits for them, and re-layouts: 15.5 us -> 7.58 us
  starting transfers between devices: 103 us -> 95.2 us
  Pallas kernels: 117 us -> 111 us
    ppermute x28, waiting for transfers between devices: 21.4 us -> 30.3 us  [to_all(): lax.ppermute(messages[t], 'seq', [(i, (i + t) % count) for i in range(cou...]
    ppermute x3, starting transfers between devices: 21 us -> 13.1 us  [units_layer(): lax.ppermute(part, 'seq', [(i, i ^ mask) for i in range(count)])]
    squeeze x4 -> x0, local copies, waits for them, and re-layouts: 6.93 us -> none  [to_all(): messages[t]]
    pallas_call x1, Pallas kernels: 20.5 us -> 15.9 us  [units_ffn_call(): pl.pallas_call(functools.partial(units_ffn_kernel, count), in_specs=[pl.B...]
  transfers between devices with their start and end apart: 46 -> 46, of which waited for: 26 -> 31; matrix products, arithmetic and copies ran while one was open for 5% -> 2% of each run, Pallas kernels for 25% -> 25%
where the time goes in v1:
time: 324 us; the launch traced here: 319 us
  Pallas kernels  111 us (34%)
  starting transfers between devices  95.2 us (29%)
  waiting for transfers between devices  83 us (26%)
  between operations  15.3 us (5%)
  local copies, waits for them, and re-layouts  7.58 us (2%)
  other arithmetic  6.49 us (2%)
    ppermute x28, starting transfers between devices, to_all(): lax.ppermute(messages[t], 'seq', [(i, (i + t) % count) for i in range(cou...  56.9 us
    ppermute x14, waiting for transfers between devices, swap_with(): lax.ppermute(value, ('seq', 'batch'), [(i, i ^ mask) for i in range(devic...  47 us
    ppermute x28, waiting for transfers between devices, to_all(): lax.ppermute(messages[t], 'seq', [(i, (i + t) % count) for i in range(cou...  30.3 us
    ppermute x14, starting transfers between devices, swap_with(): lax.ppermute(value, ('seq', 'batch'), [(i, i ^ mask) for i in range(devic...  25.1 us
    pallas_call x1, Pallas kernels, units_backward_call(): pl.pallas_call(functools.partial(units_backward_kernel, count), in_specs=...  25.1 us
    pallas_call x1, Pallas kernels, units_ffn_call(): pl.pallas_call(functools.partial(units_ffn_kernel, count), in_specs=[pl.B...  15.9 us
    ppermute x3, starting transfers between devices, units_layer(): lax.ppermute(part, 'seq', [(i, i ^ mask) for i in range(count)])  13.1 us
    pallas_call x1, Pallas kernels, units_forward_call(): pl.pallas_call(functools.partial(units_forward_kernel, count), in_specs=[...  13 us
  transfers between devices with their start and end apart: 46, of which 31 were waited for; matrix products, arithmetic and copies ran while one was open for 2% of the time, Pallas kernels for 25%

profile of v1, /device:TPU:0, one launch (start us, length us, event | category | flops | bytes accessed | tf_op | source)
XLA Modules:
  0.0 318.7 jit_solution(8240999205906599469)
XLA Ops:
  9.4 7.0 %project.1 = (bf16[640,128]{1,0:T(8,128)(2,1)}, bf16[640,128]{1,0:T(8,128)(2,1)}, bf16[640,128]{1,0:T(8,128)(2,1)}, bf16[640,128]{1,0:T(8,128)(2,1)}, bf16[640,1...) custom-call(s32[1]{0:T(128)} %bitcast.32.ids, ...), custom_call_target="tpu_custom_call" | custom-call | tf_op jit(solution)/shard_map/project/pallas_call | solution.py:1022
  16.4 3.0 collective-permute-start.28
  19.4 1.6 collective-permute-start.29
  25.3 2.8 collective-permute-done.35
  28.1 3.4 %collective-permute-start.32 = (bf16[640,128]{1,0:T(8,128)(2,1)}, bf16[640,128]{1,0:T(8,128)(2,1)S(1)}, u32[]{:S(2)}, u32[]{:S(2)}) collective-permute-start(bf16[640,128]{1,0:T(8,128)(2,1)} %get-tuple-element.223), channel_id=1, source_target_pairs={{0,20},{4,24},{8,28},{12,0},{16,4},{20,8},{24,12},{28,16},{1,21},{... | collective-permute-start | bytes 491528 | tf_op jit(solution)/shard_map/ppermute | solution.py:1644
  34.1 7.0 %collective-permute-done.30.refs_3_ = bf16[640,128]{1,0:T(8,128)(2,1)S(1)} collective-permute-done((bf16[640,128]{1,0:T(8,128)(2,1)}, bf16[640,128]{1,0:T(8,128)(2,1)S(1)}, u32[]{:S(2)}, u32[]{:S(2)}) %collective-permute-start.30) | collective-permute-done | bytes 163872 | tf_op jit(solution)/shard_map/ppermute | solution.py:1644
  42.2 8.6 %collective-permute-start.43 = (bf16[2,256,128]{2,1,0:T(8,128)(2,1)S(1)}, bf16[2,256,128]{2,1,0:T(8,128)(2,1)S(1)}, u32[]{:S(2)}, u32[]{:S(2)}) collective-permute-start(bf16[2,256,128]{2,1,0:T(8,128)(2,1)S(1)} %pad_maximum_fusion.3), channel_id=1, source_target_pairs={{0,8},{4,12},{8,0},{12,4},{16,24},{20,28},{24,16},{28,20},{1,9},{5... | collective-permute-start | bytes 393224 | tf_op jit(solution)/shard_map/ppermute | solution.py:1723
  50.7 2.9 collective-permute-done.43
  53.7 3.0 collective-permute-start.44
  57.6 13.0 %units_forward.1 = (bf16[384,128]{1,0:T(8,128)(2,1)S(1)}, bf16[384,128]{1,0:T(8,128)(2,1)S(1)}, bf16[384,128]{1,0:T(8,128)(2,1)S(1)}, bf16[384,128]{1,0:T(8,128)...) custom-call(s32[1]{0:T(128)} %bitcast.32.ids, ...), custom_call_target="tpu_custom_call" | custom-call | tf_op jit(solution)/shard_map/units_forward/pallas_call | solution.py:1097
  70.7 3.3 %collective-permute-start.36 = (bf16[384,128]{1,0:T(8,128)(2,1)S(1)}, bf16[384,128]{1,0:T(8,128)(2,1)S(1)}, u32[]{:S(2)}, u32[]{:S(2)}) collective-permute-start(bf16[384,128]{1,0:T(8,128)(2,1)S(1)} %get-tuple-element.236), channel_id=1, source_target_pairs={{0,4},{4,8},{8,12},{12,16},{16,20},{20,24},{24,28},{28,0},{1,5},{5... | collective-permute-start | bytes 294920 | tf_op jit(solution)/shard_map/ppermute | solution.py:1644
  74.9 3.0 collective-permute-start.39
  82.4 2.9 last_unit_forward.1
  89.1 15.9 %feed_forward.1 = (f32[3,256,576]{2,1,0:T(8,128)S(1)}, bf16[3,256,576]{2,1,0:T(8,128)(2,1)}, bf16[768,1536]{1,0:T(8,128)(2,1)}, bf16[768,1536]{1,0:T(8,128)(2,1)...) custom-call(s32[1]{0:T(128)} %bitcast.32.ids, bf16[3,576,256]{2,1,0:T(8,128)(2,1)S(1)} %bitcast.61, ...), custom_call_target="tpu_custom_call" | custom-call | tf_op jit(solution)/shard_map/feed_forward/pallas_call | solution.py:1359
  107.0 193.6 %conditional.1 = (bf16[3,576,256]{2,1,0:T(8,128)(2,1)}, bf16[3,576,256]{2,1,0:T(8,128)(2,1)}, bf16[4096,128]{1,0:T(8,128)(2,1)}, bf16[4096,128]{1,0:T(8,128)(2,1)}) conditional(s32[]{:T(128)} %bitcast.31, () %tuple.17, (s32[1]{0:T(128)}, f32[3,256,576]{2,1,0:T(8,128)S(1)}, bf16[3,576,256]{2,1,0:T(8,128)(2,1)}, bf16[768,1536]{1,0:T(8,128)(2,1)}, ...), branch_computations={%region_0.1_spmd, %region_1.2_spmd} | conditional | flops 6684727 | bytes 61016176 | solution.py:1768
  107.0 12.6 %feed_back.1 = (f32[3,256,576]{2,1,0:T(8,128)}, bf16[1,384,128]{2,1,0:T(8,128)(2,1)}, f32[1,576]{1,0:T(1,128)}, bf16[384,128]{1,0:T(8,128)(2,1)}, bf16[384,128]{...) custom-call(s32[1]{0:T(128)} %get-tuple-element.93.ids, ...), custom_call_target="tpu_custom_call" | custom-call | tf_op jit(solution)/shard_map/cond/branch_1_fun/feed_back/pallas_call | solution.py:1461
  119.7 2.8 collective-permute-start
  122.5 3.5 %collective-permute-start.1 = (bf16[384,128]{1,0:T(8,128)(2,1)}, bf16[384,128]{1,0:T(8,128)(2,1)S(1)}, u32[]{:S(2)}, u32[]{:S(2)}) collective-permute-start(bf16[384,128]{1,0:T(8,128)(2,1)} %get-tuple-element.122), channel_id=1, source_target_pairs={{0,8},{4,12},{8,16},{12,20},{16,24},{20,28},{24,0},{28,4},{1,9},{5... | collective-permute-start | bytes 294920 | tf_op jit(solution)/shard_map/cond/branch_1_fun/ppermute | solution.py:1644
  126.3 2.0 collective-permute-start.3
  128.2 2.9 collective-permute-start.4
  133.1 3.3 %collective-permute-start.6 = (bf16[384,128]{1,0:T(8,128)(2,1)}, bf16[384,128]{1,0:T(8,128)(2,1)S(1)}, u32[]{:S(2)}, u32[]{:S(2)}) collective-permute-start(bf16[384,128]{1,0:T(8,128)(2,1)} %get-tuple-element.127), channel_id=1, source_target_pairs={{0,28},{4,0},{8,4},{12,8},{16,12},{20,16},{24,20},{28,24},{1,29},{... | collective-permute-start | bytes 294920 | tf_op jit(solution)/shard_map/cond/branch_1_fun/ppermute | solution.py:1644
  137.3 5.9 %last_unit_backward.1 = (bf16[8,256,128]{2,1,0:T(8,128)(2,1)S(1)}, f32[768,128]{1,0:T(8,128)S(1)}) custom-call(s32[1]{0:T(128)} %get-tuple-element.93.ids, bf16[768,128]{1,0:T(8,128)(2,1)} %get-tuple-element.113.q_ref, bf16[8,256,128]{2,1,0:T(8,128)(2,1)S(1)} %copy-done.8, bf16[384,128]{1,0:T(8,128)(2,1)S(1)} %bitcast.59, bf16[384,128]{1,0:T(8,128)(2,1)} %bitcast.84, ...), custom_call_target="tpu_custom_call" | custom-call | tf_op jit(solution)/shard_map/cond/branch_1_fun/last_unit_backward/pallas_call | solution.py:1186
  144.8 2.5 collective-permute-done.6.refs_7_
  147.9 25.1 %units_backward.1 = (bf16[896,128]{1,0:T(8,128)(2,1)}, bf16[896,128]{1,0:T(8,128)(2,1)}, bf16[896,128]{1,0:T(8,128)(2,1)}, bf16[896,128]{1,0:T(8,128)(2,1)}, bf1...) custom-call(s32[1]{0:T(128)} %get-tuple-element.93.ids, ...), custom_call_target="tpu_custom_call" | custom-call | tf_op jit(solution)/shard_map/cond/branch_1_fun/units_backward/pallas_call | solution.py:1244
  174.1 7.7 %collective-permute-start.8 = (bf16[896,128]{1,0:T(8,128)(2,1)}, bf16[896,128]{1,0:T(8,128)(2,1)}, u32[]{:S(2)}, u32[]{:S(2)}) collective-permute-start(bf16[896,128]{1,0:T(8,128)(2,1)} %get-tuple-element.142), channel_id=1, source_target_pairs={{0,8},{4,12},{8,16},{12,20},{16,24},{20,28},{24,0},{28,4},{1,9},{5... | collective-permute-start | bytes 688136 | tf_op jit(solution)/shard_map/cond/branch_1_fun/ppermute | solution.py:1644
  183.3 3.4 %collective-permute-start.11 = (bf16[896,128]{1,0:T(8,128)(2,1)}, bf16[896,128]{1,0:T(8,128)(2,1)}, u32[]{:S(2)}, u32[]{:S(2)}) collective-permute-start(bf16[896,128]{1,0:T(8,128)(2,1)} %get-tuple-element.145), channel_id=1, source_target_pairs={{0,20},{4,24},{8,28},{12,0},{16,4},{20,8},{24,12},{28,16},{1,21},{... | collective-permute-start | bytes 688136 | tf_op jit(solution)/shard_map/cond/branch_1_fun/ppermute | solution.py:1644
  186.7 2.1 collective-permute-done.7.refs_1_
  189.0 5.5 %collective-permute-start.13 = (bf16[896,128]{1,0:T(8,128)(2,1)}, bf16[896,128]{1,0:T(8,128)(2,1)}, u32[]{:S(2)}, u32[]{:S(2)}) collective-permute-start(bf16[896,128]{1,0:T(8,128)(2,1)} %get-tuple-element.147), channel_id=1, source_target_pairs={{0,28},{4,0},{8,4},{12,8},{16,12},{20,16},{24,20},{28,24},{1,29},{... | collective-permute-start | bytes 688136 | tf_op jit(solution)/shard_map/cond/branch_1_fun/ppermute | solution.py:1644
  194.5 7.4 %feed_out.1 = (bf16[3,576,256]{2,1,0:T(8,128)(2,1)}, bf16[5,576,128]{2,1,0:T(8,128)(2,1)}) custom-call(f32[3,256,576]{2,1,0:T(8,128)S(1)} %get-tuple-element.90.mid_ref, bf16[3,256,576]{2,1,0:T(8,128)(2,1)} %get-tuple-element.91.attn_ref, bf16[768,1536]{1,0:T(8,128)(2,1)} %get-tuple-element.92.hid_ref, f32[3,256,576]{2,1,0:T(8,128)} %get-tuple-element.101.d_mid_ref, ...), custom_call_target="tpu_custom_call" | custom-call | tf_op jit(solution)/shard_map/cond/branch_1_fun/feed_out/pallas_call | solution.py:1517
  202.0 7.0 %collective-permute-done.9.refs_3_ = bf16[896,128]{1,0:T(8,128)(2,1)} collective-permute-done((bf16[896,128]{1,0:T(8,128)(2,1)}, bf16[896,128]{1,0:T(8,128)(2,1)}, u32[]{:S(2)}, u32[]{:S(2)}) %collective-permute-start.9) | collective-permute-done | bytes 229408 | tf_op jit(solution)/shard_map/cond/branch_1_fun/ppermute | solution.py:1644
  210.8 2.5 collective-permute-done.13.refs_7_
  213.3 9.9 %last_part.1 = (bf16[3,576,256]{2,1,0:T(8,128)(2,1)}, bf16[2,4096,128]{2,1,0:T(8,128)(2,1)}) custom-call(s32[1]{0:T(128)} %get-tuple-element.93.ids, bf16[3,576,256]{2,1,0:T(8,128)(2,1)S(1)} %get-tuple-element.105.x_ref, bf16[3,256,576]{2,1,0:T(8,128)(2,1)} %get-tuple-element.106.a_ref, f32[576]{0:T(1024)S(1)} %get-tuple-element.107.norm_ref, ...), custom_call_target="tpu_custom_call" | custom-call | tf_op jit(solution)/shard_map/cond/branch_1_fun/last_part/pallas_call | solution.py:1628
  224.8 2.8 collective-permute-done.14
  229.1 3.5 %collective-permute-start.17 = (bf16[1024,128]{1,0:T(8,128)(2,1)S(1)}, bf16[1024,128]{1,0:T(8,128)(2,1)S(1)}, u32[]{:S(2)}, u32[]{:S(2)}) collective-permute-start(bf16[1024,128]{1,0:T(8,128)(2,1)S(1)} %get-tuple-element.271), channel_id=1, source_target_pairs={{0,6},{1,7},{2,4},{3,5},{4,2},{5,3},{6,0},{7,1},{8,14},{9,15},{10,... | collective-permute-start | bytes 786440 | tf_op jit(solution)/shard_map/cond/branch_1_fun/ppermute | solution.py:788
  233.2 6.5 %collective-permute-done.17 = bf16[1024,128]{1,0:T(8,128)(2,1)S(1)} collective-permute-done((bf16[1024,128]{1,0:T(8,128)(2,1)S(1)}, bf16[1024,128]{1,0:T(8,128)(2,1)S(1)}, u32[]{:S(2)}, u32[]{:S(2)}) %collective-permute-start.17) | collective-permute-done | bytes 262176 | tf_op jit(solution)/shard_map/cond/branch_1_fun/ppermute | solution.py:788
  239.7 7.6 %collective-permute-done.16 = bf16[1024,128]{1,0:T(8,128)(2,1)S(1)} collective-permute-done((bf16[1024,128]{1,0:T(8,128)(2,1)S(1)}, bf16[1024,128]{1,0:T(8,128)(2,1)S(1)}, u32[]{:S(2)}, u32[]{:S(2)}) %collective-permute-start.16) | collective-permute-done | bytes 262176 | tf_op jit(solution)/shard_map/cond/branch_1_fun/ppermute | solution.py:788
  247.4 11.2 %collective-permute-start.20 = (bf16[256,128]{1,0:T(8,128)(2,1)S(1)}, bf16[256,128]{1,0:T(8,128)(2,1)S(1)}, u32[]{:S(2)}, u32[]{:S(2)}) collective-permute-start(bf16[256,128]{1,0:T(8,128)(2,1)S(1)} %get-tuple-element.274), channel_id=1, source_target_pairs={{0,16},{1,17},{2,18},{3,19},{4,20},{5,21},{6,22},{7,23},{8,24},{9,... | collective-permute-start | bytes 196616 | tf_op jit(solution)/shard_map/cond/branch_1_fun/ppermute | solution.py:788
  258.7 2.5 collective-permute-start.19
  261.2 3.9 %collective-permute-done.20 = bf16[256,128]{1,0:T(8,128)(2,1)S(1)} collective-permute-done((bf16[256,128]{1,0:T(8,128)(2,1)S(1)}, bf16[256,128]{1,0:T(8,128)(2,1)S(1)}, u32[]{:S(2)}, u32[]{:S(2)}) %collective-permute-start.20) | collective-permute-done | bytes 65568 | tf_op jit(solution)/shard_map/cond/branch_1_fun/ppermute | solution.py:788
  266.2 2.4 collective-permute-start.23
  269.8 3.9 %collective-permute-done.23 = bf16[256,128]{1,0:T(8,128)(2,1)S(1)} collective-permute-done((bf16[256,128]{1,0:T(8,128)(2,1)S(1)}, bf16[256,128]{1,0:T(8,128)(2,1)S(1)}, u32[]{:S(2)}, u32[]{:S(2)}) %collective-permute-start.23) | collective-permute-done | bytes 65568 | tf_op jit(solution)/shard_map/cond/branch_1_fun/ppermute | solution.py:788
  276.2 1.9 collective-permute-start.26
  278.1 1.7 collective-permute-start.25
  279.8 11.7 %collective-permute-done.26 = bf16[4,256,128]{2,1,0:T(8,128)(2,1)S(1)} collective-permute-done((bf16[4,256,128]{2,1,0:T(8,128)(2,1)S(1)}, bf16[4,256,128]{2,1,0:T(8,128)(2,1)S(1)}, u32[]{:S(2)}, u32[]{:S(2)}) %collective-permute-start.26) | collective-permute-done | bytes 262176 | tf_op jit(solution)/shard_map/cond/branch_1_fun/ppermute | solution.py:788
  291.5 4.1 %collective-permute-done.25 = bf16[4,256,128]{2,1,0:T(8,128)(2,1)S(1)} collective-permute-done((bf16[4,256,128]{2,1,0:T(8,128)(2,1)S(1)}, bf16[4,256,128]{2,1,0:T(8,128)(2,1)S(1)}, u32[]{:S(2)}, u32[]{:S(2)}) %collective-permute-start.25) | collective-permute-done | bytes 262176 | tf_op jit(solution)/shard_map/cond/branch_1_fun/ppermute | solution.py:788
  297.4 3.0 collective-permute-done.27
  300.6 3.9 %attn_unfold.1 = (f32[576,576]{1,0:T(8,128)}, f32[192,576]{1,0:T(8,128)}, f32[192,576]{1,0:T(8,128)}, f32[576]{0:T(1024)}, f32[576,576]{1,0:T(8,128)}, /*index=5*/f32[576]{0:T(1024)}) custom-call(s32[1]{0:T(128)} %bitcast.41.side, bf16[4096,128]{1,0:T(8,128)(2,1)} %get-tuple-element.258.mine, bf16[4096,128]{1,0:T(8,128)(2,1)} %get-tuple-element.259.other), custom_call_target="tpu_custom_call" | custom-call | tf_op jit(solution)/shard_map/attn_unfold/pallas_call | solution.py:609
  304.5 7.2 %ffn_unfold.1 = (f32[576,1536]{1,0:T(8,128)}, f32[576,1536]{1,0:T(8,128)}, f32[576,1536]{1,0:T(8,128)}) custom-call(bf16[2,18,576,128]{3,2,1,0:T(8,128)(2,1)} %all-reduce.2.cloned.1.call-done.gate_in.up_in.down_in, bf16[2,18,576,128]{3,2,1,0:T(8,128)(2,1)} %all-reduce.2.cloned.1.call-done.gate_in.up_in.down_in, ...), custom_call_target="tpu_custom_call" | custom-call | tf_op jit(solution)/shard_map/ffn_unfold/pallas_call | solution.py:582
  (154 shorter events, 41.8 us)
Async XLA Ops:
  7.2 297.3 %all-reduce.2.cloned.1.call-start = ((), (), s32[]{:S(2)}) async-start(), calls=%async_computation | async-start | bytes 10616832 | tf_op jit(solution)/shard_map/psum | solution.py:1735
  9.4 79.6 %copy-start.4 = (bf16[256,3,576]{0,2,1:T(8,128)(2,1)S(1)}, bf16[256,3,576]{0,2,1:T(8,128)(2,1)}, u32[]{:S(2)}) copy-start(bf16[256,3,576]{0,2,1:T(8,128)(2,1)} %param.14) | copy-start | bytes 2654212
  16.4 72.6 %copy-start.36 = (f32[576]{0:T(1024)S(1)}, f32[576]{0:T(1024)}, u32[]{:S(2)}) copy-start(f32[576]{0:T(1024)} %norm_ref.3) | copy-start | bytes 6916
  16.4 15.1 %collective-permute-start.28 = (bf16[640,128]{1,0:T(8,128)(2,1)}, bf16[640,128]{1,0:T(8,128)(2,1)S(1)}, u32[]{:S(2)}, u32[]{:S(2)}) collective-permute-start(bf16[640,128]{1,0:T(8,128)(2,1)} %get-tuple-element.219), channel_id=1, source_target_pairs={{0,4},{4,8},{8,12},{12,16},{16,20},{20,24},{24,28},{28,0},{1,5},{5... | collective-permute-start | bytes 491528 | tf_op jit(solution)/shard_map/ppermute | solution.py:1644
  19.4 13.6 %collective-permute-start.29 = (bf16[640,128]{1,0:T(8,128)(2,1)}, bf16[640,128]{1,0:T(8,128)(2,1)S(1)}, u32[]{:S(2)}, u32[]{:S(2)}) collective-permute-start(bf16[640,128]{1,0:T(8,128)(2,1)} %get-tuple-element.220), channel_id=1, source_target_pairs={{0,8},{4,12},{8,16},{12,20},{16,24},{20,28},{24,0},{28,4},{1,9},{5... | collective-permute-start | bytes 491528 | tf_op jit(solution)/shard_map/ppermute | solution.py:1644
  21.0 7.1 %collective-permute-start.35 = (bf16[1,256,128]{2,1,0:T(8,128)(2,1)}, bf16[1,256,128]{2,1,0:T(8,128)(2,1)S(1)}, u32[]{:S(2)}, u32[]{:S(2)}) collective-permute-start(bf16[1,256,128]{2,1,0:T(8,128)(2,1)} %get-tuple-element.226), channel_id=1, source_target_pairs={{0,4},{4,0},{8,12},{12,8},{16,20},{20,16},{24,28},{28,24},{1,5},{5... | collective-permute-start | bytes 196616 | tf_op jit(solution)/shard_map/ppermute | solution.py:1723
  22.6 18.6 %collective-permute-start.30 = (bf16[640,128]{1,0:T(8,128)(2,1)}, bf16[640,128]{1,0:T(8,128)(2,1)S(1)}, u32[]{:S(2)}, u32[]{:S(2)}) collective-permute-start(bf16[640,128]{1,0:T(8,128)(2,1)} %get-tuple-element.221), channel_id=1, source_target_pairs={{0,12},{4,16},{8,20},{12,24},{16,28},{20,0},{24,4},{28,8},{1,13},{... | collective-permute-start | bytes 491528 | tf_op jit(solution)/shard_map/ppermute | solution.py:1644
  24.0 17.4 %collective-permute-start.31 = (bf16[640,128]{1,0:T(8,128)(2,1)}, bf16[640,128]{1,0:T(8,128)(2,1)S(1)}, u32[]{:S(2)}, u32[]{:S(2)}) collective-permute-start(bf16[640,128]{1,0:T(8,128)(2,1)} %get-tuple-element.222), channel_id=1, source_target_pairs={{0,16},{4,20},{8,24},{12,28},{16,0},{20,4},{24,8},{28,12},{1,17},{... | collective-permute-start | bytes 491528 | tf_op jit(solution)/shard_map/ppermute | solution.py:1644
  28.1 13.3 %collective-permute-start.32 = (bf16[640,128]{1,0:T(8,128)(2,1)}, bf16[640,128]{1,0:T(8,128)(2,1)S(1)}, u32[]{:S(2)}, u32[]{:S(2)}) collective-permute-start(bf16[640,128]{1,0:T(8,128)(2,1)} %get-tuple-element.223), channel_id=1, source_target_pairs={{0,20},{4,24},{8,28},{12,0},{16,4},{20,8},{24,12},{28,16},{1,21},{... | collective-permute-start | bytes 491528 | tf_op jit(solution)/shard_map/ppermute | solution.py:1644
  31.5 9.9 %collective-permute-start.33 = (bf16[640,128]{1,0:T(8,128)(2,1)}, bf16[640,128]{1,0:T(8,128)(2,1)S(1)}, u32[]{:S(2)}, u32[]{:S(2)}) collective-permute-start(bf16[640,128]{1,0:T(8,128)(2,1)} %get-tuple-element.224), channel_id=1, source_target_pairs={{0,24},{4,28},{8,0},{12,4},{16,8},{20,12},{24,16},{28,20},{1,25},{... | collective-permute-start | bytes 491528 | tf_op jit(solution)/shard_map/ppermute | solution.py:1644
  33.0 9.1 %collective-permute-start.34 = (bf16[640,128]{1,0:T(8,128)(2,1)}, bf16[640,128]{1,0:T(8,128)(2,1)S(1)}, u32[]{:S(2)}, u32[]{:S(2)}) collective-permute-start(bf16[640,128]{1,0:T(8,128)(2,1)} %get-tuple-element.225), channel_id=1, source_target_pairs={{0,28},{4,0},{8,4},{12,8},{16,12},{20,16},{24,20},{28,24},{1,29},{... | collective-permute-start | bytes 491528 | tf_op jit(solution)/shard_map/ppermute | solution.py:1644
  42.2 11.5 %collective-permute-start.43 = (bf16[2,256,128]{2,1,0:T(8,128)(2,1)S(1)}, bf16[2,256,128]{2,1,0:T(8,128)(2,1)S(1)}, u32[]{:S(2)}, u32[]{:S(2)}) collective-permute-start(bf16[2,256,128]{2,1,0:T(8,128)(2,1)S(1)} %pad_maximum_fusion.3), channel_id=1, source_target_pairs={{0,8},{4,12},{8,0},{12,4},{16,24},{20,28},{24,16},{28,20},{1,9},{5... | collective-permute-start | bytes 393224 | tf_op jit(solution)/shard_map/ppermute | solution.py:1723
  53.7 28.1 %collective-permute-start.44 = (bf16[4,256,128]{2,1,0:T(8,128)(2,1)S(1)}, bf16[4,256,128]{2,1,0:T(8,128)(2,1)S(1)}, u32[]{:S(2)}, u32[]{:S(2)}) collective-permute-start(bf16[4,256,128]{2,1,0:T(8,128)(2,1)S(1)} %pad_maximum_fusion.2), channel_id=1, source_target_pairs={{0,24},{4,28},{8,16},{12,20},{16,8},{20,12},{24,0},{28,4},{1,25},{... | collective-permute-start | bytes 786440 | tf_op jit(solution)/shard_map/ppermute | solution.py:1723
  70.7 8.3 %collective-permute-start.36 = (bf16[384,128]{1,0:T(8,128)(2,1)S(1)}, bf16[384,128]{1,0:T(8,128)(2,1)S(1)}, u32[]{:S(2)}, u32[]{:S(2)}) collective-permute-start(bf16[384,128]{1,0:T(8,128)(2,1)S(1)} %get-tuple-element.236), channel_id=1, source_target_pairs={{0,4},{4,8},{8,12},{12,16},{16,20},{20,24},{24,28},{28,0},{1,5},{5... | collective-permute-start | bytes 294920 | tf_op jit(solution)/shard_map/ppermute | solution.py:1644
  74.0 6.8 %collective-permute-start.37 = (bf16[384,128]{1,0:T(8,128)(2,1)S(1)}, bf16[384,128]{1,0:T(8,128)(2,1)S(1)}, u32[]{:S(2)}, u32[]{:S(2)}) collective-permute-start(bf16[384,128]{1,0:T(8,128)(2,1)S(1)} %get-tuple-element.237), channel_id=1, source_target_pairs={{0,8},{4,12},{8,16},{12,20},{16,24},{20,28},{24,0},{28,4},{1,9},{5... | collective-permute-start | bytes 294920 | tf_op jit(solution)/shard_map/ppermute | solution.py:1644
  74.0 11.7 %collective-permute-start.38 = (bf16[384,128]{1,0:T(8,128)(2,1)S(1)}, bf16[384,128]{1,0:T(8,128)(2,1)S(1)}, u32[]{:S(2)}, u32[]{:S(2)}) collective-permute-start(bf16[384,128]{1,0:T(8,128)(2,1)S(1)} %get-tuple-element.238), channel_id=1, source_target_pairs={{0,12},{4,16},{8,20},{12,24},{16,28},{20,0},{24,4},{28,8},{1,13},{... | collective-permute-start | bytes 294920 | tf_op jit(solution)/shard_map/ppermute | solution.py:1644
  74.9 11.9 %collective-permute-start.39 = (bf16[384,128]{1,0:T(8,128)(2,1)S(1)}, bf16[384,128]{1,0:T(8,128)(2,1)S(1)}, u32[]{:S(2)}, u32[]{:S(2)}) collective-permute-start(bf16[384,128]{1,0:T(8,128)(2,1)S(1)} %get-tuple-element.239), channel_id=1, source_target_pairs={{0,16},{4,20},{8,24},{12,28},{16,0},{20,4},{24,8},{28,12},{1,17},{... | collective-permute-start | bytes 294920 | tf_op jit(solution)/shard_map/ppermute | solution.py:1644
  78.9 7.9 %collective-permute-start.40 = (bf16[384,128]{1,0:T(8,128)(2,1)S(1)}, bf16[384,128]{1,0:T(8,128)(2,1)S(1)}, u32[]{:S(2)}, u32[]{:S(2)}) collective-permute-start(bf16[384,128]{1,0:T(8,128)(2,1)S(1)} %get-tuple-element.240), channel_id=1, source_target_pairs={{0,20},{4,24},{8,28},{12,0},{16,4},{20,8},{24,12},{28,16},{1,21},{... | collective-permute-start | bytes 294920 | tf_op jit(solution)/shard_map/ppermute | solution.py:1644
  80.8 7.5 %collective-permute-start.41 = (bf16[384,128]{1,0:T(8,128)(2,1)S(1)}, bf16[384,128]{1,0:T(8,128)(2,1)S(1)}, u32[]{:S(2)}, u32[]{:S(2)}) collective-permute-start(bf16[384,128]{1,0:T(8,128)(2,1)S(1)} %get-tuple-element.241), channel_id=1, source_target_pairs={{0,24},{4,28},{8,0},{12,4},{16,8},{20,12},{24,16},{28,20},{1,25},{... | collective-permute-start | bytes 294920 | tf_op jit(solution)/shard_map/ppermute | solution.py:1644
  81.8 6.5 %collective-permute-start.42 = (bf16[384,128]{1,0:T(8,128)(2,1)S(1)}, bf16[384,128]{1,0:T(8,128)(2,1)S(1)}, u32[]{:S(2)}, u32[]{:S(2)}) collective-permute-start(bf16[384,128]{1,0:T(8,128)(2,1)S(1)} %get-tuple-element.242), channel_id=1, source_target_pairs={{0,28},{4,0},{8,4},{12,8},{16,12},{20,16},{24,20},{28,24},{1,29},{... | collective-permute-start | bytes 294920 | tf_op jit(solution)/shard_map/ppermute | solution.py:1644
  119.7 12.7 %collective-permute-start = (bf16[384,128]{1,0:T(8,128)(2,1)}, bf16[384,128]{1,0:T(8,128)(2,1)S(1)}, u32[]{:S(2)}, u32[]{:S(2)}) collective-permute-start(bf16[384,128]{1,0:T(8,128)(2,1)} %get-tuple-element.121), channel_id=1, source_target_pairs={{0,4},{4,8},{8,12},{12,16},{16,20},{20,24},{24,28},{28,0},{1,5},{5... | collective-permute-start | bytes 294920 | tf_op jit(solution)/shard_map/cond/branch_1_fun/ppermute | solution.py:1644
  122.5 10.6 %collective-permute-start.1 = (bf16[384,128]{1,0:T(8,128)(2,1)}, bf16[384,128]{1,0:T(8,128)(2,1)S(1)}, u32[]{:S(2)}, u32[]{:S(2)}) collective-permute-start(bf16[384,128]{1,0:T(8,128)(2,1)} %get-tuple-element.122), channel_id=1, source_target_pairs={{0,8},{4,12},{8,16},{12,20},{16,24},{20,28},{24,0},{28,4},{1,9},{5... | collective-permute-start | bytes 294920 | tf_op jit(solution)/shard_map/cond/branch_1_fun/ppermute | solution.py:1644
  126.0 18.7 %collective-permute-start.2 = (bf16[384,128]{1,0:T(8,128)(2,1)}, bf16[384,128]{1,0:T(8,128)(2,1)S(1)}, u32[]{:S(2)}, u32[]{:S(2)}) collective-permute-start(bf16[384,128]{1,0:T(8,128)(2,1)} %get-tuple-element.123), channel_id=1, source_target_pairs={{0,12},{4,16},{8,20},{12,24},{16,28},{20,0},{24,4},{28,8},{1,13},{... | collective-permute-start | bytes 294920 | tf_op jit(solution)/shard_map/cond/branch_1_fun/ppermute | solution.py:1644
  126.3 18.4 %collective-permute-start.3 = (bf16[384,128]{1,0:T(8,128)(2,1)}, bf16[384,128]{1,0:T(8,128)(2,1)S(1)}, u32[]{:S(2)}, u32[]{:S(2)}) collective-permute-start(bf16[384,128]{1,0:T(8,128)(2,1)} %get-tuple-element.124), channel_id=1, source_target_pairs={{0,16},{4,20},{8,24},{12,28},{16,0},{20,4},{24,8},{28,12},{1,17},{... | collective-permute-start | bytes 294920 | tf_op jit(solution)/shard_map/cond/branch_1_fun/ppermute | solution.py:1644
  128.2 16.5 %collective-permute-start.4 = (bf16[384,128]{1,0:T(8,128)(2,1)}, bf16[384,128]{1,0:T(8,128)(2,1)S(1)}, u32[]{:S(2)}, u32[]{:S(2)}) collective-permute-start(bf16[384,128]{1,0:T(8,128)(2,1)} %get-tuple-element.125), channel_id=1, source_target_pairs={{0,20},{4,24},{8,28},{12,0},{16,4},{20,8},{24,12},{28,16},{1,21},{... | collective-permute-start | bytes 294920 | tf_op jit(solution)/shard_map/cond/branch_1_fun/ppermute | solution.py:1644
  132.3 12.4 %collective-permute-start.5 = (bf16[384,128]{1,0:T(8,128)(2,1)}, bf16[384,128]{1,0:T(8,128)(2,1)S(1)}, u32[]{:S(2)}, u32[]{:S(2)}) collective-permute-start(bf16[384,128]{1,0:T(8,128)(2,1)} %get-tuple-element.126), channel_id=1, source_target_pairs={{0,24},{4,28},{8,0},{12,4},{16,8},{20,12},{24,16},{28,20},{1,25},{... | collective-permute-start | bytes 294920 | tf_op jit(solution)/shard_map/cond/branch_1_fun/ppermute | solution.py:1644
  133.1 14.2 %collective-permute-start.6 = (bf16[384,128]{1,0:T(8,128)(2,1)}, bf16[384,128]{1,0:T(8,128)(2,1)S(1)}, u32[]{:S(2)}, u32[]{:S(2)}) collective-permute-start(bf16[384,128]{1,0:T(8,128)(2,1)} %get-tuple-element.127), channel_id=1, source_target_pairs={{0,28},{4,0},{8,4},{12,8},{16,12},{20,16},{24,20},{28,24},{1,29},{... | collective-permute-start | bytes 294920 | tf_op jit(solution)/shard_map/cond/branch_1_fun/ppermute | solution.py:1644
  173.0 15.7 %collective-permute-start.7 = (bf16[896,128]{1,0:T(8,128)(2,1)}, bf16[896,128]{1,0:T(8,128)(2,1)}, u32[]{:S(2)}, u32[]{:S(2)}) collective-permute-start(bf16[896,128]{1,0:T(8,128)(2,1)} %get-tuple-element.141), channel_id=1, source_target_pairs={{0,4},{4,8},{8,12},{12,16},{16,20},{20,24},{24,28},{28,0},{1,5},{5... | collective-permute-start | bytes 688136 | tf_op jit(solution)/shard_map/cond/branch_1_fun/ppermute | solution.py:1644
  174.1 14.9 %collective-permute-start.8 = (bf16[896,128]{1,0:T(8,128)(2,1)}, bf16[896,128]{1,0:T(8,128)(2,1)}, u32[]{:S(2)}, u32[]{:S(2)}) collective-permute-start(bf16[896,128]{1,0:T(8,128)(2,1)} %get-tuple-element.142), channel_id=1, source_target_pairs={{0,8},{4,12},{8,16},{12,20},{16,24},{20,28},{24,0},{28,4},{1,9},{5... | collective-permute-start | bytes 688136 | tf_op jit(solution)/shard_map/cond/branch_1_fun/ppermute | solution.py:1644
  181.8 27.1 %collective-permute-start.9 = (bf16[896,128]{1,0:T(8,128)(2,1)}, bf16[896,128]{1,0:T(8,128)(2,1)}, u32[]{:S(2)}, u32[]{:S(2)}) collective-permute-start(bf16[896,128]{1,0:T(8,128)(2,1)} %get-tuple-element.143), channel_id=1, source_target_pairs={{0,12},{4,16},{8,20},{12,24},{16,28},{20,0},{24,4},{28,8},{1,13},{... | collective-permute-start | bytes 688136 | tf_op jit(solution)/shard_map/cond/branch_1_fun/ppermute | solution.py:1644
  181.8 27.7 %collective-permute-start.10 = (bf16[896,128]{1,0:T(8,128)(2,1)}, bf16[896,128]{1,0:T(8,128)(2,1)}, u32[]{:S(2)}, u32[]{:S(2)}) collective-permute-start(bf16[896,128]{1,0:T(8,128)(2,1)} %get-tuple-element.144), channel_id=1, source_target_pairs={{0,16},{4,20},{8,24},{12,28},{16,0},{20,4},{24,8},{28,12},{1,17},{... | collective-permute-start | bytes 688136 | tf_op jit(solution)/shard_map/cond/branch_1_fun/ppermute | solution.py:1644
  183.3 26.2 %collective-permute-start.11 = (bf16[896,128]{1,0:T(8,128)(2,1)}, bf16[896,128]{1,0:T(8,128)(2,1)}, u32[]{:S(2)}, u32[]{:S(2)}) collective-permute-start(bf16[896,128]{1,0:T(8,128)(2,1)} %get-tuple-element.145), channel_id=1, source_target_pairs={{0,20},{4,24},{8,28},{12,0},{16,4},{20,8},{24,12},{28,16},{1,21},{... | collective-permute-start | bytes 688136 | tf_op jit(solution)/shard_map/cond/branch_1_fun/ppermute | solution.py:1644
  188.8 22.0 %collective-permute-start.12 = (bf16[896,128]{1,0:T(8,128)(2,1)}, bf16[896,128]{1,0:T(8,128)(2,1)}, u32[]{:S(2)}, u32[]{:S(2)}) collective-permute-start(bf16[896,128]{1,0:T(8,128)(2,1)} %get-tuple-element.146), channel_id=1, source_target_pairs={{0,24},{4,28},{8,0},{12,4},{16,8},{20,12},{24,16},{28,20},{1,25},{... | collective-permute-start | bytes 688136 | tf_op jit(solution)/shard_map/cond/branch_1_fun/ppermute | solution.py:1644
  189.0 24.3 %collective-permute-start.13 = (bf16[896,128]{1,0:T(8,128)(2,1)}, bf16[896,128]{1,0:T(8,128)(2,1)}, u32[]{:S(2)}, u32[]{:S(2)}) collective-permute-start(bf16[896,128]{1,0:T(8,128)(2,1)} %get-tuple-element.147), channel_id=1, source_target_pairs={{0,28},{4,0},{8,4},{12,8},{16,12},{20,16},{24,20},{28,24},{1,29},{... | collective-permute-start | bytes 688136 | tf_op jit(solution)/shard_map/cond/branch_1_fun/ppermute | solution.py:1644
  224.6 2.9 collective-permute-start.14
  229.1 10.6 %collective-permute-start.17 = (bf16[1024,128]{1,0:T(8,128)(2,1)S(1)}, bf16[1024,128]{1,0:T(8,128)(2,1)S(1)}, u32[]{:S(2)}, u32[]{:S(2)}) collective-permute-start(bf16[1024,128]{1,0:T(8,128)(2,1)S(1)} %get-tuple-element.271), channel_id=1, source_target_pairs={{0,6},{1,7},{2,4},{3,5},{4,2},{5,3},{6,0},{7,1},{8,14},{9,15},{10,... | collective-permute-start | bytes 786440 | tf_op jit(solution)/shard_map/cond/branch_1_fun/ppermute | solution.py:788
  232.6 14.7 %collective-permute-start.16 = (bf16[1024,128]{1,0:T(8,128)(2,1)S(1)}, bf16[1024,128]{1,0:T(8,128)(2,1)S(1)}, u32[]{:S(2)}, u32[]{:S(2)}) collective-permute-start(bf16[1024,128]{1,0:T(8,128)(2,1)S(1)} %get-tuple-element.272), channel_id=1, source_target_pairs={{0,4},{1,5},{2,6},{3,7},{4,0},{5,1},{6,2},{7,3},{8,12},{9,13},{10,... | collective-permute-start | bytes 786440 | tf_op jit(solution)/shard_map/cond/branch_1_fun/ppermute | solution.py:788
  232.6 14.7 %collective-permute-start.15 = (bf16[1024,128]{1,0:T(8,128)(2,1)S(1)}, bf16[1024,128]{1,0:T(8,128)(2,1)S(1)}, u32[]{:S(2)}, u32[]{:S(2)}) collective-permute-start(bf16[1024,128]{1,0:T(8,128)(2,1)S(1)} %get-tuple-element.270), channel_id=1, source_target_pairs={{0,2},{1,3},{2,0},{3,1},{4,6},{5,7},{6,4},{7,5},{8,10},{9,11},{10,... | collective-permute-start | bytes 786440 | tf_op jit(solution)/shard_map/cond/branch_1_fun/ppermute | solution.py:788
  247.4 17.7 %collective-permute-start.20 = (bf16[256,128]{1,0:T(8,128)(2,1)S(1)}, bf16[256,128]{1,0:T(8,128)(2,1)S(1)}, u32[]{:S(2)}, u32[]{:S(2)}) collective-permute-start(bf16[256,128]{1,0:T(8,128)(2,1)S(1)} %get-tuple-element.274), channel_id=1, source_target_pairs={{0,16},{1,17},{2,18},{3,19},{4,20},{5,21},{6,22},{7,23},{8,24},{9,... | collective-permute-start | bytes 196616 | tf_op jit(solution)/shard_map/cond/branch_1_fun/ppermute | solution.py:788
  258.7 6.9 %collective-permute-start.19 = (bf16[256,128]{1,0:T(8,128)(2,1)S(1)}, bf16[256,128]{1,0:T(8,128)(2,1)S(1)}, u32[]{:S(2)}, u32[]{:S(2)}) collective-permute-start(bf16[256,128]{1,0:T(8,128)(2,1)S(1)} %get-tuple-element.275), channel_id=1, source_target_pairs={{0,24},{1,25},{2,26},{3,27},{4,28},{5,29},{6,30},{7,31},{8,16},{9,... | collective-permute-start | bytes 196616 | tf_op jit(solution)/shard_map/cond/branch_1_fun/ppermute | solution.py:788
  261.2 5.0 %collective-permute-start.18 = (bf16[256,128]{1,0:T(8,128)(2,1)S(1)}, bf16[256,128]{1,0:T(8,128)(2,1)S(1)}, u32[]{:S(2)}, u32[]{:S(2)}) collective-permute-start(bf16[256,128]{1,0:T(8,128)(2,1)S(1)} %get-tuple-element.273), channel_id=1, source_target_pairs={{0,8},{1,9},{2,10},{3,11},{4,12},{5,13},{6,14},{7,15},{8,0},{9,1},... | collective-permute-start | bytes 196616 | tf_op jit(solution)/shard_map/cond/branch_1_fun/ppermute | solution.py:788
  266.2 7.5 %collective-permute-start.23 = (bf16[256,128]{1,0:T(8,128)(2,1)S(1)}, bf16[256,128]{1,0:T(8,128)(2,1)S(1)}, u32[]{:S(2)}, u32[]{:S(2)}) collective-permute-start(bf16[256,128]{1,0:T(8,128)(2,1)S(1)} %fusion.8), channel_id=1, source_target_pairs={{0,16},{1,17},{2,18},{3,19},{4,20},{5,21},{6,22},{7,23},{8,24},{9,... | collective-permute-start | bytes 196616 | tf_op jit(solution)/shard_map/cond/branch_1_fun/ppermute | solution.py:788
  268.6 6.3 %collective-permute-start.22 = (bf16[256,128]{1,0:T(8,128)(2,1)S(1)}, bf16[256,128]{1,0:T(8,128)(2,1)S(1)}, u32[]{:S(2)}, u32[]{:S(2)}) collective-permute-start(bf16[256,128]{1,0:T(8,128)(2,1)S(1)} %fusion.8), channel_id=1, source_target_pairs={{0,24},{1,25},{2,26},{3,27},{4,28},{5,29},{6,30},{7,31},{8,16},{9,... | collective-permute-start | bytes 196616 | tf_op jit(solution)/shard_map/cond/branch_1_fun/ppermute | solution.py:788
  269.6 6.4 %collective-permute-start.21 = (bf16[256,128]{1,0:T(8,128)(2,1)S(1)}, bf16[256,128]{1,0:T(8,128)(2,1)S(1)}, u32[]{:S(2)}, u32[]{:S(2)}) collective-permute-start(bf16[256,128]{1,0:T(8,128)(2,1)S(1)} %fusion.8), channel_id=1, source_target_pairs={{0,8},{1,9},{2,10},{3,11},{4,12},{5,13},{6,14},{7,15},{8,0},{9,1},... | collective-permute-start | bytes 196616 | tf_op jit(solution)/shard_map/cond/branch_1_fun/ppermute | solution.py:788
  276.2 15.3 %collective-permute-start.26 = (bf16[4,256,128]{2,1,0:T(8,128)(2,1)S(1)}, bf16[4,256,128]{2,1,0:T(8,128)(2,1)S(1)}, u32[]{:S(2)}, u32[]{:S(2)}) collective-permute-start(bf16[4,256,128]{2,1,0:T(8,128)(2,1)S(1)} %bitcast.74), channel_id=1, source_target_pairs={{0,6},{1,7},{2,4},{3,5},{4,2},{5,3},{6,0},{7,1},{8,14},{9,15},{10,... | collective-permute-start | bytes 786440 | tf_op jit(solution)/shard_map/cond/branch_1_fun/ppermute | solution.py:788
  278.1 17.5 %collective-permute-start.25 = (bf16[4,256,128]{2,1,0:T(8,128)(2,1)S(1)}, bf16[4,256,128]{2,1,0:T(8,128)(2,1)S(1)}, u32[]{:S(2)}, u32[]{:S(2)}) collective-permute-start(bf16[4,256,128]{2,1,0:T(8,128)(2,1)S(1)} %bitcast.75), channel_id=1, source_target_pairs={{0,4},{1,5},{2,6},{3,7},{4,0},{5,1},{6,2},{7,3},{8,12},{9,13},{10,... | collective-permute-start | bytes 786440 | tf_op jit(solution)/shard_map/cond/branch_1_fun/ppermute | solution.py:788
  279.8 15.9 %collective-permute-start.24 = (bf16[4,256,128]{2,1,0:T(8,128)(2,1)S(1)}, bf16[4,256,128]{2,1,0:T(8,128)(2,1)S(1)}, u32[]{:S(2)}, u32[]{:S(2)}) collective-permute-start(bf16[4,256,128]{2,1,0:T(8,128)(2,1)S(1)} %bitcast.76), channel_id=1, source_target_pairs={{0,2},{1,3},{2,0},{3,1},{4,6},{5,7},{6,4},{7,5},{8,10},{9,11},{10,... | collective-permute-start | bytes 786440 | tf_op jit(solution)/shard_map/cond/branch_1_fun/ppermute | solution.py:788
  297.4 3.0 collective-permute-start.27
  (36 other events, 438.7 us)
Sparse Core Ops, SparseCore 0:
  105.1 199.3 all-reduce.1

commit v2 on v1

--- a/solution.py
+++ b/solution.py
@@ -568,26 +568,29 @@
 
 
 def ffn_unfold_kernel(gate_in, up_in, down_in, gate_ref, up_ref, down_ref):
-    for source, target in ((gate_in, gate_ref), (up_in, up_ref), (down_in, down_ref)):
-        for u in range(source.shape[1]):
-            target[:, u * LANES : (u + 1) * LANES] = source[0, u].astype(f32)
+    tiles = gate_in.shape[1]
+    for t in range(tiles):
+        lanes = slice(t * LANES, (t + 1) * LANES)
+        gate_ref[:, lanes] = gate_in[0, t].astype(f32)
+        up_ref[:, lanes] = up_in[0, t].astype(f32)
+        down_ref[:, lanes] = down_in[t // (tiles // 2), t % (tiles // 2)].astype(f32)
 
 
 def ffn_unfold_call(sums, width, hidden):
     tiles = hidden // LANES
-    chunk = 2
-    steps = tiles // chunk
+    steps = 2
+    rows = width // steps
     sums = sums.reshape(2, tiles + tiles // 2, width, LANES)
-    block = (1, chunk, width, LANES)
+    block = (1, tiles, rows, LANES)
     return pl.pallas_call(
         ffn_unfold_kernel,
         grid=(steps,),
         in_specs=[
-            pl.BlockSpec(block, lambda i: (0, i, 0, 0)),
-            pl.BlockSpec(block, lambda i: (1, i, 0, 0)),
-            pl.BlockSpec(block, lambda i: (i // (steps // 2), steps + i % (steps // 2), 0, 0)),
+            pl.BlockSpec(block, lambda i: (0, 0, i, 0)),
+            pl.BlockSpec(block, lambda i: (1, 0, i, 0)),
+            pl.BlockSpec((2, tiles // 2, rows, LANES), lambda i: (0, 2, i, 0)),
         ],
-        out_specs=[pl.BlockSpec((width, chunk * LANES), lambda i: (0, i))] * 3,
+        out_specs=[pl.BlockSpec((rows, hidden), lambda i: (i, 0))] * 3,
         out_shape=[jax.ShapeDtypeStruct((width, hidden), f32)] * 3,
         compiler_params=params(60),
         name="ffn_unfold",
@@ -1541,7 +1544,7 @@
     g_out_ref, *refs,
 ):
     messages = refs[:count]
-    out_ref, g_ref, units = refs[count:]
+    core, out_ref, keep_ref, send_ref, g_ref, units = refs[count:]
     me = ids[0]
     seqs, width, rows = x_ref.shape
     for t in range(count):
@@ -1608,6 +1611,8 @@
     for t in range(square):
         put(g_ref, attn_place(square + KV_HEADS + t), width, g_out_ref[t])
     clear_rest(g_ref, 2 * square + KV_HEADS, width)
+    keep_ref[...] = g_ref[core[0]]
+    send_ref[...] = g_ref[1 - core[0]]
 
 
 def clear_rest(g_ref, places, width):
@@ -1619,23 +1624,26 @@
 
 
 def units_last_call(
-    ids, x, a, norm, w_query, w_key, w_value, cos, sin, d_mid, last_d_q, g_out, messages, parts
+    ids, x, a, norm, w_query, w_key, w_value, cos, sin, d_mid, last_d_q, g_out, messages, parts, core
 ):
     seqs, width, rows = x.shape
     count = len(messages)
     vmem = pl.BlockSpec(memory_space=pltpu.VMEM)
+    smem = pl.BlockSpec(memory_space=pltpu.SMEM)
     places = -(-(2 * -(-width // LANES) + KV_HEADS) // 2)
+    half = jax.ShapeDtypeStruct((half_rows(places, width, parts), LANES), bf16)
     return pl.pallas_call(
         functools.partial(units_last_kernel, count),
-        in_specs=[pl.BlockSpec(memory_space=pltpu.SMEM)] + [vmem] * (11 + count),
+        in_specs=[smem] + [vmem] * (11 + count) + [smem],
         out_shape=[
             jax.ShapeDtypeStruct((seqs, width, rows), bf16),
-            jax.ShapeDtypeStruct((2, half_rows(places, width, parts), LANES), bf16),
+            half,
+            half,
         ],
-        scratch_shapes=[pltpu.VMEM((count + 1, rows * 5 // 2, LANES), bf16)],
+        scratch_shapes=[pltpu.VMEM((2,) + half.shape, bf16), pltpu.VMEM((count + 1, rows * 5 // 2, LANES), bf16)],
         compiler_params=params(60),
         name="last_part",
-    )(ids, x, a, norm, w_query, w_key, w_value, cos, sin, d_mid, last_d_q, g_out, *messages)
+    )(ids, x, a, norm, w_query, w_key, w_value, cos, sin, d_mid, last_d_q, g_out, *messages, core)
 
 
 def to_all(messages):
@@ -1745,11 +1753,12 @@
         d_all = units_backward_call(
             ids, to_all(d_messages), q, kv, attn_out, log_total, last_d_kv
         )
-        d_tokens, g_attn = units_last_call(
+        core = (lax.axis_index("batch") & 1).astype(jnp.int32).reshape(1)
+        d_tokens, keep, send = units_last_call(
             ids, x, a, norm_one, w_query, wk_turned, wv_turned, cos, sin, d_mid, last_d_q, g_out,
-            to_all(d_all), devices,
+            to_all(d_all), devices, core,
         )
-        return (block_out, d_tokens) + sum_over(g_attn)
+        return (block_out, d_tokens) + sum_over(add_low(keep, swap_with(send, 1, devices)), 1)
 
     block_out, d_tokens, *attn_sums = in_one_piece(
         places_ok,
@@ -1795,8 +1804,8 @@
     wk_turned, wv_turned, w_down_turned = w_key.T, w_value.T, w_down.T
     cos, sin = rope_tables(positions)
     norm_one, norm_two = norm_attn, norm_mlp
-    def sum_over(value):
-        for stage, place in zip(stages, places):
+    def sum_over(value, done=0):
+        for stage, place in zip(stages[done:], places[done:]):
             value = scatter_stage(value, stage, place, devices)
         return gather_sums(value, stages, places, devices, 1)
 

time: 324 us -> 322 us (level)
  transfers between devices with their start and end apart: 46 -> 46, of which waited for: 31 -> 33; matrix products, arithmetic and copies ran while one was open for 2% -> 2% of each run, Pallas kernels for 25% -> 25%
where the time goes in v2:
time: 322 us; the launch traced here: 318 us
  Pallas kernels  110 us (34%)
  starting transfers between devices  96.1 us (30%)
  waiting for transfers between devices  83.8 us (26%)
  between operations  15.3 us (5%)
  other arithmetic  6.48 us (2%)
  local copies, waits for them, and re-layouts  6.11 us (2%)
    ppermute x28, starting transfers between devices, to_all(): lax.ppermute(messages[t], 'seq', [(i, (i + t) % count) for i in range(cou...  56.7 us
    ppermute x14, waiting for transfers between devices, swap_with(): lax.ppermute(value, ('seq', 'batch'), [(i, i ^ mask) for i in range(devic...  46.1 us
    ppermute x28, waiting for transfers between devices, to_all(): lax.ppermute(messages[t], 'seq', [(i, (i + t) % count) for i in range(cou...  30.6 us
    ppermute x14, starting transfers between devices, swap_with(): lax.ppermute(value, ('seq', 'batch'), [(i, i ^ mask) for i in range(devic...  26.3 us
    pallas_call x1, Pallas kernels, units_backward_call(): pl.pallas_call(functools.partial(units_backward_kernel, count), in_specs=...  25.1 us
    pallas_call x1, Pallas kernels, units_ffn_call(): pl.pallas_call(functools.partial(units_ffn_kernel, count), in_specs=[pl.B...  15.8 us
    ppermute x3, starting transfers between devices, units_layer(): lax.ppermute(part, 'seq', [(i, i ^ mask) for i in range(count)])  13.1 us
    pallas_call x1, Pallas kernels, units_forward_call(): pl.pallas_call(functools.partial(units_forward_kernel, count), in_specs=[...  13 us
  transfers between devices with their start and end apart: 46, of which 33 were waited for; matrix products, arithmetic and copies ran while one was open for 2% of the time, Pallas kernels for 25%

profile of v2, /device:TPU:0, one launch (start us, length us, event | category | flops | bytes accessed | tf_op | source)
XLA Modules:
  0.0 317.8 jit_solution(7016517372554117223)
XLA Ops:
  9.4 7.0 %project.1 = (bf16[640,128]{1,0:T(8,128)(2,1)}, bf16[640,128]{1,0:T(8,128)(2,1)}, bf16[640,128]{1,0:T(8,128)(2,1)}, bf16[640,128]{1,0:T(8,128)(2,1)}, bf16[640,1...) custom-call(s32[1]{0:T(128)} %bitcast.30.ids, ...), custom_call_target="tpu_custom_call" | custom-call | tf_op jit(solution)/shard_map/project/pallas_call | solution.py:1025
  16.4 3.0 collective-permute-start.28
  19.4 1.6 collective-permute-start.29
  21.0 1.5 collective-permute-start.35
  25.3 2.8 collective-permute-done.35
  28.1 3.4 %collective-permute-start.32 = (bf16[640,128]{1,0:T(8,128)(2,1)}, bf16[640,128]{1,0:T(8,128)(2,1)S(1)}, u32[]{:S(2)}, u32[]{:S(2)}) collective-permute-start(bf16[640,128]{1,0:T(8,128)(2,1)} %get-tuple-element.221), channel_id=1, source_target_pairs={{0,20},{4,24},{8,28},{12,0},{16,4},{20,8},{24,12},{28,16},{1,21},{... | collective-permute-start | bytes 491528 | tf_op jit(solution)/shard_map/ppermute | solution.py:1652
  34.1 7.0 %collective-permute-done.30.refs_3_ = bf16[640,128]{1,0:T(8,128)(2,1)S(1)} collective-permute-done((bf16[640,128]{1,0:T(8,128)(2,1)}, bf16[640,128]{1,0:T(8,128)(2,1)S(1)}, u32[]{:S(2)}, u32[]{:S(2)}) %collective-permute-start.30) | collective-permute-done | bytes 163872 | tf_op jit(solution)/shard_map/ppermute | solution.py:1652
  42.2 8.6 %collective-permute-start.43 = (bf16[2,256,128]{2,1,0:T(8,128)(2,1)S(1)}, bf16[2,256,128]{2,1,0:T(8,128)(2,1)S(1)}, u32[]{:S(2)}, u32[]{:S(2)}) collective-permute-start(bf16[2,256,128]{2,1,0:T(8,128)(2,1)S(1)} %pad_maximum_fusion.3), channel_id=1, source_target_pairs={{0,8},{4,12},{8,0},{12,4},{16,24},{20,28},{24,16},{28,20},{1,9},{5... | collective-permute-start | bytes 393224 | tf_op jit(solution)/shard_map/ppermute | solution.py:1731
  50.7 2.9 collective-permute-done.43
  53.7 3.0 collective-permute-start.44
  57.6 13.0 %units_forward.1 = (bf16[384,128]{1,0:T(8,128)(2,1)S(1)}, bf16[384,128]{1,0:T(8,128)(2,1)S(1)}, bf16[384,128]{1,0:T(8,128)(2,1)S(1)}, bf16[384,128]{1,0:T(8,128)...) custom-call(s32[1]{0:T(128)} %bitcast.30.ids, ...), custom_call_target="tpu_custom_call" | custom-call | tf_op jit(solution)/shard_map/units_forward/pallas_call | solution.py:1100
  70.7 3.3 %collective-permute-start.36 = (bf16[384,128]{1,0:T(8,128)(2,1)S(1)}, bf16[384,128]{1,0:T(8,128)(2,1)S(1)}, u32[]{:S(2)}, u32[]{:S(2)}) collective-permute-start(bf16[384,128]{1,0:T(8,128)(2,1)S(1)} %get-tuple-element.234), channel_id=1, source_target_pairs={{0,4},{4,8},{8,12},{12,16},{16,20},{20,24},{24,28},{28,0},{1,5},{5... | collective-permute-start | bytes 294920 | tf_op jit(solution)/shard_map/ppermute | solution.py:1652
  74.9 3.0 collective-permute-start.39
  82.4 2.9 last_unit_forward.1
  89.0 15.8 %feed_forward.1 = (f32[3,256,576]{2,1,0:T(8,128)S(1)}, bf16[3,256,576]{2,1,0:T(8,128)(2,1)}, bf16[768,1536]{1,0:T(8,128)(2,1)}, bf16[768,1536]{1,0:T(8,128)(2,1)...) custom-call(s32[1]{0:T(128)} %bitcast.30.ids, bf16[3,576,256]{2,1,0:T(8,128)(2,1)S(1)} %bitcast.57, ...), custom_call_target="tpu_custom_call" | custom-call | tf_op jit(solution)/shard_map/feed_forward/pallas_call | solution.py:1362
  107.0 192.4 %conditional.1 = (bf16[3,576,256]{2,1,0:T(8,128)(2,1)}, bf16[3,576,256]{2,1,0:T(8,128)(2,1)}, bf16[4096,128]{1,0:T(8,128)(2,1)}, bf16[4096,128]{1,0:T(8,128)(2,1)}) conditional(s32[]{:T(128)} %bitcast.29, () %tuple.17, (s32[1]{0:T(128)}, f32[3,256,576]{2,1,0:T(8,128)S(1)}, bf16[3,576,256]{2,1,0:T(8,128)(2,1)}, bf16[768,1536]{1,0:T(8,128)(2,1)}, ...), branch_computations={%region_0.1_spmd, %region_1.2_spmd} | conditional | flops 6684723 | bytes 50530336 | solution.py:1777
  107.0 12.6 %feed_back.1 = (f32[3,256,576]{2,1,0:T(8,128)}, bf16[1,384,128]{2,1,0:T(8,128)(2,1)}, f32[1,576]{1,0:T(1,128)}, bf16[384,128]{1,0:T(8,128)(2,1)}, bf16[384,128]{...) custom-call(s32[1]{0:T(128)} %get-tuple-element.91.ids, ...), custom_call_target="tpu_custom_call" | custom-call | tf_op jit(solution)/shard_map/cond/branch_1_fun/feed_back/pallas_call | solution.py:1464
  119.6 2.8 collective-permute-start
  122.4 3.5 %collective-permute-start.1 = (bf16[384,128]{1,0:T(8,128)(2,1)}, bf16[384,128]{1,0:T(8,128)(2,1)S(1)}, u32[]{:S(2)}, u32[]{:S(2)}) collective-permute-start(bf16[384,128]{1,0:T(8,128)(2,1)} %get-tuple-element.120), channel_id=1, source_target_pairs={{0,8},{4,12},{8,16},{12,20},{16,24},{20,28},{24,0},{28,4},{1,9},{5... | collective-permute-start | bytes 294920 | tf_op jit(solution)/shard_map/cond/branch_1_fun/ppermute | solution.py:1652
  126.2 2.0 collective-permute-start.3
  128.2 2.8 collective-permute-start.4
  133.0 3.3 %collective-permute-start.6 = (bf16[384,128]{1,0:T(8,128)(2,1)}, bf16[384,128]{1,0:T(8,128)(2,1)S(1)}, u32[]{:S(2)}, u32[]{:S(2)}) collective-permute-start(bf16[384,128]{1,0:T(8,128)(2,1)} %get-tuple-element.125), channel_id=1, source_target_pairs={{0,28},{4,0},{8,4},{12,8},{16,12},{20,16},{24,20},{28,24},{1,29},{... | collective-permute-start | bytes 294920 | tf_op jit(solution)/shard_map/cond/branch_1_fun/ppermute | solution.py:1652
  137.3 5.9 %last_unit_backward.1 = (bf16[8,256,128]{2,1,0:T(8,128)(2,1)S(1)}, f32[768,128]{1,0:T(8,128)S(1)}) custom-call(s32[1]{0:T(128)} %get-tuple-element.91.ids, bf16[768,128]{1,0:T(8,128)(2,1)} %get-tuple-element.111.q_ref, bf16[8,256,128]{2,1,0:T(8,128)(2,1)S(1)} %copy-done.8, bf16[384,128]{1,0:T(8,128)(2,1)S(1)} %bitcast.55, bf16[384,128]{1,0:T(8,128)(2,1)} %bitcast.78, ...), custom_call_target="tpu_custom_call" | custom-call | tf_op jit(solution)/shard_map/cond/branch_1_fun/last_unit_backward/pallas_call | solution.py:1189
  145.2 2.4 collective-permute-done.6.refs_7_
  148.2 25.1 %units_backward.1 = (bf16[896,128]{1,0:T(8,128)(2,1)}, bf16[896,128]{1,0:T(8,128)(2,1)}, bf16[896,128]{1,0:T(8,128)(2,1)}, bf16[896,128]{1,0:T(8,128)(2,1)}, bf1...) custom-call(s32[1]{0:T(128)} %get-tuple-element.91.ids, ...), custom_call_target="tpu_custom_call" | custom-call | tf_op jit(solution)/shard_map/cond/branch_1_fun/units_backward/pallas_call | solution.py:1247
  174.0 7.7 %collective-permute-start.8 = (bf16[896,128]{1,0:T(8,128)(2,1)}, bf16[896,128]{1,0:T(8,128)(2,1)}, u32[]{:S(2)}, u32[]{:S(2)}) collective-permute-start(bf16[896,128]{1,0:T(8,128)(2,1)} %get-tuple-element.140), channel_id=1, source_target_pairs={{0,8},{4,12},{8,16},{12,20},{16,24},{20,28},{24,0},{28,4},{1,9},{5... | collective-permute-start | bytes 688136 | tf_op jit(solution)/shard_map/cond/branch_1_fun/ppermute | solution.py:1652
  183.3 3.3 %collective-permute-start.11 = (bf16[896,128]{1,0:T(8,128)(2,1)}, bf16[896,128]{1,0:T(8,128)(2,1)}, u32[]{:S(2)}, u32[]{:S(2)}) collective-permute-start(bf16[896,128]{1,0:T(8,128)(2,1)} %get-tuple-element.143), channel_id=1, source_target_pairs={{0,20},{4,24},{8,28},{12,0},{16,4},{20,8},{24,12},{28,16},{1,21},{... | collective-permute-start | bytes 688136 | tf_op jit(solution)/shard_map/cond/branch_1_fun/ppermute | solution.py:1652
  186.6 2.1 collective-permute-done.7.refs_1_
  188.9 5.7 %collective-permute-start.13 = (bf16[896,128]{1,0:T(8,128)(2,1)}, bf16[896,128]{1,0:T(8,128)(2,1)}, u32[]{:S(2)}, u32[]{:S(2)}) collective-permute-start(bf16[896,128]{1,0:T(8,128)(2,1)} %get-tuple-element.145), channel_id=1, source_target_pairs={{0,28},{4,0},{8,4},{12,8},{16,12},{20,16},{24,20},{28,24},{1,29},{... | collective-permute-start | bytes 688136 | tf_op jit(solution)/shard_map/cond/branch_1_fun/ppermute | solution.py:1652
  194.6 7.4 %feed_out.1 = (bf16[3,576,256]{2,1,0:T(8,128)(2,1)}, bf16[5,576,128]{2,1,0:T(8,128)(2,1)}) custom-call(f32[3,256,576]{2,1,0:T(8,128)S(1)} %get-tuple-element.88.mid_ref, bf16[3,256,576]{2,1,0:T(8,128)(2,1)} %get-tuple-element.89.attn_ref, bf16[768,1536]{1,0:T(8,128)(2,1)} %get-tuple-element.90.hid_ref, f32[3,256,576]{2,1,0:T(8,128)} %get-tuple-element.99.d_mid_ref, ...), custom_call_target="tpu_custom_call" | custom-call | tf_op jit(solution)/shard_map/cond/branch_1_fun/feed_out/pallas_call | solution.py:1520
  202.0 6.9 %collective-permute-done.9.refs_3_ = bf16[896,128]{1,0:T(8,128)(2,1)} collective-permute-done((bf16[896,128]{1,0:T(8,128)(2,1)}, bf16[896,128]{1,0:T(8,128)(2,1)}, u32[]{:S(2)}, u32[]{:S(2)}) %collective-permute-start.9) | collective-permute-done | bytes 229408 | tf_op jit(solution)/shard_map/cond/branch_1_fun/ppermute | solution.py:1652
  210.7 2.6 collective-permute-done.13.refs_7_
  213.3 9.9 %last_part.1 = (bf16[3,576,256]{2,1,0:T(8,128)(2,1)}, bf16[4096,128]{1,0:T(8,128)(2,1)}, bf16[4096,128]{1,0:T(8,128)(2,1)}) custom-call(s32[1]{0:T(128)} %get-tuple-element.91.ids, bf16[3,576,256]{2,1,0:T(8,128)(2,1)S(1)} %get-tuple-element.103.x_ref, bf16[3,256,576]{2,1,0:T(8,128)(2,1)} %get-tuple-element.104.a_ref, f32[576]{0:T(1024)S(1)} %get-tuple-element.105.norm_ref, ...), custom_call_target="tpu_custom_call" | custom-call | tf_op jit(solution)/shard_map/cond/branch_1_fun/last_part/pallas_call | solution.py:1635
  223.1 2.9 collective-permute-done.14
  227.6 3.6 %collective-permute-start.17 = (bf16[1024,128]{1,0:T(8,128)(2,1)S(1)}, bf16[1024,128]{1,0:T(8,128)(2,1)S(1)}, u32[]{:S(2)}, u32[]{:S(2)}) collective-permute-start(bf16[1024,128]{1,0:T(8,128)(2,1)S(1)} %get-tuple-element.269), channel_id=1, source_target_pairs={{0,6},{1,7},{2,4},{3,5},{4,2},{5,3},{6,0},{7,1},{8,14},{9,15},{10,... | collective-permute-start | bytes 786440 | tf_op jit(solution)/shard_map/cond/branch_1_fun/ppermute | solution.py:791
  231.8 6.5 %collective-permute-done.17 = bf16[1024,128]{1,0:T(8,128)(2,1)S(1)} collective-permute-done((bf16[1024,128]{1,0:T(8,128)(2,1)S(1)}, bf16[1024,128]{1,0:T(8,128)(2,1)S(1)}, u32[]{:S(2)}, u32[]{:S(2)}) %collective-permute-start.17) | collective-permute-done | bytes 262176 | tf_op jit(solution)/shard_map/cond/branch_1_fun/ppermute | solution.py:791
  238.3 6.3 %collective-permute-done.16 = bf16[1024,128]{1,0:T(8,128)(2,1)S(1)} collective-permute-done((bf16[1024,128]{1,0:T(8,128)(2,1)S(1)}, bf16[1024,128]{1,0:T(8,128)(2,1)S(1)}, u32[]{:S(2)}, u32[]{:S(2)}) %collective-permute-start.16) | collective-permute-done | bytes 262176 | tf_op jit(solution)/shard_map/cond/branch_1_fun/ppermute | solution.py:791
  244.8 12.4 %collective-permute-start.20 = (bf16[256,128]{1,0:T(8,128)(2,1)S(1)}, bf16[256,128]{1,0:T(8,128)(2,1)S(1)}, u32[]{:S(2)}, u32[]{:S(2)}) collective-permute-start(bf16[256,128]{1,0:T(8,128)(2,1)S(1)} %get-tuple-element.272), channel_id=1, source_target_pairs={{0,16},{1,17},{2,18},{3,19},{4,20},{5,21},{6,22},{7,23},{8,24},{9,... | collective-permute-start | bytes 196616 | tf_op jit(solution)/shard_map/cond/branch_1_fun/ppermute | solution.py:791
  257.3 2.5 collective-permute-start.19
  259.8 3.8 %collective-permute-done.20 = bf16[256,128]{1,0:T(8,128)(2,1)S(1)} collective-permute-done((bf16[256,128]{1,0:T(8,128)(2,1)S(1)}, bf16[256,128]{1,0:T(8,128)(2,1)S(1)}, u32[]{:S(2)}, u32[]{:S(2)}) %collective-permute-start.20) | collective-permute-done | bytes 65568 | tf_op jit(solution)/shard_map/cond/branch_1_fun/ppermute | solution.py:791
  264.7 2.5 collective-permute-start.23
  268.3 4.0 %collective-permute-done.23 = bf16[256,128]{1,0:T(8,128)(2,1)S(1)} collective-permute-done((bf16[256,128]{1,0:T(8,128)(2,1)S(1)}, bf16[256,128]{1,0:T(8,128)(2,1)S(1)}, u32[]{:S(2)}, u32[]{:S(2)}) %collective-permute-start.23) | collective-permute-done | bytes 65568 | tf_op jit(solution)/shard_map/cond/branch_1_fun/ppermute | solution.py:791
  274.5 1.7 collective-permute-start.26
  278.1 12.1 %collective-permute-done.26 = bf16[4,256,128]{2,1,0:T(8,128)(2,1)S(1)} collective-permute-done((bf16[4,256,128]{2,1,0:T(8,128)(2,1)S(1)}, bf16[4,256,128]{2,1,0:T(8,128)(2,1)S(1)}, u32[]{:S(2)}, u32[]{:S(2)}) %collective-permute-start.26) | collective-permute-done | bytes 262176 | tf_op jit(solution)/shard_map/cond/branch_1_fun/ppermute | solution.py:791
  290.2 4.2 %collective-permute-done.25 = bf16[4,256,128]{2,1,0:T(8,128)(2,1)S(1)} collective-permute-done((bf16[4,256,128]{2,1,0:T(8,128)(2,1)S(1)}, bf16[4,256,128]{2,1,0:T(8,128)(2,1)S(1)}, u32[]{:S(2)}, u32[]{:S(2)}) %collective-permute-start.25) | collective-permute-done | bytes 262176 | tf_op jit(solution)/shard_map/cond/branch_1_fun/ppermute | solution.py:791
  296.1 3.0 collective-permute-done.27
  299.3 3.9 %attn_unfold.1 = (f32[576,576]{1,0:T(8,128)}, f32[192,576]{1,0:T(8,128)}, f32[192,576]{1,0:T(8,128)}, f32[576]{0:T(1024)}, f32[576,576]{1,0:T(8,128)}, /*index=5*/f32[576]{0:T(1024)}) custom-call(s32[1]{0:T(128)} %bitcast.39.side, bf16[4096,128]{1,0:T(8,128)(2,1)} %get-tuple-element.256.mine, bf16[4096,128]{1,0:T(8,128)(2,1)} %get-tuple-element.257.other), custom_call_target="tpu_custom_call" | custom-call | tf_op jit(solution)/shard_map/attn_unfold/pallas_call | solution.py:612
  304.5 6.2 %ffn_unfold.1 = (f32[576,1536]{1,0:T(8,128)}, f32[576,1536]{1,0:T(8,128)}, f32[576,1536]{1,0:T(8,128)}) custom-call(bf16[2,18,576,128]{3,2,1,0:T(8,128)(2,1)} %all-reduce.2.cloned.1.call-done.gate_in.up_in.down_in, bf16[2,18,576,128]{3,2,1,0:T(8,128)(2,1)} %all-reduce.2.cloned.1.call-done.gate_in.up_in.down_in, ...), custom_call_target="tpu_custom_call" | custom-call | tf_op jit(solution)/shard_map/ffn_unfold/pallas_call | solution.py:585
  (151 shorter events, 41.7 us)
Async XLA Ops:
  7.2 297.3 %all-reduce.2.cloned.1.call-start = ((), (), s32[]{:S(2)}) async-start(), calls=%async_computation | async-start | bytes 10616832 | tf_op jit(solution)/shard_map/psum | solution.py:1743
  9.4 79.6 %copy-start.4 = (bf16[256,3,576]{0,2,1:T(8,128)(2,1)S(1)}, bf16[256,3,576]{0,2,1:T(8,128)(2,1)}, u32[]{:S(2)}) copy-start(bf16[256,3,576]{0,2,1:T(8,128)(2,1)} %param.14) | copy-start | bytes 2654212
  16.4 72.6 %copy-start.35 = (f32[576]{0:T(1024)S(1)}, f32[576]{0:T(1024)}, u32[]{:S(2)}) copy-start(f32[576]{0:T(1024)} %norm_ref.3) | copy-start | bytes 6916
  16.4 15.1 %collective-permute-start.28 = (bf16[640,128]{1,0:T(8,128)(2,1)}, bf16[640,128]{1,0:T(8,128)(2,1)S(1)}, u32[]{:S(2)}, u32[]{:S(2)}) collective-permute-start(bf16[640,128]{1,0:T(8,128)(2,1)} %get-tuple-element.217), channel_id=1, source_target_pairs={{0,4},{4,8},{8,12},{12,16},{16,20},{20,24},{24,28},{28,0},{1,5},{5... | collective-permute-start | bytes 491528 | tf_op jit(solution)/shard_map/ppermute | solution.py:1652
  19.4 13.6 %collective-permute-start.29 = (bf16[640,128]{1,0:T(8,128)(2,1)}, bf16[640,128]{1,0:T(8,128)(2,1)S(1)}, u32[]{:S(2)}, u32[]{:S(2)}) collective-permute-start(bf16[640,128]{1,0:T(8,128)(2,1)} %get-tuple-element.218), channel_id=1, source_target_pairs={{0,8},{4,12},{8,16},{12,20},{16,24},{20,28},{24,0},{28,4},{1,9},{5... | collective-permute-start | bytes 491528 | tf_op jit(solution)/shard_map/ppermute | solution.py:1652
  21.0 7.1 %collective-permute-start.35 = (bf16[1,256,128]{2,1,0:T(8,128)(2,1)}, bf16[1,256,128]{2,1,0:T(8,128)(2,1)S(1)}, u32[]{:S(2)}, u32[]{:S(2)}) collective-permute-start(bf16[1,256,128]{2,1,0:T(8,128)(2,1)} %get-tuple-element.224), channel_id=1, source_target_pairs={{0,4},{4,0},{8,12},{12,8},{16,20},{20,16},{24,28},{28,24},{1,5},{5... | collective-permute-start | bytes 196616 | tf_op jit(solution)/shard_map/ppermute | solution.py:1731
  22.6 18.6 %collective-permute-start.30 = (bf16[640,128]{1,0:T(8,128)(2,1)}, bf16[640,128]{1,0:T(8,128)(2,1)S(1)}, u32[]{:S(2)}, u32[]{:S(2)}) collective-permute-start(bf16[640,128]{1,0:T(8,128)(2,1)} %get-tuple-element.219), channel_id=1, source_target_pairs={{0,12},{4,16},{8,20},{12,24},{16,28},{20,0},{24,4},{28,8},{1,13},{... | collective-permute-start | bytes 491528 | tf_op jit(solution)/shard_map/ppermute | solution.py:1652
  24.0 17.4 %collective-permute-start.31 = (bf16[640,128]{1,0:T(8,128)(2,1)}, bf16[640,128]{1,0:T(8,128)(2,1)S(1)}, u32[]{:S(2)}, u32[]{:S(2)}) collective-permute-start(bf16[640,128]{1,0:T(8,128)(2,1)} %get-tuple-element.220), channel_id=1, source_target_pairs={{0,16},{4,20},{8,24},{12,28},{16,0},{20,4},{24,8},{28,12},{1,17},{... | collective-permute-start | bytes 491528 | tf_op jit(solution)/shard_map/ppermute | solution.py:1652
  28.1 13.3 %collective-permute-start.32 = (bf16[640,128]{1,0:T(8,128)(2,1)}, bf16[640,128]{1,0:T(8,128)(2,1)S(1)}, u32[]{:S(2)}, u32[]{:S(2)}) collective-permute-start(bf16[640,128]{1,0:T(8,128)(2,1)} %get-tuple-element.221), channel_id=1, source_target_pairs={{0,20},{4,24},{8,28},{12,0},{16,4},{20,8},{24,12},{28,16},{1,21},{... | collective-permute-start | bytes 491528 | tf_op jit(solution)/shard_map/ppermute | solution.py:1652
  31.5 9.9 %collective-permute-start.33 = (bf16[640,128]{1,0:T(8,128)(2,1)}, bf16[640,128]{1,0:T(8,128)(2,1)S(1)}, u32[]{:S(2)}, u32[]{:S(2)}) collective-permute-start(bf16[640,128]{1,0:T(8,128)(2,1)} %get-tuple-element.222), channel_id=1, source_target_pairs={{0,24},{4,28},{8,0},{12,4},{16,8},{20,12},{24,16},{28,20},{1,25},{... | collective-permute-start | bytes 491528 | tf_op jit(solution)/shard_map/ppermute | solution.py:1652
  33.0 9.1 %collective-permute-start.34 = (bf16[640,128]{1,0:T(8,128)(2,1)}, bf16[640,128]{1,0:T(8,128)(2,1)S(1)}, u32[]{:S(2)}, u32[]{:S(2)}) collective-permute-start(bf16[640,128]{1,0:T(8,128)(2,1)} %get-tuple-element.223), channel_id=1, source_target_pairs={{0,28},{4,0},{8,4},{12,8},{16,12},{20,16},{24,20},{28,24},{1,29},{... | collective-permute-start | bytes 491528 | tf_op jit(solution)/shard_map/ppermute | solution.py:1652
  42.2 11.5 %collective-permute-start.43 = (bf16[2,256,128]{2,1,0:T(8,128)(2,1)S(1)}, bf16[2,256,128]{2,1,0:T(8,128)(2,1)S(1)}, u32[]{:S(2)}, u32[]{:S(2)}) collective-permute-start(bf16[2,256,128]{2,1,0:T(8,128)(2,1)S(1)} %pad_maximum_fusion.3), channel_id=1, source_target_pairs={{0,8},{4,12},{8,0},{12,4},{16,24},{20,28},{24,16},{28,20},{1,9},{5... | collective-permute-start | bytes 393224 | tf_op jit(solution)/shard_map/ppermute | solution.py:1731
  53.7 28.1 %collective-permute-start.44 = (bf16[4,256,128]{2,1,0:T(8,128)(2,1)S(1)}, bf16[4,256,128]{2,1,0:T(8,128)(2,1)S(1)}, u32[]{:S(2)}, u32[]{:S(2)}) collective-permute-start(bf16[4,256,128]{2,1,0:T(8,128)(2,1)S(1)} %pad_maximum_fusion.2), channel_id=1, source_target_pairs={{0,24},{4,28},{8,16},{12,20},{16,8},{20,12},{24,0},{28,4},{1,25},{... | collective-permute-start | bytes 786440 | tf_op jit(solution)/shard_map/ppermute | solution.py:1731
  70.7 8.3 %collective-permute-start.36 = (bf16[384,128]{1,0:T(8,128)(2,1)S(1)}, bf16[384,128]{1,0:T(8,128)(2,1)S(1)}, u32[]{:S(2)}, u32[]{:S(2)}) collective-permute-start(bf16[384,128]{1,0:T(8,128)(2,1)S(1)} %get-tuple-element.234), channel_id=1, source_target_pairs={{0,4},{4,8},{8,12},{12,16},{16,20},{20,24},{24,28},{28,0},{1,5},{5... | collective-permute-start | bytes 294920 | tf_op jit(solution)/shard_map/ppermute | solution.py:1652
  74.0 6.8 %collective-permute-start.37 = (bf16[384,128]{1,0:T(8,128)(2,1)S(1)}, bf16[384,128]{1,0:T(8,128)(2,1)S(1)}, u32[]{:S(2)}, u32[]{:S(2)}) collective-permute-start(bf16[384,128]{1,0:T(8,128)(2,1)S(1)} %get-tuple-element.235), channel_id=1, source_target_pairs={{0,8},{4,12},{8,16},{12,20},{16,24},{20,28},{24,0},{28,4},{1,9},{5... | collective-permute-start | bytes 294920 | tf_op jit(solution)/shard_map/ppermute | solution.py:1652
  74.0 11.7 %collective-permute-start.38 = (bf16[384,128]{1,0:T(8,128)(2,1)S(1)}, bf16[384,128]{1,0:T(8,128)(2,1)S(1)}, u32[]{:S(2)}, u32[]{:S(2)}) collective-permute-start(bf16[384,128]{1,0:T(8,128)(2,1)S(1)} %get-tuple-element.236), channel_id=1, source_target_pairs={{0,12},{4,16},{8,20},{12,24},{16,28},{20,0},{24,4},{28,8},{1,13},{... | collective-permute-start | bytes 294920 | tf_op jit(solution)/shard_map/ppermute | solution.py:1652
  74.9 11.9 %collective-permute-start.39 = (bf16[384,128]{1,0:T(8,128)(2,1)S(1)}, bf16[384,128]{1,0:T(8,128)(2,1)S(1)}, u32[]{:S(2)}, u32[]{:S(2)}) collective-permute-start(bf16[384,128]{1,0:T(8,128)(2,1)S(1)} %get-tuple-element.237), channel_id=1, source_target_pairs={{0,16},{4,20},{8,24},{12,28},{16,0},{20,4},{24,8},{28,12},{1,17},{... | collective-permute-start | bytes 294920 | tf_op jit(solution)/shard_map/ppermute | solution.py:1652
  78.9 7.9 %collective-permute-start.40 = (bf16[384,128]{1,0:T(8,128)(2,1)S(1)}, bf16[384,128]{1,0:T(8,128)(2,1)S(1)}, u32[]{:S(2)}, u32[]{:S(2)}) collective-permute-start(bf16[384,128]{1,0:T(8,128)(2,1)S(1)} %get-tuple-element.238), channel_id=1, source_target_pairs={{0,20},{4,24},{8,28},{12,0},{16,4},{20,8},{24,12},{28,16},{1,21},{... | collective-permute-start | bytes 294920 | tf_op jit(solution)/shard_map/ppermute | solution.py:1652
  80.8 7.5 %collective-permute-start.41 = (bf16[384,128]{1,0:T(8,128)(2,1)S(1)}, bf16[384,128]{1,0:T(8,128)(2,1)S(1)}, u32[]{:S(2)}, u32[]{:S(2)}) collective-permute-start(bf16[384,128]{1,0:T(8,128)(2,1)S(1)} %get-tuple-element.239), channel_id=1, source_target_pairs={{0,24},{4,28},{8,0},{12,4},{16,8},{20,12},{24,16},{28,20},{1,25},{... | collective-permute-start | bytes 294920 | tf_op jit(solution)/shard_map/ppermute | solution.py:1652
  81.8 6.5 %collective-permute-start.42 = (bf16[384,128]{1,0:T(8,128)(2,1)S(1)}, bf16[384,128]{1,0:T(8,128)(2,1)S(1)}, u32[]{:S(2)}, u32[]{:S(2)}) collective-permute-start(bf16[384,128]{1,0:T(8,128)(2,1)S(1)} %get-tuple-element.240), channel_id=1, source_target_pairs={{0,28},{4,0},{8,4},{12,8},{16,12},{20,16},{24,20},{28,24},{1,29},{... | collective-permute-start | bytes 294920 | tf_op jit(solution)/shard_map/ppermute | solution.py:1652
  119.6 12.7 %collective-permute-start = (bf16[384,128]{1,0:T(8,128)(2,1)}, bf16[384,128]{1,0:T(8,128)(2,1)S(1)}, u32[]{:S(2)}, u32[]{:S(2)}) collective-permute-start(bf16[384,128]{1,0:T(8,128)(2,1)} %get-tuple-element.119), channel_id=1, source_target_pairs={{0,4},{4,8},{8,12},{12,16},{16,20},{20,24},{24,28},{28,0},{1,5},{5... | collective-permute-start | bytes 294920 | tf_op jit(solution)/shard_map/cond/branch_1_fun/ppermute | solution.py:1652
  122.4 10.6 %collective-permute-start.1 = (bf16[384,128]{1,0:T(8,128)(2,1)}, bf16[384,128]{1,0:T(8,128)(2,1)S(1)}, u32[]{:S(2)}, u32[]{:S(2)}) collective-permute-start(bf16[384,128]{1,0:T(8,128)(2,1)} %get-tuple-element.120), channel_id=1, source_target_pairs={{0,8},{4,12},{8,16},{12,20},{16,24},{20,28},{24,0},{28,4},{1,9},{5... | collective-permute-start | bytes 294920 | tf_op jit(solution)/shard_map/cond/branch_1_fun/ppermute | solution.py:1652
  125.9 18.7 %collective-permute-start.2 = (bf16[384,128]{1,0:T(8,128)(2,1)}, bf16[384,128]{1,0:T(8,128)(2,1)S(1)}, u32[]{:S(2)}, u32[]{:S(2)}) collective-permute-start(bf16[384,128]{1,0:T(8,128)(2,1)} %get-tuple-element.121), channel_id=1, source_target_pairs={{0,12},{4,16},{8,20},{12,24},{16,28},{20,0},{24,4},{28,8},{1,13},{... | collective-permute-start | bytes 294920 | tf_op jit(solution)/shard_map/cond/branch_1_fun/ppermute | solution.py:1652
  126.2 18.4 %collective-permute-start.3 = (bf16[384,128]{1,0:T(8,128)(2,1)}, bf16[384,128]{1,0:T(8,128)(2,1)S(1)}, u32[]{:S(2)}, u32[]{:S(2)}) collective-permute-start(bf16[384,128]{1,0:T(8,128)(2,1)} %get-tuple-element.122), channel_id=1, source_target_pairs={{0,16},{4,20},{8,24},{12,28},{16,0},{20,4},{24,8},{28,12},{1,17},{... | collective-permute-start | bytes 294920 | tf_op jit(solution)/shard_map/cond/branch_1_fun/ppermute | solution.py:1652
  128.2 16.5 %collective-permute-start.4 = (bf16[384,128]{1,0:T(8,128)(2,1)}, bf16[384,128]{1,0:T(8,128)(2,1)S(1)}, u32[]{:S(2)}, u32[]{:S(2)}) collective-permute-start(bf16[384,128]{1,0:T(8,128)(2,1)} %get-tuple-element.123), channel_id=1, source_target_pairs={{0,20},{4,24},{8,28},{12,0},{16,4},{20,8},{24,12},{28,16},{1,21},{... | collective-permute-start | bytes 294920 | tf_op jit(solution)/shard_map/cond/branch_1_fun/ppermute | solution.py:1652
  132.3 12.9 %collective-permute-start.5 = (bf16[384,128]{1,0:T(8,128)(2,1)}, bf16[384,128]{1,0:T(8,128)(2,1)S(1)}, u32[]{:S(2)}, u32[]{:S(2)}) collective-permute-start(bf16[384,128]{1,0:T(8,128)(2,1)} %get-tuple-element.124), channel_id=1, source_target_pairs={{0,24},{4,28},{8,0},{12,4},{16,8},{20,12},{24,16},{28,20},{1,25},{... | collective-permute-start | bytes 294920 | tf_op jit(solution)/shard_map/cond/branch_1_fun/ppermute | solution.py:1652
  133.0 14.5 %collective-permute-start.6 = (bf16[384,128]{1,0:T(8,128)(2,1)}, bf16[384,128]{1,0:T(8,128)(2,1)S(1)}, u32[]{:S(2)}, u32[]{:S(2)}) collective-permute-start(bf16[384,128]{1,0:T(8,128)(2,1)} %get-tuple-element.125), channel_id=1, source_target_pairs={{0,28},{4,0},{8,4},{12,8},{16,12},{20,16},{24,20},{28,24},{1,29},{... | collective-permute-start | bytes 294920 | tf_op jit(solution)/shard_map/cond/branch_1_fun/ppermute | solution.py:1652
  173.3 15.4 %collective-permute-start.7 = (bf16[896,128]{1,0:T(8,128)(2,1)}, bf16[896,128]{1,0:T(8,128)(2,1)}, u32[]{:S(2)}, u32[]{:S(2)}) collective-permute-start(bf16[896,128]{1,0:T(8,128)(2,1)} %get-tuple-element.139), channel_id=1, source_target_pairs={{0,4},{4,8},{8,12},{12,16},{16,20},{20,24},{24,28},{28,0},{1,5},{5... | collective-permute-start | bytes 688136 | tf_op jit(solution)/shard_map/cond/branch_1_fun/ppermute | solution.py:1652
  174.0 14.9 %collective-permute-start.8 = (bf16[896,128]{1,0:T(8,128)(2,1)}, bf16[896,128]{1,0:T(8,128)(2,1)}, u32[]{:S(2)}, u32[]{:S(2)}) collective-permute-start(bf16[896,128]{1,0:T(8,128)(2,1)} %get-tuple-element.140), channel_id=1, source_target_pairs={{0,8},{4,12},{8,16},{12,20},{16,24},{20,28},{24,0},{28,4},{1,9},{5... | collective-permute-start | bytes 688136 | tf_op jit(solution)/shard_map/cond/branch_1_fun/ppermute | solution.py:1652
  181.7 27.2 %collective-permute-start.9 = (bf16[896,128]{1,0:T(8,128)(2,1)}, bf16[896,128]{1,0:T(8,128)(2,1)}, u32[]{:S(2)}, u32[]{:S(2)}) collective-permute-start(bf16[896,128]{1,0:T(8,128)(2,1)} %get-tuple-element.141), channel_id=1, source_target_pairs={{0,12},{4,16},{8,20},{12,24},{16,28},{20,0},{24,4},{28,8},{1,13},{... | collective-permute-start | bytes 688136 | tf_op jit(solution)/shard_map/cond/branch_1_fun/ppermute | solution.py:1652
  181.7 27.7 %collective-permute-start.10 = (bf16[896,128]{1,0:T(8,128)(2,1)}, bf16[896,128]{1,0:T(8,128)(2,1)}, u32[]{:S(2)}, u32[]{:S(2)}) collective-permute-start(bf16[896,128]{1,0:T(8,128)(2,1)} %get-tuple-element.142), channel_id=1, source_target_pairs={{0,16},{4,20},{8,24},{12,28},{16,0},{20,4},{24,8},{28,12},{1,17},{... | collective-permute-start | bytes 688136 | tf_op jit(solution)/shard_map/cond/branch_1_fun/ppermute | solution.py:1652
  183.3 26.2 %collective-permute-start.11 = (bf16[896,128]{1,0:T(8,128)(2,1)}, bf16[896,128]{1,0:T(8,128)(2,1)}, u32[]{:S(2)}, u32[]{:S(2)}) collective-permute-start(bf16[896,128]{1,0:T(8,128)(2,1)} %get-tuple-element.143), channel_id=1, source_target_pairs={{0,20},{4,24},{8,28},{12,0},{16,4},{20,8},{24,12},{28,16},{1,21},{... | collective-permute-start | bytes 688136 | tf_op jit(solution)/shard_map/cond/branch_1_fun/ppermute | solution.py:1652
  188.7 22.0 %collective-permute-start.12 = (bf16[896,128]{1,0:T(8,128)(2,1)}, bf16[896,128]{1,0:T(8,128)(2,1)}, u32[]{:S(2)}, u32[]{:S(2)}) collective-permute-start(bf16[896,128]{1,0:T(8,128)(2,1)} %get-tuple-element.144), channel_id=1, source_target_pairs={{0,24},{4,28},{8,0},{12,4},{16,8},{20,12},{24,16},{28,20},{1,25},{... | collective-permute-start | bytes 688136 | tf_op jit(solution)/shard_map/cond/branch_1_fun/ppermute | solution.py:1652
  188.9 24.3 %collective-permute-start.13 = (bf16[896,128]{1,0:T(8,128)(2,1)}, bf16[896,128]{1,0:T(8,128)(2,1)}, u32[]{:S(2)}, u32[]{:S(2)}) collective-permute-start(bf16[896,128]{1,0:T(8,128)(2,1)} %get-tuple-element.145), channel_id=1, source_target_pairs={{0,28},{4,0},{8,4},{12,8},{16,12},{20,16},{24,20},{28,24},{1,29},{... | collective-permute-start | bytes 688136 | tf_op jit(solution)/shard_map/cond/branch_1_fun/ppermute | solution.py:1652
  223.1 2.9 collective-permute-start.14
  227.6 10.7 %collective-permute-start.17 = (bf16[1024,128]{1,0:T(8,128)(2,1)S(1)}, bf16[1024,128]{1,0:T(8,128)(2,1)S(1)}, u32[]{:S(2)}, u32[]{:S(2)}) collective-permute-start(bf16[1024,128]{1,0:T(8,128)(2,1)S(1)} %get-tuple-element.269), channel_id=1, source_target_pairs={{0,6},{1,7},{2,4},{3,5},{4,2},{5,3},{6,0},{7,1},{8,14},{9,15},{10,... | collective-permute-start | bytes 786440 | tf_op jit(solution)/shard_map/cond/branch_1_fun/ppermute | solution.py:791
  231.2 13.5 %collective-permute-start.16 = (bf16[1024,128]{1,0:T(8,128)(2,1)S(1)}, bf16[1024,128]{1,0:T(8,128)(2,1)S(1)}, u32[]{:S(2)}, u32[]{:S(2)}) collective-permute-start(bf16[1024,128]{1,0:T(8,128)(2,1)S(1)} %get-tuple-element.270), channel_id=1, source_target_pairs={{0,4},{1,5},{2,6},{3,7},{4,0},{5,1},{6,2},{7,3},{8,12},{9,13},{10,... | collective-permute-start | bytes 786440 | tf_op jit(solution)/shard_map/cond/branch_1_fun/ppermute | solution.py:791
  231.2 13.5 %collective-permute-start.15 = (bf16[1024,128]{1,0:T(8,128)(2,1)S(1)}, bf16[1024,128]{1,0:T(8,128)(2,1)S(1)}, u32[]{:S(2)}, u32[]{:S(2)}) collective-permute-start(bf16[1024,128]{1,0:T(8,128)(2,1)S(1)} %get-tuple-element.268), channel_id=1, source_target_pairs={{0,2},{1,3},{2,0},{3,1},{4,6},{5,7},{6,4},{7,5},{8,10},{9,11},{10,... | collective-permute-start | bytes 786440 | tf_op jit(solution)/shard_map/cond/branch_1_fun/ppermute | solution.py:791
  244.8 18.7 %collective-permute-start.20 = (bf16[256,128]{1,0:T(8,128)(2,1)S(1)}, bf16[256,128]{1,0:T(8,128)(2,1)S(1)}, u32[]{:S(2)}, u32[]{:S(2)}) collective-permute-start(bf16[256,128]{1,0:T(8,128)(2,1)S(1)} %get-tuple-element.272), channel_id=1, source_target_pairs={{0,16},{1,17},{2,18},{3,19},{4,20},{5,21},{6,22},{7,23},{8,24},{9,... | collective-permute-start | bytes 196616 | tf_op jit(solution)/shard_map/cond/branch_1_fun/ppermute | solution.py:791
  257.3 6.9 %collective-permute-start.19 = (bf16[256,128]{1,0:T(8,128)(2,1)S(1)}, bf16[256,128]{1,0:T(8,128)(2,1)S(1)}, u32[]{:S(2)}, u32[]{:S(2)}) collective-permute-start(bf16[256,128]{1,0:T(8,128)(2,1)S(1)} %get-tuple-element.273), channel_id=1, source_target_pairs={{0,24},{1,25},{2,26},{3,27},{4,28},{5,29},{6,30},{7,31},{8,16},{9,... | collective-permute-start | bytes 196616 | tf_op jit(solution)/shard_map/cond/branch_1_fun/ppermute | solution.py:791
  259.8 4.9 %collective-permute-start.18 = (bf16[256,128]{1,0:T(8,128)(2,1)S(1)}, bf16[256,128]{1,0:T(8,128)(2,1)S(1)}, u32[]{:S(2)}, u32[]{:S(2)}) collective-permute-start(bf16[256,128]{1,0:T(8,128)(2,1)S(1)} %get-tuple-element.271), channel_id=1, source_target_pairs={{0,8},{1,9},{2,10},{3,11},{4,12},{5,13},{6,14},{7,15},{8,0},{9,1},... | collective-permute-start | bytes 196616 | tf_op jit(solution)/shard_map/cond/branch_1_fun/ppermute | solution.py:791
  264.7 7.6 %collective-permute-start.23 = (bf16[256,128]{1,0:T(8,128)(2,1)S(1)}, bf16[256,128]{1,0:T(8,128)(2,1)S(1)}, u32[]{:S(2)}, u32[]{:S(2)}) collective-permute-start(bf16[256,128]{1,0:T(8,128)(2,1)S(1)} %fusion.7), channel_id=1, source_target_pairs={{0,16},{1,17},{2,18},{3,19},{4,20},{5,21},{6,22},{7,23},{8,24},{9,... | collective-permute-start | bytes 196616 | tf_op jit(solution)/shard_map/cond/branch_1_fun/ppermute | solution.py:791
  267.2 6.3 %collective-permute-start.22 = (bf16[256,128]{1,0:T(8,128)(2,1)S(1)}, bf16[256,128]{1,0:T(8,128)(2,1)S(1)}, u32[]{:S(2)}, u32[]{:S(2)}) collective-permute-start(bf16[256,128]{1,0:T(8,128)(2,1)S(1)} %fusion.7), channel_id=1, source_target_pairs={{0,24},{1,25},{2,26},{3,27},{4,28},{5,29},{6,30},{7,31},{8,16},{9,... | collective-permute-start | bytes 196616 | tf_op jit(solution)/shard_map/cond/branch_1_fun/ppermute | solution.py:791
  268.2 6.2 %collective-permute-start.21 = (bf16[256,128]{1,0:T(8,128)(2,1)S(1)}, bf16[256,128]{1,0:T(8,128)(2,1)S(1)}, u32[]{:S(2)}, u32[]{:S(2)}) collective-permute-start(bf16[256,128]{1,0:T(8,128)(2,1)S(1)} %fusion.7), channel_id=1, source_target_pairs={{0,8},{1,9},{2,10},{3,11},{4,12},{5,13},{6,14},{7,15},{8,0},{9,1},... | collective-permute-start | bytes 196616 | tf_op jit(solution)/shard_map/cond/branch_1_fun/ppermute | solution.py:791
  274.5 15.6 %collective-permute-start.26 = (bf16[4,256,128]{2,1,0:T(8,128)(2,1)S(1)}, bf16[4,256,128]{2,1,0:T(8,128)(2,1)S(1)}, u32[]{:S(2)}, u32[]{:S(2)}) collective-permute-start(bf16[4,256,128]{2,1,0:T(8,128)(2,1)S(1)} %bitcast.70), channel_id=1, source_target_pairs={{0,6},{1,7},{2,4},{3,5},{4,2},{5,3},{6,0},{7,1},{8,14},{9,15},{10,... | collective-permute-start | bytes 786440 | tf_op jit(solution)/shard_map/cond/branch_1_fun/ppermute | solution.py:791
  276.3 18.1 %collective-permute-start.25 = (bf16[4,256,128]{2,1,0:T(8,128)(2,1)S(1)}, bf16[4,256,128]{2,1,0:T(8,128)(2,1)S(1)}, u32[]{:S(2)}, u32[]{:S(2)}) collective-permute-start(bf16[4,256,128]{2,1,0:T(8,128)(2,1)S(1)} %bitcast.71), channel_id=1, source_target_pairs={{0,4},{1,5},{2,6},{3,7},{4,0},{5,1},{6,2},{7,3},{8,12},{9,13},{10,... | collective-permute-start | bytes 786440 | tf_op jit(solution)/shard_map/cond/branch_1_fun/ppermute | solution.py:791
  277.5 17.0 %collective-permute-start.24 = (bf16[4,256,128]{2,1,0:T(8,128)(2,1)S(1)}, bf16[4,256,128]{2,1,0:T(8,128)(2,1)S(1)}, u32[]{:S(2)}, u32[]{:S(2)}) collective-permute-start(bf16[4,256,128]{2,1,0:T(8,128)(2,1)S(1)} %bitcast.72), channel_id=1, source_target_pairs={{0,2},{1,3},{2,0},{3,1},{4,6},{5,7},{6,4},{7,5},{8,10},{9,11},{10,... | collective-permute-start | bytes 786440 | tf_op jit(solution)/shard_map/cond/branch_1_fun/ppermute | solution.py:791
  296.1 3.0 collective-permute-start.27
  (35 other events, 435.8 us)
Sparse Core Ops, SparseCore 0:
  105.1 199.3 all-reduce.1
